TPU v7x, 32 devices: a whole 2x2x4 slice. The times are simulated.
32 devices in a mesh: rep: 16 (over z, x, core), shard: 2 (over y).
Axes of the slice: x: 2, y: 2, z: 4, core: 2. Of those that a mesh axis runs over, the one named last changes fastest.
Arguments:
- tokens: bfloat16 [7168, 1536], P(('rep', 'shard')), may hold values from -6 to 6
- norm_gain: bfloat16 [1536], P('shard'), may hold values from 0.5 to 1.5
- w_query: bfloat16 [1536, 1536], P('shard'), may hold values from -0.15625 to 0.15625
- key_weight: bfloat16 [1536, 512], P('shard'), may hold values from -0.15625 to 0.15625
- value_weight: bfloat16 [1536, 512], P('shard'), may hold values from -0.15625 to 0.15625
- w_out: bfloat16 [1536, 1536], P(None, 'shard'), may hold values from -1.25 to 1.25
- ffn_gain: bfloat16 [1536], P('shard'), may hold values from 0.5 to 1.5
- w_router: bfloat16 [1536, 16], P('shard'), may hold values from -0.1875 to 0.1875
- w_gate: bfloat16 [16, 1536, 512], P('shard'), may hold values from -0.15625 to 0.15625
- w_up: bfloat16 [16, 1536, 512], P('shard'), may hold values from -0.15625 to 0.15625
- w_down: bfloat16 [16, 512, 1536], P('shard'), may hold values from -0.5 to 0.5
- parents: int32 [16, 13], P('rep'), may hold values from 0 to 4, as said below
- routes: int32 [7168, 8], P(('rep', 'shard')), may hold values from 0 to 15, all different within a row; in each aligned block of 224 rows (0 to 223, 224 to 447, ...) at most 126 rows name the same one
- cotangent: bfloat16 [7168, 1536], P(('rep', 'shard')), may hold values from -6 to 6
Outputs:
- output: bfloat16 [7168, 1536], P(('rep', 'shard'))
- input_grad: bfloat16 [7168, 1536], P(('rep', 'shard'))
- grad_norm_gain: float32 [1536], P('shard')
- grad_query: float32 [1536, 1536], P('shard')
- grad_key: float32 [1536, 512], P('shard')
- grad_value: float32 [1536, 512], P('shard')
- grad_out: float32 [1536, 1536], P(None, 'shard')
- grad_ffn_gain: float32 [1536], P('shard')
- grad_router: float32 [1536, 16], P('shard')
- grad_gate: float32 [16, 1536, 512], P('shard', 'rep')
- grad_up: float32 [16, 1536, 512], P('shard', 'rep')
- grad_down: float32 [16, 512, 1536], P('shard', None, 'rep')
Inputs may be any that keep to these rules, and one draw needn't show every extreme that they name: `parents`: segments 0 to 4 have parent 0 (the trunk is its own parent, 1 to 4 are branches); each of segments 5 to 12 (leaves) names a branch. `routes`: among the 224 tokens of one device no expert is named more than 126 times, a bound that some block reaches; a token names 8 different experts.
All inputs are finite; a program needn't handle non-finite values.
Results may differ from a plain program's by a relative error of at most 0.022.
Values may be sent and summed in bfloat16 or wider, within the bound.
No kernel may reach another device: no remote copies, remote signals or barrier semaphores. Data moves between devices by JAX's collectives and lax.ppermute only.
A program may use at most 384 MiB of HBM per device.

v0:
```python
import jax
import jax.numpy as jnp
from jax import lax
from jax.sharding import PartitionSpec as P

HEAD_DIM = 64
CAP = 126


EPS = 1e-06


def tree_layout(position, seg_len):
    trunk_len = 4 * seg_len
    beyond = position - trunk_len
    segment = jnp.where(position < trunk_len, 0, 1 + beyond // seg_len)
    inner = jnp.where(
        segment <= 4, trunk_len + beyond % seg_len, trunk_len + seg_len + beyond % seg_len
    )
    depth_position = jnp.where(position < trunk_len, position, inner)
    return (segment, depth_position)


def lookup(segment, parents_row):
    labels = jnp.arange(parents_row.shape[0], dtype=jnp.int32)
    picked = jnp.where(segment[:, None] == labels[None, :], parents_row[None, :], 0)
    return jnp.sum(picked, axis=1)


def tree_mask(query_index, key_index, parents_row, seg_len):
    query_seg, unused_depth = tree_layout(query_index, seg_len)
    key_seg, other_depth = tree_layout(key_index, seg_len)
    parent_one = lookup(query_seg, parents_row)
    parent_two = lookup(parent_one, parents_row)
    key_row = key_seg[None, :]
    related = (
        (key_row == query_seg[:, None])
        | (key_row == parent_one[:, None])
        | (key_row == parent_two[:, None])
    )
    return related & (key_index[None, :] <= query_index[:, None])


def angle_tables(depth_position, half_dim):
    frequency = 10000.0 ** (-2.0 * jnp.arange(half_dim, dtype=jnp.float32) / (2 * half_dim))
    angles = depth_position.astype(jnp.float32)[:, None] * frequency[None, :]
    return (jnp.cos(angles)[:, None, :], jnp.sin(angles)[:, None, :])


def apply_rotary(values, depth_position):
    half_dim = values.shape[-1] // 2
    cosine, sine_part = angle_tables(depth_position, half_dim)
    first_half = values[..., :half_dim]
    second_half = values[..., half_dim:]
    return jnp.concatenate(
        [
            first_half * cosine - second_half * sine_part,
            second_half * cosine + first_half * sine_part,
        ],
        axis=-1,
    )


def unrotate(values, depth_position):
    half_dim = values.shape[-1] // 2
    cosine, sine_part = angle_tables(depth_position, half_dim)
    first_half = values[..., :half_dim]
    second_half = values[..., half_dim:]
    return jnp.concatenate(
        [
            first_half * cosine + second_half * sine_part,
            second_half * cosine - first_half * sine_part,
        ],
        axis=-1,
    )


def norm_backward(grad_hidden, normed, inverse, gain_full):
    scaled = grad_hidden * gain_full
    grad_gain = jnp.sum(grad_hidden * normed, axis=0)
    grad_inputs = inverse * (scaled - normed * jnp.mean(scaled * normed, axis=-1, keepdims=True))
    return (grad_gain, grad_inputs)


def expert_activation(gate_pre, up_pre):
    gate_sig = jax.nn.sigmoid(gate_pre)
    silu_val = gate_pre * gate_sig
    hidden_mid = (silu_val * up_pre).astype(jnp.bfloat16)
    return (gate_sig, silu_val, hidden_mid)


def expert_backward(
    rows, grad_rows, gate_pre, up_pre, gate_sig, silu_val, hidden_mid, gate_w, up_w, down_w
):
    grad_down_w = jnp.einsum(
        "ecf,ecd->efd", hidden_mid, grad_rows, preferred_element_type=jnp.float32
    )
    grad_mid = jnp.einsum("ecd,efd->ecf", grad_rows, down_w, preferred_element_type=jnp.float32)
    grad_gate_pre = (grad_mid * up_pre * gate_sig * (1.0 + gate_pre * (1.0 - gate_sig))).astype(
        jnp.bfloat16
    )
    grad_up_pre = (grad_mid * silu_val).astype(jnp.bfloat16)
    grad_gate_w = jnp.einsum(
        "ecd,ecf->edf", rows, grad_gate_pre, preferred_element_type=jnp.float32
    )
    grad_up_w = jnp.einsum("ecd,ecf->edf", rows, grad_up_pre, preferred_element_type=jnp.float32)
    grad_in = jnp.einsum("ecf,edf->ecd", grad_gate_pre, gate_w, preferred_element_type=jnp.float32)
    grad_in = grad_in + jnp.einsum(
        "ecf,edf->ecd", grad_up_pre, up_w, preferred_element_type=jnp.float32
    )
    return (grad_gate_w, grad_up_w, grad_down_w, grad_in)


def local(
    tokens,
    norm_gain,
    w_query,
    key_weight,
    value_weight,
    w_out,
    ffn_gain,
    w_router,
    w_gate,
    w_up,
    w_down,
    parents,
    routes,
    cotangent,
):
    groups = lax.axis_size("shard")
    member = lax.axis_index("shard")
    tok_rows = tokens.shape[0]
    model_width = tokens.shape[1]
    tree_len = tok_rows * groups
    seg_len = tree_len // 16
    q_heads = w_query.shape[1] // HEAD_DIM
    kv_heads = key_weight.shape[1] // HEAD_DIM
    group_size = q_heads // kv_heads
    experts = w_gate.shape[0] * groups
    top_count = routes.shape[1]
    score_scale = HEAD_DIM ** (-0.5)
    gain_one, query_full, key_full, value_full, out_full, gain_two, router_full = (
        lax.all_gather(norm_gain, "shard", axis=0, tiled=True),
        lax.all_gather(w_query, "shard", axis=0, tiled=True),
        lax.all_gather(key_weight, "shard", axis=0, tiled=True),
        lax.all_gather(value_weight, "shard", axis=0, tiled=True),
        lax.all_gather(w_out, "shard", axis=1, tiled=True),
        lax.all_gather(ffn_gain, "shard", axis=0, tiled=True),
        lax.all_gather(w_router, "shard", axis=0, tiled=True),
    )
    gain_one_f = gain_one.astype(jnp.float32)
    gain_two_f = gain_two.astype(jnp.float32)
    parents_row = parents[0]
    own_index = member * tok_rows + jnp.arange(tok_rows, dtype=jnp.int32)
    own_seg, depth_own = tree_layout(own_index, seg_len)
    key_index = jnp.arange(tree_len, dtype=jnp.int32)
    visible = tree_mask(own_index, key_index, parents_row, seg_len)
    inputs = tokens.astype(jnp.float32)
    inv_one = lax.rsqrt(jnp.mean(inputs * inputs, axis=-1, keepdims=True) + EPS)
    normed_one = inputs * inv_one
    hidden_first = (normed_one * gain_one_f).astype(jnp.bfloat16)
    query_raw = jnp.dot(hidden_first, query_full, preferred_element_type=jnp.float32)
    key_unrotated = jnp.dot(hidden_first, key_full, preferred_element_type=jnp.float32)
    value_raw = jnp.dot(hidden_first, value_full, preferred_element_type=jnp.float32)
    query_rotated = apply_rotary(query_raw.reshape(tok_rows, q_heads, HEAD_DIM), depth_own).astype(
        jnp.bfloat16
    )
    key_rotated = (
        apply_rotary(key_unrotated.reshape(tok_rows, kv_heads, HEAD_DIM), depth_own)
        .reshape(tok_rows, kv_heads * HEAD_DIM)
        .astype(jnp.bfloat16)
    )
    value_low = value_raw.astype(jnp.bfloat16)
    key_tree, value_tree = (
        lax.all_gather(key_rotated, "shard", axis=0, tiled=True),
        lax.all_gather(value_low, "shard", axis=0, tiled=True),
    )
    query_heads = query_rotated.reshape(tok_rows, kv_heads, group_size, HEAD_DIM).transpose(
        1, 2, 0, 3
    )
    key_heads = key_tree.reshape(tree_len, kv_heads, HEAD_DIM).transpose(1, 0, 2)
    value_heads = value_tree.reshape(tree_len, kv_heads, HEAD_DIM).transpose(1, 0, 2)

    def head_scores(query_one, key_one):
        scores = (
            jnp.einsum("gqd,kd->gqk", query_one, key_one, preferred_element_type=jnp.float32)
            * score_scale
        )
        return jnp.where(visible[None], scores, -1e30)

    def head_forward(operands):
        query_one, key_one, value_one = operands
        scores = head_scores(query_one, key_one)
        row_peak = jnp.max(scores, axis=-1, keepdims=True)
        exp_scores = jnp.exp(scores - row_peak)
        row_total = jnp.sum(exp_scores, axis=-1, keepdims=True)
        weights_low = (exp_scores / row_total).astype(jnp.bfloat16)
        attended_one = jnp.einsum(
            "gqk,kd->gqd", weights_low, value_one, preferred_element_type=jnp.float32
        )
        return (attended_one, row_peak + jnp.log(row_total))

    attended, log_total = lax.map(head_forward, (query_heads, key_heads, value_heads))
    mixed_heads = (
        attended.transpose(2, 0, 1, 3).reshape(tok_rows, q_heads * HEAD_DIM).astype(jnp.bfloat16)
    )
    branch = jnp.dot(mixed_heads, out_full, preferred_element_type=jnp.float32)
    middle = inputs + branch
    inv_two = lax.rsqrt(jnp.mean(middle * middle, axis=-1, keepdims=True) + EPS)
    normed_two = middle * inv_two
    hidden_two = (normed_two * gain_two_f).astype(jnp.bfloat16)
    logits = jnp.dot(hidden_two, router_full, preferred_element_type=jnp.float32)
    route_hot = (routes[:, :, None] == jnp.arange(experts, dtype=jnp.int32)[None, None, :]).astype(
        jnp.float32
    )
    chosen = jnp.sum(route_hot * logits[:, None, :], axis=-1)
    chosen_peak = jnp.max(chosen, axis=-1, keepdims=True)
    gate_exp = jnp.exp(chosen - chosen_peak)
    gates = gate_exp / jnp.sum(gate_exp, axis=-1, keepdims=True)
    flat_routes = routes.reshape(-1)
    expert_hot = (flat_routes[:, None] == jnp.arange(experts, dtype=jnp.int32)[None, :]).astype(
        jnp.int32
    )
    rank_before = jnp.cumsum(expert_hot, axis=0) - expert_hot
    slot_index = jnp.sum(rank_before * expert_hot, axis=1)
    destination = flat_routes * CAP + slot_index
    source = jnp.arange(tok_rows * top_count, dtype=jnp.int32) // top_count
    buffer = (
        jnp.zeros((experts * CAP, model_width), jnp.bfloat16)
        .at[destination]
        .set(hidden_two[source])
        .reshape(experts, CAP, model_width)
    )
    gate_part = jnp.einsum(
        "ecd,edf->ecf",
        buffer,
        lax.all_gather(w_gate, "shard", axis=0, tiled=True),
        preferred_element_type=jnp.float32,
    )
    up_part = jnp.einsum(
        "ecd,edf->ecf",
        buffer,
        lax.all_gather(w_up, "shard", axis=0, tiled=True),
        preferred_element_type=jnp.float32,
    )
    gate_sig, silu_val, hidden_mid = expert_activation(gate_part, up_part)
    expert_out = jnp.einsum(
        "ecf,efd->ecd",
        hidden_mid,
        lax.all_gather(w_down, "shard", axis=0, tiled=True),
        preferred_element_type=jnp.float32,
    )
    paired = expert_out.reshape(experts * CAP, model_width)[destination].reshape(
        tok_rows, top_count, model_width
    )
    mixture = jnp.sum(gates[..., None] * paired, axis=1)
    result = (middle + mixture).astype(jnp.bfloat16)
    grad_top = cotangent.astype(jnp.float32)
    grad_gates = jnp.sum(paired * grad_top[:, None, :], axis=-1)
    grad_chosen = gates * (grad_gates - jnp.sum(gates * grad_gates, axis=-1, keepdims=True))
    grad_logits = jnp.sum(grad_chosen[..., None] * route_hot, axis=1).astype(jnp.bfloat16)
    grad_router_full = jnp.dot(hidden_two.T, grad_logits, preferred_element_type=jnp.float32)
    grad_paired = (
        (gates[..., None] * grad_top[:, None, :])
        .astype(jnp.bfloat16)
        .reshape(tok_rows * top_count, model_width)
    )
    grad_slots = (
        jnp.zeros((experts * CAP, model_width), jnp.bfloat16)
        .at[destination]
        .set(grad_paired)
        .reshape(experts, CAP, model_width)
    )
    gate_full, up_full, down_full = (
        lax.all_gather(w_gate, "shard", axis=0, tiled=True),
        lax.all_gather(w_up, "shard", axis=0, tiled=True),
        lax.all_gather(w_down, "shard", axis=0, tiled=True),
    )
    grad_gate_all, grad_up_all, grad_down_all, grad_buffer = expert_backward(
        buffer,
        grad_slots,
        gate_part,
        up_part,
        gate_sig,
        silu_val,
        hidden_mid,
        gate_full,
        up_full,
        down_full,
    )
    grad_gate_local, grad_up_local, grad_down_local = (
        lax.psum_scatter(
            grad_gate_all.astype(jnp.bfloat16), "shard", scatter_dimension=0, tiled=True
        ).astype(jnp.float32),
        lax.psum_scatter(
            grad_up_all.astype(jnp.bfloat16), "shard", scatter_dimension=0, tiled=True
        ).astype(jnp.float32),
        lax.psum_scatter(
            grad_down_all.astype(jnp.bfloat16), "shard", scatter_dimension=0, tiled=True
        ).astype(jnp.float32),
    )
    expert_sums = (
        lax.psum_scatter(
            grad_gate_local.astype(jnp.bfloat16), "rep", scatter_dimension=1, tiled=True
        ).astype(jnp.float32),
        lax.psum_scatter(
            grad_up_local.astype(jnp.bfloat16), "rep", scatter_dimension=1, tiled=True
        ).astype(jnp.float32),
        lax.psum_scatter(
            grad_down_local.astype(jnp.bfloat16), "rep", scatter_dimension=2, tiled=True
        ).astype(jnp.float32),
    )
    grad_routed = grad_buffer.reshape(experts * CAP, model_width)[destination].reshape(
        tok_rows, top_count, model_width
    )
    grad_hidden_two = jnp.dot(
        grad_logits, router_full.T, preferred_element_type=jnp.float32
    ) + jnp.sum(grad_routed, axis=1)
    grad_gain_two, grad_norm_two = norm_backward(grad_hidden_two, normed_two, inv_two, gain_two_f)
    grad_middle = grad_top + grad_norm_two
    grad_branch = grad_middle.astype(jnp.bfloat16)
    grad_out_full = jnp.dot(mixed_heads.T, grad_branch, preferred_element_type=jnp.float32)
    grad_mixed = jnp.dot(grad_branch, out_full.T, preferred_element_type=jnp.float32).astype(
        jnp.bfloat16
    )
    grad_heads = grad_mixed.reshape(tok_rows, kv_heads, group_size, HEAD_DIM).transpose(1, 2, 0, 3)

    def head_backward(operands):
        query_one, key_one, value_one, grad_one, log_one = operands
        probs = jnp.exp(head_scores(query_one, key_one) - log_one)
        probs_low = probs.astype(jnp.bfloat16)
        grad_probs = jnp.einsum(
            "gqd,kd->gqk", grad_one, value_one, preferred_element_type=jnp.float32
        )
        grad_value_one = jnp.einsum(
            "gqk,gqd->kd", probs_low, grad_one, preferred_element_type=jnp.float32
        )
        row_delta = jnp.sum(probs * grad_probs, axis=-1, keepdims=True)
        grad_scores = (probs * (grad_probs - row_delta) * score_scale).astype(jnp.bfloat16)
        grad_query_one = jnp.einsum(
            "gqk,kd->gqd", grad_scores, key_one, preferred_element_type=jnp.float32
        )
        grad_key_one = jnp.einsum(
            "gqk,gqd->kd", grad_scores, query_one, preferred_element_type=jnp.float32
        )
        return (grad_query_one, grad_key_one, grad_value_one)

    grad_query_heads, grad_key_heads, grad_value_heads = lax.map(
        head_backward, (query_heads, key_heads, value_heads, grad_heads, log_total)
    )
    grad_query_rot = grad_query_heads.transpose(2, 0, 1, 3).reshape(tok_rows, q_heads, HEAD_DIM)
    grad_key_tree = grad_key_heads.transpose(1, 0, 2).reshape(tree_len, kv_heads * HEAD_DIM)
    grad_value_tree = grad_value_heads.transpose(1, 0, 2).reshape(tree_len, kv_heads * HEAD_DIM)
    own_key_grad, own_value_grad = (
        lax.psum_scatter(
            grad_key_tree.astype(jnp.bfloat16), "shard", scatter_dimension=0, tiled=True
        ).astype(jnp.float32),
        lax.psum_scatter(
            grad_value_tree.astype(jnp.bfloat16), "shard", scatter_dimension=0, tiled=True
        ).astype(jnp.float32),
    )
    query_grad_low = (
        unrotate(grad_query_rot, depth_own)
        .reshape(tok_rows, q_heads * HEAD_DIM)
        .astype(jnp.bfloat16)
    )
    key_grad_low = (
        unrotate(own_key_grad.reshape(tok_rows, kv_heads, HEAD_DIM), depth_own)
        .reshape(tok_rows, kv_heads * HEAD_DIM)
        .astype(jnp.bfloat16)
    )
    value_grad_low = own_value_grad.astype(jnp.bfloat16)
    grad_query_full = jnp.dot(hidden_first.T, query_grad_low, preferred_element_type=jnp.float32)
    grad_key_full = jnp.dot(hidden_first.T, key_grad_low, preferred_element_type=jnp.float32)
    grad_value_full = jnp.dot(hidden_first.T, value_grad_low, preferred_element_type=jnp.float32)
    grad_hidden_one = jnp.dot(query_grad_low, query_full.T, preferred_element_type=jnp.float32)
    grad_hidden_one = grad_hidden_one + jnp.dot(
        key_grad_low, key_full.T, preferred_element_type=jnp.float32
    )
    grad_hidden_one = grad_hidden_one + jnp.dot(
        value_grad_low, value_full.T, preferred_element_type=jnp.float32
    )
    grad_gain_one, grad_norm_one = norm_backward(grad_hidden_one, normed_one, inv_one, gain_one_f)
    input_grad = (grad_middle + grad_norm_one).astype(jnp.bfloat16)
    shard_sums = (
        lax.psum_scatter(
            grad_gain_one.astype(jnp.bfloat16), "shard", scatter_dimension=0, tiled=True
        ).astype(jnp.float32),
        lax.psum_scatter(
            grad_query_full.astype(jnp.bfloat16), "shard", scatter_dimension=0, tiled=True
        ).astype(jnp.float32),
        lax.psum_scatter(
            grad_key_full.astype(jnp.bfloat16), "shard", scatter_dimension=0, tiled=True
        ).astype(jnp.float32),
        lax.psum_scatter(
            grad_value_full.astype(jnp.bfloat16), "shard", scatter_dimension=0, tiled=True
        ).astype(jnp.float32),
        lax.psum_scatter(
            grad_out_full.astype(jnp.bfloat16), "shard", scatter_dimension=1, tiled=True
        ).astype(jnp.float32),
        lax.psum_scatter(
            grad_gain_two.astype(jnp.bfloat16), "shard", scatter_dimension=0, tiled=True
        ).astype(jnp.float32),
        lax.psum_scatter(
            grad_router_full.astype(jnp.bfloat16), "shard", scatter_dimension=0, tiled=True
        ).astype(jnp.float32),
    )
    summed = (
        lax.psum(shard_sums[0].astype(jnp.bfloat16), "rep").astype(jnp.float32),
        lax.psum(shard_sums[1].astype(jnp.bfloat16), "rep").astype(jnp.float32),
        lax.psum(shard_sums[2].astype(jnp.bfloat16), "rep").astype(jnp.float32),
        lax.psum(shard_sums[3].astype(jnp.bfloat16), "rep").astype(jnp.float32),
        lax.psum(shard_sums[4].astype(jnp.bfloat16), "rep").astype(jnp.float32),
        lax.psum(shard_sums[5].astype(jnp.bfloat16), "rep").astype(jnp.float32),
        lax.psum(shard_sums[6].astype(jnp.bfloat16), "rep").astype(jnp.float32),
    )
    return (
        result,
        input_grad,
        summed[0],
        summed[1],
        summed[2],
        summed[3],
        summed[4],
        summed[5],
        summed[6],
        expert_sums[0],
        expert_sums[1],
        expert_sums[2],
    )


def solution(mesh):
    return jax.shard_map(
        local,
        mesh=mesh,
        in_specs=(
            P(("rep", "shard"), None),
            P("shard"),
            P("shard", None),
            P("shard", None),
            P("shard", None),
            P(None, "shard"),
            P("shard"),
            P("shard", None),
            P("shard", None, None),
            P("shard", None, None),
            P("shard", None, None),
            P("rep", None),
            P(("rep", "shard"), None),
            P(("rep", "shard"), None),
        ),
        out_specs=(
            P(("rep", "shard"), None),
            P(("rep", "shard"), None),
            P("shard"),
            P("shard", None),
            P("shard", None),
            P("shard", None),
            P(None, "shard"),
            P("shard"),
            P("shard", None),
            P("shard", "rep", None),
            P("shard", "rep", None),
            P("shard", None, "rep"),
        ),
        check_vma=False,
    )
```

profile of v0, /device:TPU:0, one launch (start us, length us, event | category | flops | bytes accessed | tf_op | source)
XLA Modules:
  0.0 2948.3 jit_solution(14338360215502360737)
XLA Ops:
  51.6 17.3 all-gather.14.cloned.1.call-done
  80.0 53.1 %all-gather.10.cloned.1.call-done = bf16[1536,1536]{1,0:T(8,128)(2,1)} async-done(((bf16[768,1536]{1,0:T(8,128)(2,1)}), bf16[1536,1536]{1,0:T(8,128)(2,1)}) %all-gather.10.cloned.1.call-update) | async-done | bytes 4718608 | tf_op jit(solution)/shard_map/all_gather | solution.py:144
  138.8 37.9 %while.30 = (s32[]{:T(128)}, bf16[8,3,224,64]{2,3,1,0:T(8,128)(2,1)S(1)}, f32[8,3,224,1]{2,1,3,0:T(4,128)}, bf16[8,3,224,64]{2,3,1,0:T(8,128)(2,1)}, bf16[8,448,...) while((s32[]{:T(128)}, ...), condition=%wide.region_6.7_spmd.clone.clone, body=%wide.region_3.6_spmd.clone.sunk.clone | while | flops 80180576 | bytes 4445165 | solution.py:203
  176.7 20.5 all-gather.16.cloned.1.call-done
  202.9 23.6 scatter_custom_fusion.1
  233.2 36.3 %scatter_custom_fusion = bf16[2016,1536]{1,0:T(8,128)(2,1)} fusion(s32[1792]{0:T(1024)} %copy-done.52, bf16[224,1536]{1,0:T(8,128)(2,1)S(1)} %multiply_convert_fusion.3, s32[2048]{0:T(1024)} %pad_clamp_fusion.1, bf16[]{:T(256)} %constant.139.clone.1), kind=kCustom, calls=%fused_computation.89 | custom fusion | bytes 6193664 | tf_op jit(solution)/shard_map/scatter | solution.py:231
  276.0 216.3 %all-gather.18.cloned.1.call-done = bf16[16,1536,512]{2,1,0:T(8,128)(2,1)} async-done(((bf16[8,1536,512]{2,1,0:T(8,128)(2,1)}), bf16[16,1536,512]{2,1,0:T(8,128)(2,1)}) %all-gather.18.cloned.1.call-update) | async-done | bytes 25165840 | tf_op jit(solution)/shard_map/all_gather | solution.py:237
  492.3 18.9 fusion.131
  511.2 276.3 %all-gather.20.cloned.1.call-done = bf16[16,1536,512]{2,1,0:T(8,128)(2,1)} async-done(((bf16[8,1536,512]{2,1,0:T(8,128)(2,1)}), bf16[16,1536,512]{2,1,0:T(8,128)(2,1)}) %all-gather.20.cloned.1.call-update) | async-done | bytes 25165840 | tf_op jit(solution)/shard_map/all_gather | solution.py:243
  787.5 18.7 fusion.132
  806.2 276.6 %all-gather.22.cloned.1.call-done = bf16[16,512,1536]{2,1,0:T(8,128)(2,1)} async-done(((bf16[8,512,1536]{2,1,0:T(8,128)(2,1)}), bf16[16,512,1536]{2,1,0:T(8,128)(2,1)}) %all-gather.22.cloned.1.call-update) | async-done | bytes 25165840 | tf_op jit(solution)/shard_map/all_gather | solution.py:250
  1151.8 18.3 fusion.134
  1170.1 20.2 convolution_add_fusion
  1232.0 72.6 %while.31 = (s32[]{:T(128)}, f32[8,3,224,64]{2,3,1,0:T(8,128)}, bf16[8,448,64]{1,2,0:T(8,128)(2,1)}, bf16[8,448,64]{1,2,0:T(8,128)(2,1)}, bf16[8,3,224,64]{2,3,1...) while((s32[]{:T(128)}, f32[8,3,224,64]{2,3,1,0:T(8,128)}, ...), condition=%wide.region_24.25_spmd.clone.clone, body=%wide.region_22.24_spmd.clone.sunk.clone | while | flops 197595328 | bytes 16062729 | solution.py:348
  1395.2 62.8 %reduce-scatter.30.cloned.1.call-done = bf16[1536,768]{1,0:T(8,128)(2,1)} async-done(((bf16[1536,1536]{1,0:T(8,128)(2,1)}), bf16[1536,768]{1,0:T(8,128)(2,1)}) %reduce-scatter.30.cloned.1.call-update) | async-done | bytes 2359312 | tf_op jit(solution)/shard_map/reduce_scatter | solution.py:398
  1458.0 63.0 %reduce-scatter.24.cloned.1.call-done = bf16[768,1536]{1,0:T(8,128)(2,1)} async-done(((bf16[1536,1536]{1,0:T(8,128)(2,1)}), bf16[768,1536]{1,0:T(8,128)(2,1)}) %reduce-scatter.24.cloned.1.call-update) | async-done | bytes 2359312 | tf_op jit(solution)/shard_map/reduce_scatter | solution.py:389
  1521.1 281.4 %reduce-scatter.48.cloned.1.call-done = bf16[8,512,1536]{2,1,0:T(8,128)(2,1)} async-done(((bf16[16,512,1536]{2,1,0:T(8,128)(2,1)}), bf16[8,512,1536]{2,1,0:T(8,128)(2,1)}) %reduce-scatter.48.cloned.1.call-update) | async-done | bytes 12582928
  1819.7 264.3 %reduce-scatter.44.cloned.1.call-done = bf16[8,1536,512]{2,1,0:T(8,128)(2,1)} async-done(((bf16[16,1536,512]{2,1,0:T(8,128)(2,1)}), bf16[8,1536,512]{2,1,0:T(8,128)(2,1)}) %reduce-scatter.44.cloned.1.call-update) | async-done | bytes 12582928
  2084.2 281.2 %reduce-scatter.46.cloned.1.call-done = bf16[8,1536,512]{2,1,0:T(8,128)(2,1)} async-done(((bf16[16,1536,512]{2,1,0:T(8,128)(2,1)}), bf16[8,1536,512]{2,1,0:T(8,128)(2,1)}) %reduce-scatter.46.cloned.1.call-update) | async-done | bytes 12582928
  2379.9 62.6 %all-reduce.5 = (bf16[768]{0:T(1024)(128)(2,1)S(1)}, bf16[768]{0:T(1024)(128)(2,1)S(1)}, bf16[768,16]{0,1:T(8,128)(2,1)S(1)}) all-reduce(bf16[768]{0:T(1024)(128)(2,1)S(1)} %dynamic-slice.1, bf16[768]{0:T(1024)(128)(2,1)S(1)} %dynamic-slice.3, ...), channel_id=1, replica_groups=mesh['rep'=16,'shard'=2] {'rep'}, use_global_device_ids=true, to_apply=%region_30.31 | all-reduce | flops 13824 | bytes 55296 | tf_op jit(solution)/shard_map/psum | solution.py:409
  2446.9 75.6 %all-reduce.10.cloned.1.call-done = (bf16[768,1536]{1,0:T(8,128)(2,1)}, bf16[768,512]{1,0:T(8,128)(2,1)}, bf16[768,512]{1,0:T(8,128)(2,1)}, bf16[1536,768]{1,0:T(8,128)(2,1)}) async-done(((bf16[768,1536]{1,0:T(8,128)(2,1)}, bf16[768,512]{1,0:T(8,128)(2,1)}, bf16[768,512]{1,0:T(8,128)(2,1)}, bf16[1536,768]{1,0:T(8,128)(2,1)}), (bf16[768,1536]{1,0:T(8,128)(2,1)}, bf16[768,512]{1,0:T(8,128)(2,1)}, ...) | async-done | bytes 6291472 | tf_op jit(solution)/shard_map/psum | solution.py:410
  2532.4 129.5 %reduce-scatter.38.cloned.1.call-done = bf16[8,512,96]{1,0,2:T(8,128)(2,1)} async-done(((bf16[8,512,1536]{1,0,2:T(8,128)(2,1)}), bf16[8,512,96]{1,0,2:T(8,128)(2,1)}) %reduce-scatter.38.cloned.1.call-update) | async-done | bytes 786448 | tf_op jit(solution)/shard_map/reduce_scatter | solution.py:309
  2664.4 135.9 %reduce-scatter.34.cloned.1.call-done = bf16[8,96,512]{2,1,0:T(8,128)(2,1)} async-done(((bf16[8,1536,512]{2,1,0:T(8,128)(2,1)}), bf16[8,96,512]{2,1,0:T(8,128)(2,1)}) %reduce-scatter.34.cloned.1.call-update) | async-done | bytes 786448 | tf_op jit(solution)/shard_map/reduce_scatter | solution.py:303
  2802.7 136.0 %reduce-scatter.36.cloned.1.call-done = bf16[8,96,512]{2,1,0:T(8,128)(2,1)} async-done(((bf16[8,1536,512]{2,1,0:T(8,128)(2,1)}), bf16[8,96,512]{2,1,0:T(8,128)(2,1)}) %reduce-scatter.36.cloned.1.call-update) | async-done | bytes 786448 | tf_op jit(solution)/shard_map/reduce_scatter | solution.py:306
  (384 shorter events, 443.5 us)
Async XLA Ops:
  7.2 32.9 %all-gather.12.cloned.1.call-start = ((), (), s32[]{:S(2)}) async-start(), calls=%async_computation.14 | async-start | bytes 2359296 | tf_op jit(solution)/shard_map/all_gather | solution.py:145
  7.9 60.9 %all-gather.14.cloned.1.call-start = ((), (), s32[]{:S(2)}) async-start(), calls=%async_computation.15 | async-start | bytes 2359296 | tf_op jit(solution)/shard_map/all_gather | solution.py:146
  8.7 124.4 %all-gather.10.cloned.1.call-start = ((), (), s32[]{:S(2)}) async-start(), calls=%async_computation.13 | async-start | bytes 7077888 | tf_op jit(solution)/shard_map/all_gather | solution.py:144
  9.4 187.8 %all-gather.16.cloned.1.call-start = ((), (), s32[]{:S(2)}) async-start(), calls=%async_computation.16 | async-start | bytes 7077888 | tf_op jit(solution)/shard_map/all_gather | solution.py:147
  10.0 482.3 %all-gather.18.cloned.1.call-start = ((), (), s32[]{:S(2)}) async-start(), calls=%async_computation.17 | async-start | bytes 37748736 | tf_op jit(solution)/shard_map/all_gather | solution.py:237
  10.6 776.9 %all-gather.20.cloned.1.call-start = ((), (), s32[]{:S(2)}) async-start(), calls=%async_computation.18 | async-start | bytes 37748736 | tf_op jit(solution)/shard_map/all_gather | solution.py:243
  11.2 1071.6 %all-gather.22.cloned.1.call-start = ((), (), s32[]{:S(2)}) async-start(), calls=%async_computation.19 | async-start | bytes 37748736 | tf_op jit(solution)/shard_map/all_gather | solution.py:250
  11.9 1308.7 %reduce-scatter.40.cloned.1.call-start = ((), (), s32[]{:S(2)}) async-start(), calls=%async_computation.28 | async-start | bytes 688128
  17.7 115.4 %copy-start.31 = (f32[1536]{0:T(1024)}, f32[1536]{0:T(1024)S(1)}, u32[]{:S(2)}) copy-start(f32[1536]{0:T(1024)S(1)} %reshape.494) | copy-start | bytes 18436
  80.0 57.4 %copy-start.24 = (f32[224,32]{0,1:T(8,128)S(1)}, f32[224,32]{0,1:T(8,128)}, u32[]{:S(2)}) copy-start(f32[224,32]{0,1:T(8,128)} %copy-done.23) | copy-start | bytes 86020
  1151.8 71.9 %copy-start.47 = (bf16[224,16]{0,1:T(8,128)(2,1)}, bf16[224,16]{0,1:T(8,128)(2,1)S(1)}, u32[]{:S(2)}) copy-start(bf16[224,16]{0,1:T(8,128)(2,1)S(1)} %select_reduce_fusion) | copy-start | bytes 21508
  1306.6 30.8 %reduce-scatter.42.cloned.1.call-start = ((), (), s32[]{:S(2)}) async-start(), calls=%async_computation.29 | async-start | bytes 688128
  1307.7 87.4 %reduce-scatter.26.cloned.1.call-start = ((), (), s32[]{:S(2)}) async-start(), calls=%async_computation.21 | async-start | bytes 2359296 | tf_op jit(solution)/shard_map/reduce_scatter | solution.py:392
  1323.8 71.4 %reduce-scatter.28.cloned.1.call-start = ((), (), s32[]{:S(2)}) async-start(), calls=%async_computation.22 | async-start | bytes 2359296 | tf_op jit(solution)/shard_map/reduce_scatter | solution.py:395
  1340.2 117.7 %reduce-scatter.30.cloned.1.call-start = ((), (), s32[]{:S(2)}) async-start(), calls=%async_computation.23 | async-start | bytes 7077888 | tf_op jit(solution)/shard_map/reduce_scatter | solution.py:398
  1343.9 177.1 %reduce-scatter.24.cloned.1.call-start = ((), (), s32[]{:S(2)}) async-start(), calls=%async_computation.20 | async-start | bytes 7077888 | tf_op jit(solution)/shard_map/reduce_scatter | solution.py:389
  1349.7 452.8 %reduce-scatter.48.cloned.1.call-start = ((), (), s32[]{:S(2)}) async-start(), calls=%async_computation.32 | async-start | bytes 37748736
  1364.7 719.3 %reduce-scatter.44.cloned.1.call-start = ((), (), s32[]{:S(2)}) async-start(), calls=%async_computation.30 | async-start | bytes 37748736
  1378.9 986.5 %reduce-scatter.46.cloned.1.call-start = ((), (), s32[]{:S(2)}) async-start(), calls=%async_computation.31 | async-start | bytes 37748736
  1393.1 986.8 %reduce-scatter.32.cloned.1.call-start = ((), (), s32[]{:S(2)}) async-start(), calls=%async_computation.24 | async-start | bytes 73728 | tf_op jit(solution)/shard_map/reduce_scatter | solution.py:404
  1395.0 1127.4 %all-reduce.10.cloned.1.call-start = ((), (), s32[]{:S(2)}) async-start(), calls=%async_computation.33 | async-start | bytes 12582912 | tf_op jit(solution)/shard_map/psum | solution.py:410
  1521.0 1140.9 %reduce-scatter.38.cloned.1.call-start = ((), (), s32[]{:S(2)}) async-start(), calls=%async_computation.27 | async-start | bytes 13369344 | tf_op jit(solution)/shard_map/reduce_scatter | solution.py:309
  1819.6 980.7 %reduce-scatter.34.cloned.1.call-start = ((), (), s32[]{:S(2)}) async-start(), calls=%async_computation.25 | async-start | bytes 13369344 | tf_op jit(solution)/shard_map/reduce_scatter | solution.py:303
  2084.0 854.8 %reduce-scatter.36.cloned.1.call-start = ((), (), s32[]{:S(2)}) async-start(), calls=%async_computation.26 | async-start | bytes 13369344 | tf_op jit(solution)/shard_map/reduce_scatter | solution.py:306
  (58 other events, 470.5 us)
Sparse Core Ops, SparseCore 0:
  9.6 30.4 all-gather.11
  41.6 27.2 all-gather.13
  70.4 62.6 all-gather.9
  134.5 62.6 all-gather.15
  198.6 293.6 all-gather.17
  493.7 293.7 all-gather.19
  789.0 293.7 all-gather.21
  1306.8 13.8 reduce-scatter.39
  1323.6 13.8 reduce-scatter.41
  1340.1 26.0 reduce-scatter.25
  1369.1 26.0 reduce-scatter.27
  1397.9 59.9 reduce-scatter.29
  1460.9 59.9 reduce-scatter.23
  1523.1 279.3 reduce-scatter.47
  1804.6 279.2 reduce-scatter.43
  2086.1 279.2 reduce-scatter.45
  2368.1 9.8 reduce-scatter.31
  2381.7 140.6 all-reduce.9
  2527.0 134.7 reduce-scatter.37
  2666.3 133.9 reduce-scatter.33
  2804.9 133.8 reduce-scatter.35
where the time goes:
time: 2960 us; the launch traced here: 2950 us
  waiting for transfers between devices  2320 us (78%)
  matrix products  271 us (9%)
  local copies, waits for them, and re-layouts  142 us (5%)
  blocking collectives  98.5 us (3%)
  other arithmetic  94.4 us (3%)
    unnamed x26, waiting for transfers between devices  858 us
    all_gather x1, waiting for transfers between devices, local(): lax.all_gather(w_down, 'shard', axis=0, tiled=True)  277 us
    all_gather x1, waiting for transfers between devices, local(): lax.all_gather(w_up, 'shard', axis=0, tiled=True)  276 us
    all_gather x1, waiting for transfers between devices, local(): lax.all_gather(w_gate, 'shard', axis=0, tiled=True)  216 us
    reduce_scatter x1, waiting for transfers between devices, local(): lax.psum_scatter(grad_up_local.astype(jnp.bfloat16), 'rep', scatter_dimen...  136 us
    reduce_scatter x1, waiting for transfers between devices, local(): lax.psum_scatter(grad_gate_local.astype(jnp.bfloat16), 'rep', scatter_dim...  136 us
    reduce_scatter x1, waiting for transfers between devices, local(): lax.psum_scatter(grad_down_local.astype(jnp.bfloat16), 'rep', scatter_dim...  130 us
    psum x1, waiting for transfers between devices, local(): lax.psum(shard_sums[1].astype(jnp.bfloat16), 'rep').astype(jnp.float32)  75.6 us
  transfers between devices with their start and end apart: 21, of which 19 were waited for; matrix products, arithmetic and copies ran while one was open for 9% of the time, Pallas kernels for 0%

commit v1 on v0

v1 whole, which is shorter than its diff:
```python
import jax
import jax.numpy as jnp
from jax import lax
from jax.sharding import PartitionSpec as P

HEAD_DIM = 64
EPS = 1e-06
BF = jnp.bfloat16
F32 = jnp.float32


def tree_layout(position, seg_len):
    trunk_len = 4 * seg_len
    beyond = position - trunk_len
    segment = jnp.where(position < trunk_len, 0, 1 + beyond // seg_len)
    inner = jnp.where(
        segment <= 4, trunk_len + beyond % seg_len, trunk_len + seg_len + beyond % seg_len
    )
    depth_position = jnp.where(position < trunk_len, position, inner)
    return (segment, depth_position)


def lookup(segment, parents_row):
    labels = jnp.arange(parents_row.shape[0], dtype=jnp.int32)
    picked = jnp.where(segment[:, None] == labels[None, :], parents_row[None, :], 0)
    return jnp.sum(picked, axis=1)


def tree_mask(query_index, key_index, parents_row, seg_len):
    query_seg, _ = tree_layout(query_index, seg_len)
    key_seg, _ = tree_layout(key_index, seg_len)
    parent_one = lookup(query_seg, parents_row)
    parent_two = lookup(parent_one, parents_row)
    key_row = key_seg[None, :]
    related = (
        (key_row == query_seg[:, None])
        | (key_row == parent_one[:, None])
        | (key_row == parent_two[:, None])
    )
    return related & (key_index[None, :] <= query_index[:, None])


def angle_tables(depth_position, half_dim):
    frequency = 10000.0 ** (-2.0 * jnp.arange(half_dim, dtype=F32) / (2 * half_dim))
    angles = depth_position.astype(F32)[:, None] * frequency[None, :]
    return (jnp.cos(angles)[:, None, :], jnp.sin(angles)[:, None, :])


def rotate(values, tables, sign):
    cosine, sine = tables
    half = values.shape[-1] // 2
    first = values[..., :half]
    second = values[..., half:]
    return jnp.concatenate(
        [first * cosine - sign * second * sine, second * cosine + sign * first * sine], axis=-1
    )


def dot(a, b, dims):
    return lax.dot_general(a, b, (dims, ((), ())), preferred_element_type=F32)


def nn(a, b):
    return dot(a, b, ((1,), (0,)))


def nt(a, b):
    return dot(a, b, ((1,), (1,)))


def tn(a, b):
    return dot(a, b, ((0,), (0,)))


class Mesh:
    def __init__(self):
        self.groups = lax.axis_size("shard")
        self.member = lax.axis_index("shard")
        self.reps = lax.axis_size("rep")
        self.rep = lax.axis_index("rep")
        self.core = self.rep % 2
        self.chip = self.rep // 2
        self.chips = self.reps // 2
        rows = self.chips // 2
        order = [2 * z for z in range(rows)] + [2 * z + 1 for z in range(rows - 1, -1, -1)]
        self.ring = []
        for place, chip in enumerate(order):
            after, before = order[(place + 1) % self.chips], order[place - 1]
            self.ring += [(2 * chip, 2 * after), (2 * chip + 1, 2 * before + 1)]
        self.place = jnp.where(
            self.chip % 2 == 0, self.chip // 2, self.chips - 1 - self.chip // 2
        )
        self.way = 1 - 2 * self.core

    def chip_at(self, place):
        place = place % self.chips
        rows = self.chips // 2
        return jnp.where(place < rows, 2 * place, 2 * (self.chips - 1 - place) + 1)

    def swap_shard(self, v):
        return lax.ppermute(v, "shard", [(0, 1), (1, 0)])

    def swap_core(self, v):
        return lax.ppermute(v, "rep", [(r, r ^ 1) for r in range(self.reps)])

    def along_ring(self, v):
        return lax.ppermute(v, "rep", self.ring)

    def part(self, v, axis, which):
        size = v.shape[axis] // self.groups
        return lax.dynamic_slice_in_dim(v, which * size, size, axis)

    def gather(self, v, axis):
        if self.groups != 2:
            return lax.all_gather(v, "shard", axis=axis, tiled=True)
        other = self.swap_shard(v)
        return self.in_order(self.member, v, other, axis)

    def in_order(self, which, mine, other, axis):
        return jnp.where(
            which == 0,
            jnp.concatenate([mine, other], axis),
            jnp.concatenate([other, mine], axis),
        )

    def exchange(self, v, split_axis, concat_axis):
        if self.groups != 2:
            return lax.all_to_all(v, "shard", split_axis, concat_axis, tiled=True)
        other = self.swap_shard(self.part(v, split_axis, 1 - self.member))
        mine = self.part(v, split_axis, self.member)
        return self.in_order(self.member, mine, other, concat_axis)

    def scatter(self, v, axis):
        if self.groups != 2:
            return lax.psum_scatter(
                v.astype(BF), "shard", scatter_dimension=axis, tiled=True
            ).astype(F32)
        other = self.swap_shard(self.part(v, axis, 1 - self.member).astype(BF))
        return self.part(v, axis, self.member).astype(F32) + other.astype(F32)

    def total(self, v):
        if self.groups != 2:
            return lax.psum(v, "shard")
        return v + self.swap_shard(v)

    def ring_scatter(self, own):
        held = own(self.chip_at(self.place - self.way))
        for step in range(self.chips - 1):
            came = self.along_ring(held)
            mine = own(self.chip_at(self.place - self.way * (step + 2)))
            held = (came.astype(F32) + mine.astype(F32)).astype(BF)
        return held

    def ring_gather(self, held, axis):
        size = held.shape[axis]
        shape = list(held.shape)
        shape[axis] = size * self.chips
        whole = jnp.zeros(shape, held.dtype)
        whole = lax.dynamic_update_slice_in_dim(
            whole, held, self.chip_at(self.place) * size, axis
        )
        for step in range(self.chips - 1):
            held = self.along_ring(held)
            at = self.chip_at(self.place - self.way * (step + 1)) * size
            whole = lax.dynamic_update_slice_in_dim(whole, held, at, axis)
        return whole

    def all_reduce(self, v):
        half = v.shape[0] // 2
        v = v.astype(BF)
        mine = lax.dynamic_slice_in_dim(v, self.core * half, half, 0)
        other = self.swap_core(
            lax.dynamic_slice_in_dim(v, (1 - self.core) * half, half, 0)
        )
        both = (mine.astype(F32) + other.astype(F32)).astype(BF)
        chunk = half // self.chips
        held = self.ring_scatter(
            lambda chip: lax.dynamic_slice_in_dim(both, chip * chunk, chunk, 0)
        )
        whole = self.ring_gather(held, 0)
        return self.in_order(self.core, whole, self.swap_core(whole), 0).astype(F32)

    def butterfly(self, v):
        bit = 1
        while bit < self.reps:
            v = v + lax.ppermute(v, "rep", [(r, r ^ bit) for r in range(self.reps)])
            bit *= 2
        return v


def local(
    tokens,
    norm_gain,
    w_query,
    key_weight,
    value_weight,
    w_out,
    ffn_gain,
    w_router,
    w_gate,
    w_up,
    w_down,
    parents,
    routes,
    cotangent,
):
    me = Mesh()
    tok_rows, width = tokens.shape
    tree_len = tok_rows * me.groups
    seg_len = tree_len // 16
    columns = width // me.groups
    q_heads = w_query.shape[1] // HEAD_DIM // me.groups
    kv_heads = key_weight.shape[1] // HEAD_DIM // me.groups
    per_key = q_heads // kv_heads
    experts = w_gate.shape[0] * me.groups
    per_core = w_gate.shape[0] // 2
    hidden = w_gate.shape[2]
    scale = HEAD_DIM ** (-0.5)
    q_width, k_width = q_heads * HEAD_DIM, kv_heads * HEAD_DIM

    own_rows = tokens.astype(F32)
    inv_rows = lax.rsqrt(jnp.mean(own_rows * own_rows, axis=-1, keepdims=True) + EPS)
    inputs = me.exchange(tokens, 1, 0).astype(F32)
    inv_one = me.gather(inv_rows, 0)
    normed_one = inputs * inv_one
    gain_one = norm_gain.astype(F32)
    hidden_first = (normed_one * gain_one).astype(BF)
    raw_q = me.scatter(nn(hidden_first, w_query), 1)
    raw_k = me.scatter(nn(hidden_first, key_weight), 1)
    value_low = me.scatter(nn(hidden_first, value_weight), 1).astype(BF)

    route_hot = jnp.any(
        routes[:, :, None] == jnp.arange(experts, dtype=jnp.int32)[None, None, :], axis=1
    ).astype(F32)
    routed = me.gather(route_hot, 0)
    gain_two = ffn_gain.astype(F32)
    gain_two_full = me.gather(ffn_gain, 0).astype(F32)
    router_full = me.gather(w_router, 0)
    grad_tree = me.gather(cotangent, 0)
    grad_all = jnp.concatenate([grad_tree, me.swap_core(grad_tree)], 0)
    routed_other = me.swap_core(routed)

    index = jnp.arange(tree_len, dtype=jnp.int32)
    _, depth = tree_layout(index, seg_len)
    tables = angle_tables(depth, HEAD_DIM // 2)
    visible = tree_mask(index, index, parents[0], seg_len)

    def heads(v):
        return v.reshape(tree_len, -1, HEAD_DIM)

    query_rot = rotate(heads(raw_q), tables, 1.0).astype(BF)
    key_rot = rotate(heads(raw_k), tables, 1.0).astype(BF)
    query_h = query_rot.reshape(tree_len, kv_heads, per_key, HEAD_DIM).transpose(1, 2, 0, 3)
    key_h = key_rot.transpose(1, 0, 2)
    value_h = heads(value_low).transpose(1, 0, 2)

    def scores_of(q, k):
        s = jnp.einsum("gqd,kd->gqk", q, k, preferred_element_type=F32) * scale
        return jnp.where(visible[None], s, -1e30)

    def head_forward(operands):
        q, k, v = operands
        s = scores_of(q, k)
        peak = jnp.max(s, axis=-1, keepdims=True)
        e = jnp.exp(s - peak)
        total = jnp.sum(e, axis=-1, keepdims=True)
        probs = (e / total).astype(BF)
        return (
            jnp.einsum("gqk,kd->gqd", probs, v, preferred_element_type=F32),
            peak + jnp.log(total),
        )

    attended_h, log_total = lax.map(head_forward, (query_h, key_h, value_h))
    attended = attended_h.transpose(2, 0, 1, 3).reshape(tree_len, q_width).astype(BF)
    attended_full = me.gather(attended, 1)
    middle = inputs + nn(attended_full, w_out)
    squares = me.total(jnp.sum(middle * middle, axis=-1, keepdims=True))
    inv_two = lax.rsqrt(squares / width + EPS)
    normed_two = middle * inv_two
    hidden_own = (normed_two * gain_two).astype(BF)
    hidden_tree = me.gather(hidden_own, 1)
    hidden_all = jnp.concatenate([hidden_tree, me.swap_core(hidden_tree)], 0)

    def gates_of(h, on):
        logits = nn(h, router_full)
        logits = jnp.where(on > 0, logits, -1e30)
        peak = jnp.max(logits, axis=-1, keepdims=True)
        e = jnp.exp(logits - peak) * on
        return e / jnp.sum(e, axis=-1, keepdims=True)

    gates_all = gates_of(hidden_all, jnp.concatenate([routed, routed_other], 0))
    gates = gates_all[:tree_len]

    mixed = jnp.zeros((2 * tree_len, width), F32)
    grad_hidden = jnp.zeros((2 * tree_len, width), F32)
    grad_gate_columns = []
    sums = []
    for j in range(per_core):
        which = me.core * per_core + j
        gate_w = lax.dynamic_index_in_dim(w_gate, which, 0, keepdims=False)
        up_w = lax.dynamic_index_in_dim(w_up, which, 0, keepdims=False)
        down_w = lax.dynamic_index_in_dim(w_down, which, 0, keepdims=False)
        gate = lax.dynamic_slice_in_dim(
            gates_all, me.member * (2 * per_core) + which, 1, 1
        )
        gate_pre = nn(hidden_all, gate_w)
        up_pre = nn(hidden_all, up_w)
        grad_mid = nt(grad_all, down_w)
        sig = jax.nn.sigmoid(gate_pre)
        silu = gate_pre * sig
        mid = silu * up_pre
        grad_gate_columns.append(jnp.sum(grad_mid * mid, axis=-1, keepdims=True))
        act = (gate * mid).astype(BF)
        mixed = mixed + nn(act, down_w)
        grad_mid = gate * grad_mid
        grad_gate_pre = (grad_mid * up_pre * sig * (1.0 + gate_pre * (1.0 - sig))).astype(BF)
        grad_up_pre = (grad_mid * silu).astype(BF)
        grad_hidden = grad_hidden + nt(grad_gate_pre, gate_w) + nt(grad_up_pre, up_w)
        own = jnp.stack(
            [
                tn(hidden_all, grad_gate_pre).astype(BF),
                tn(hidden_all, grad_up_pre).astype(BF),
                tn(grad_all, act).astype(BF),
            ]
        )
        chunk = width // me.chips
        sums.append(
            me.ring_scatter(
                lambda chip, own=own: lax.dynamic_slice_in_dim(own, chip * chunk, chunk, 1)
            )
        )

    def over_cores(v):
        return v[:tree_len] + me.swap_core(v[tree_len:].astype(BF)).astype(F32)

    mixed = over_cores(mixed)
    grad_hidden = over_cores(grad_hidden)
    placed = lax.dynamic_update_slice_in_dim(
        jnp.zeros((tree_len, width), F32), middle, me.member * columns, 1
    )
    result = me.scatter(mixed + placed, 0).astype(BF)

    own_columns = jnp.concatenate(grad_gate_columns, 1)
    both = me.in_order(
        me.core, own_columns[:tree_len], me.swap_core(own_columns[tree_len:]), 1
    )
    grad_gates = me.gather(both, 1)
    grad_logits = (
        gates * (grad_gates - jnp.sum(gates * grad_gates, axis=-1, keepdims=True))
    ).astype(BF)
    grad_router = tn(hidden_own, grad_logits)
    grad_hidden_two = nt(grad_logits, w_router) + me.scatter(grad_hidden, 1)
    grad_gain_two = jnp.sum(grad_hidden_two * normed_two, axis=0)
    scaled = grad_hidden_two * gain_two
    mean = me.total(jnp.sum(scaled * normed_two, axis=-1, keepdims=True)) / width
    grad_own = me.part(grad_tree, 1, me.member).astype(F32)
    grad_middle = grad_own + inv_two * (scaled - normed_two * mean)
    grad_branch = grad_middle.astype(BF)
    grad_out = me.all_reduce(tn(attended_full, grad_branch))
    grad_attended = me.scatter(nt(grad_branch, w_out), 1).astype(BF)

    grad_h = grad_attended.reshape(tree_len, kv_heads, per_key, HEAD_DIM).transpose(1, 2, 0, 3)

    def head_backward(operands):
        q, k, v, g, log_one = operands
        probs = jnp.exp(scores_of(q, k) - log_one)
        probs_low = probs.astype(BF)
        grad_probs = jnp.einsum("gqd,kd->gqk", g, v, preferred_element_type=F32)
        grad_v = jnp.einsum("gqk,gqd->kd", probs_low, g, preferred_element_type=F32)
        delta = jnp.sum(probs * grad_probs, axis=-1, keepdims=True)
        grad_s = (probs * (grad_probs - delta) * scale).astype(BF)
        grad_q = jnp.einsum("gqk,kd->gqd", grad_s, k, preferred_element_type=F32)
        grad_k = jnp.einsum("gqk,gqd->kd", grad_s, q, preferred_element_type=F32)
        return (grad_q, grad_k, grad_v)

    grad_q, grad_k, grad_v = lax.map(head_backward, (query_h, key_h, value_h, grad_h, log_total))
    grad_q = grad_q.transpose(2, 0, 1, 3).reshape(tree_len, q_heads, HEAD_DIM)
    grad_q = rotate(grad_q, tables, -1.0).reshape(tree_len, q_width).astype(BF)
    grad_k = rotate(grad_k.transpose(1, 0, 2), tables, -1.0)
    grad_k = grad_k.reshape(tree_len, k_width).astype(BF)
    grad_v = grad_v.transpose(1, 0, 2).reshape(tree_len, k_width).astype(BF)
    grad_q_full = me.gather(grad_q, 1)
    grad_k_full = me.gather(grad_k, 1)
    grad_v_full = me.gather(grad_v, 1)
    grad_query = me.all_reduce(tn(hidden_first, grad_q_full))
    grad_key = me.all_reduce(tn(hidden_first, grad_k_full))
    grad_value = me.all_reduce(tn(hidden_first, grad_v_full))
    grad_hidden_one = (
        nt(grad_q_full, w_query) + nt(grad_k_full, key_weight) + nt(grad_v_full, value_weight)
    )
    grad_gain_one = jnp.sum(grad_hidden_one * normed_one, axis=0)
    scaled = grad_hidden_one * gain_one
    mean = me.total(jnp.sum(scaled * normed_one, axis=-1, keepdims=True)) / width
    input_grad = (grad_middle + inv_one * (scaled - normed_one * mean)).astype(BF)
    input_grad = me.exchange(input_grad, 0, 1)

    small = me.butterfly(
        jnp.concatenate([grad_gain_one[None], grad_gain_two[None], grad_router.T], 0)
    )

    stacked = jnp.stack(sums)
    half = width // me.reps
    mine = lax.dynamic_slice_in_dim(stacked, me.core * half, half, 2)
    other = me.swap_core(
        lax.dynamic_slice_in_dim(stacked, (1 - me.core) * half, half, 2)
    )
    ordered = me.in_order(me.core, mine, other, 0).astype(F32)

    return (
        result,
        input_grad,
        small[0],
        grad_query,
        grad_key,
        grad_value,
        grad_out,
        small[1],
        small[2:].T,
        ordered[:, 0],
        ordered[:, 1],
        ordered[:, 2].transpose(0, 2, 1),
    )


def solution(mesh):
    return jax.shard_map(
        local,
        mesh=mesh,
        in_specs=(
            P(("rep", "shard"), None),
            P("shard"),
            P("shard", None),
            P("shard", None),
            P("shard", None),
            P(None, "shard"),
            P("shard"),
            P("shard", None),
            P("shard", None, None),
            P("shard", None, None),
            P("shard", None, None),
            P("rep", None),
            P(("rep", "shard"), None),
            P(("rep", "shard"), None),
        ),
        out_specs=(
            P(("rep", "shard"), None),
            P(("rep", "shard"), None),
            P("shard"),
            P("shard", None),
            P("shard", None),
            P("shard", None),
            P(None, "shard"),
            P("shard"),
            P("shard", None),
            P("shard", "rep", None),
            P("shard", "rep", None),
            P("shard", None, "rep"),
        ),
        check_vma=False,
    )
```

time: 2960 us -> 822 us (0.28)
  waiting for transfers between devices: 2320 us -> 256 us
  starting transfers between devices: 1.23 us -> 143 us
  local copies, waits for them, and re-layouts: 142 us -> 31.4 us
  blocking collectives: 98.5 us -> 0 us
  matrix products: 271 us -> 308 us
    all_gather x7 -> x0, waiting for transfers between devices: 863 us -> none  [the longest x1 277 us: local(): lax.all_gather(w_down, 'shard', axis=0, tiled=True)]
    unnamed x26 -> x0, waiting for transfers between devices: 858 us -> none
    reduce_scatter x8 -> x0, waiting for transfers between devices: 527 us -> none  [the longest x1 136 us: local(): lax.psum_scatter(grad_up_local.astype(jnp.bfloat16), 'rep', scatter_dimen...]
    ppermute x0 -> x124, waiting for transfers between devices: none -> 256 us  [the longest x84 173 us: along_ring(): return lax.ppermute(v, 'rep', self.ring)]
    ppermute x0 -> x124, starting transfers between devices: none -> 143 us  [the longest x84 116 us: along_ring(): return lax.ppermute(v, 'rep', self.ring)]
    psum x1 -> x0, waiting for transfers between devices: 75.6 us -> none  [local(): lax.psum(shard_sums[1].astype(jnp.bfloat16), 'rep').astype(jnp.float32)]
    psum x1 -> x0, blocking collectives: 62.6 us -> none  [local(): lax.psum(shard_sums[0].astype(jnp.bfloat16), 'rep').astype(jnp.float32)]
    dot_general x80 -> x79, matrix products: 271 us -> 308 us  [the longest x51 209 us: dot(): return lax.dot_general(a, b, (dims, ((), ())), preferred_element_type=F32)]
  transfers between devices with their start and end apart: 21 -> 124, of which waited for: 19 -> 75; matrix products, arithmetic and copies ran while one was open for 9% -> 40% of each run, Pallas kernels for 0% -> 0%
where the time goes in v1:
time: 822 us; the launch traced here: 813 us
  matrix products  308 us (37%)
  waiting for transfers between devices  256 us (31%)
  starting transfers between devices  143 us (17%)
  other arithmetic  71.7 us (9%)
  local copies, waits for them, and re-layouts  31.4 us (4%)
    dot_general x51, matrix products, dot(): return lax.dot_general(a, b, (dims, ((), ())), preferred_element_type=F32)  209 us
    ppermute x84, waiting for transfers between devices, along_ring(): return lax.ppermute(v, 'rep', self.ring)  173 us
    ppermute x84, starting transfers between devices, along_ring(): return lax.ppermute(v, 'rep', self.ring)  116 us
    ppermute x21, waiting for transfers between devices, swap_shard(): return lax.ppermute(v, 'shard', [(0, 1), (1, 0)])  72.9 us
    dot_general x4, matrix products, head_backward(): grad_q = jnp.einsum('gqk,kd->gqd', grad_s, k, preferred_element_type=F32)  23.5 us
    convert_element_type x48, other arithmetic, ring_scatter(): held = (came.astype(F32) + mine.astype(F32)).astype(BF)  23.3 us
    dot_general x4, matrix products, head_backward(): grad_k = jnp.einsum('gqk,gqd->kd', grad_s, q, preferred_element_type=F32)  23.2 us
    ppermute x21, starting transfers between devices, swap_shard(): return lax.ppermute(v, 'shard', [(0, 1), (1, 0)])  21.8 us
  transfers between devices with their start and end apart: 124, of which 75 were waited for; matrix products, arithmetic and copies ran while one was open for 40% of the time, Pallas kernels for 0%

profile of v1, /device:TPU:0, one launch (start us, length us, event | category | flops | bytes accessed | tf_op | source)
XLA Modules:
  0.0 813.1 jit_solution(991487326367096290)
XLA Ops:
  8.3 5.9 collective-permute-done.3
  26.9 15.5 %collective-permute-done.5 = bf16[448,256]{1,0:T(8,128)(2,1)S(1)} collective-permute-done((bf16[448,256]{1,0:T(8,128)(2,1)S(1)}, bf16[448,256]{1,0:T(8,128)(2,1)S(1)}, u32[]{:S(2)}, u32[]{:S(2)}) %collective-permute-start.5) | collective-permute-done | bytes 229408 | tf_op jit(solution)/shard_map/ppermute | solution.py:101
  55.9 22.4 %while.30 = (s32[]{:T(128)}, bf16[4,3,448,64]{2,3,1,0:T(8,128)(2,1)}, f32[4,3,448,1]{2,1,3,0:T(4,128)}, bf16[4,3,448,64]{2,3,1,0:T(8,128)(2,1)S(1)}, bf16[4,448,...) while((s32[]{:T(128)}, ...), condition=%wide.region_7.8_spmd.clone.clone, body=%wide.region_4.7_spmd.clone.sunk.clone | while | flops 162769600 | bytes 8831581 | solution.py:273
  82.9 16.5 %collective-permute-done.7 = bf16[448,768]{1,0:T(8,128)(2,1)S(1)} collective-permute-done((bf16[448,768]{1,0:T(8,128)(2,1)}, bf16[448,768]{1,0:T(8,128)(2,1)S(1)}, u32[]{:S(2)}, u32[]{:S(2)}) %collective-permute-start.7) | collective-permute-done | bytes 688160 | tf_op jit(solution)/shard_map/ppermute | solution.py:101
  104.1 7.4 collective-permute-done.14
  115.1 16.7 %collective-permute-done.9 = bf16[448,768]{1,0:T(8,128)(2,1)S(1)} collective-permute-done((bf16[448,768]{1,0:T(8,128)(2,1)S(1)}, bf16[448,768]{1,0:T(8,128)(2,1)S(1)}, u32[]{:S(2)}, u32[]{:S(2)}) %collective-permute-start.9) | collective-permute-done | bytes 688160 | tf_op jit(solution)/shard_map/ppermute | solution.py:101
  207.2 5.5 fusion.125
  244.9 5.8 fusion.119
  298.2 17.7 %add_add_fusion = f32[896,1536]{1,0:T(8,128)} fusion(f32[896,1536]{1,0:T(8,128)} %fusion.107, f32[896,1536]{1,0:T(8,128)} %fusion.115, f32[896,1536]{1,0:T(8,128)} %fusion.119, f32[896,1536]{1,0:T(8,128)} %fusion.127, f32[896,1536]{1,0:T(8,128)} %fusion.131, f32[896,1536]{1,0:T(8,128)} %fusion.143, f32[896,1536]{1,0:T(8,128)} %fusion.139, ...), kind=kOutput, calls=%fused_computation.68 | convolution fusion | flops 1418919936 | bytes 46530564 | tf_op jit(solution)/shard_map/dot_general | solution.py:60
  316.0 6.3 fusion.113
  324.0 11.3 %add_add_fusion.1 = f32[896,1536]{1,0:T(8,128)} fusion(f32[896,1536]{1,0:T(8,128)} %fusion.113, f32[896,1536]{1,0:T(8,128)} %fusion.137, f32[896,1536]{1,0:T(8,128)} %fusion.125, bf16[896,512]{0,1:T(8,128)(2,1)S(1)} %get-tuple-element.236, bf16[8,512,1536]{2,1,0:T(8,128)(2,1)} %param.28, s32[]{:T(128)S(6)} %select_n.981), kind=kOutput, calls=%fused_computation.69 | convolution fusion | flops 1413414912 | bytes 24510468 | tf_op jit(solution)/shard_map/dot_general | solution.py:60
  426.1 87.3 %while.31 = (s32[]{:T(128)}, f32[4,3,448,64]{2,3,1,0:T(8,128)}, f32[4,448,64]{1,2,0:T(8,128)}, bf16[4,448,64]{1,2,0:T(8,128)(2,1)}, bf16[4,3,448,64]{2,3,1,0:T(8...) while((s32[]{:T(128)}, f32[4,3,448,64]{2,3,1,0:T(8,128)}, ...), condition=%wide.region_19.20_spmd.clone.clone, body=%wide.region_17.19_spmd.clone.sunk.clone | while | flops 395189760 | bytes 31687544 | solution.py:376
  433.4 5.9 fusion.354
  439.2 5.8 fusion.355
  455.2 5.9 fusion.354
  461.1 5.8 fusion.355
  477.0 5.9 fusion.354
  482.9 5.8 fusion.355
  498.8 5.9 fusion.354
  504.7 5.8 fusion.355
  542.7 9.4 %collective-permute-done.80 = bf16[96,768]{1,0:T(8,128)(2,1)S(1)} collective-permute-done((bf16[96,768]{1,0:T(8,128)(2,1)S(1)}, bf16[96,768]{1,0:T(8,128)(2,1)S(1)}, u32[]{:S(2)}, u32[]{:S(2)}) %collective-permute-start.80) | collective-permute-done | bytes 147488 | tf_op jit(solution)/shard_map/ppermute | solution.py:107
  612.7 8.1 collective-permute-done.52
  690.3 8.1 collective-permute-done.76
  715.5 6.7 collective-permute-done.85
  (683 shorter events, 622.0 us)
Async XLA Ops:
  196.3 142.3 %collective-permute-start.95 = (bf16[3,192,512]{2,1,0:T(8,128)(2,1)S(1)}, bf16[3,192,512]{2,1,0:T(8,128)(2,1)}, u32[]{:S(2)}, u32[]{:S(2)}) collective-permute-start(bf16[3,192,512]{2,1,0:T(8,128)(2,1)S(1)} %constant_dynamic-slice_fusion.5), channel_id=1, source_target_pairs={{0,8},{2,6},{8,16},{10,2},{16,24},{18,10},{24,28},{26,18},{28,20},... | collective-permute-start | bytes 1769480 | tf_op jit(solution)/shard_map/ppermute | solution.py:107
  234.0 106.0 %collective-permute-start.102 = (bf16[3,192,512]{2,1,0:T(8,128)(2,1)S(1)}, bf16[3,192,512]{2,1,0:T(8,128)(2,1)}, u32[]{:S(2)}, u32[]{:S(2)}) collective-permute-start(bf16[3,192,512]{2,1,0:T(8,128)(2,1)S(1)} %constant_dynamic-slice_fusion.4), channel_id=1, source_target_pairs={{0,8},{2,6},{8,16},{10,2},{16,24},{18,10},{24,28},{26,18},{28,20},... | collective-permute-start | bytes 1769480 | tf_op jit(solution)/shard_map/ppermute | solution.py:107
  266.6 76.2 %collective-permute-start.109 = (bf16[3,192,512]{2,1,0:T(8,128)(2,1)S(1)}, bf16[3,192,512]{2,1,0:T(8,128)(2,1)}, u32[]{:S(2)}, u32[]{:S(2)}) collective-permute-start(bf16[3,192,512]{2,1,0:T(8,128)(2,1)S(1)} %constant_dynamic-slice_fusion.3), channel_id=1, source_target_pairs={{0,8},{2,6},{8,16},{10,2},{16,24},{18,10},{24,28},{26,18},{28,20},... | collective-permute-start | bytes 1769480 | tf_op jit(solution)/shard_map/ppermute | solution.py:107
  296.6 49.1 %collective-permute-start.116 = (bf16[3,192,512]{2,1,0:T(8,128)(2,1)S(1)}, bf16[3,192,512]{2,1,0:T(8,128)(2,1)}, u32[]{:S(2)}, u32[]{:S(2)}) collective-permute-start(bf16[3,192,512]{2,1,0:T(8,128)(2,1)S(1)} %constant_dynamic-slice_fusion.2), channel_id=1, source_target_pairs={{0,8},{2,6},{8,16},{10,2},{16,24},{18,10},{24,28},{26,18},{28,20},... | collective-permute-start | bytes 1769480 | tf_op jit(solution)/shard_map/ppermute | solution.py:107
  337.5 35.3 %collective-permute-start.12 = (bf16[448,1536]{1,0:T(8,128)(2,1)S(1)}, bf16[448,1536]{1,0:T(8,128)(2,1)S(1)}, u32[]{:S(2)}, u32[]{:S(2)}) collective-permute-start(bf16[448,1536]{1,0:T(8,128)(2,1)S(1)} %slice.136), channel_id=1, source_target_pairs={{0,2},{2,0},{4,6},{6,4},{8,10},{10,8},{12,14},{14,12},{16,18},{18,... | collective-permute-start | bytes 4128776 | tf_op jit(solution)/shard_map/ppermute | solution.py:104
  400.7 137.2 %collective-permute-start.79 = (bf16[768,768]{1,0:T(8,128)(2,1)}, bf16[768,768]{1,0:T(8,128)(2,1)}, u32[]{:S(2)}, u32[]{:S(2)}) collective-permute-start(bf16[768,768]{1,0:T(8,128)(2,1)} %constant_dynamic-slice_fusion.7), channel_id=1, source_target_pairs={{0,2},{2,0},{4,6},{6,4},{8,10},{10,8},{12,14},{14,12},{16,18},{18,... | collective-permute-start | bytes 3538952 | tf_op jit(solution)/shard_map/ppermute | solution.py:104
  406.8 106.6 %collective-permute-start.13 = (bf16[224,1536]{1,0:T(8,128)(2,1)}, bf16[224,1536]{1,0:T(8,128)(2,1)}, u32[]{:S(2)}, u32[]{:S(2)}) collective-permute-start(bf16[224,1536]{1,0:T(8,128)(2,1)} %dynamic-slice_convert_fusion.2), channel_id=1, source_target_pairs={{0,1},{1,0},{2,3},{3,2},{4,5},{5,4},{6,7},{7,6},{8,9},{9,8},{10,11... | collective-permute-start | bytes 2064392 | tf_op jit(solution)/shard_map/ppermute | solution.py:101
  413.1 107.0 %collective-permute-start.99 = (bf16[3,192,512]{2,1,0:T(8,128)(2,1)}, bf16[3,192,512]{2,1,0:T(8,128)(2,1)}, u32[]{:S(2)}, u32[]{:S(2)}) collective-permute-start(bf16[3,192,512]{2,1,0:T(8,128)(2,1)} %add_convert_fusion.28), channel_id=1, source_target_pairs={{0,8},{2,6},{8,16},{10,2},{16,24},{18,10},{24,28},{26,18},{28,20},... | collective-permute-start | bytes 1769480 | tf_op jit(solution)/shard_map/ppermute | solution.py:107
  419.4 102.7 %collective-permute-start.106 = (bf16[3,192,512]{2,1,0:T(8,128)(2,1)}, bf16[3,192,512]{2,1,0:T(8,128)(2,1)}, u32[]{:S(2)}, u32[]{:S(2)}) collective-permute-start(bf16[3,192,512]{2,1,0:T(8,128)(2,1)} %add_convert_fusion.21), channel_id=1, source_target_pairs={{0,8},{2,6},{8,16},{10,2},{16,24},{18,10},{24,28},{26,18},{28,20},... | collective-permute-start | bytes 1769480 | tf_op jit(solution)/shard_map/ppermute | solution.py:107
  422.0 103.2 %collective-permute-start.113 = (bf16[3,192,512]{2,1,0:T(8,128)(2,1)}, bf16[3,192,512]{2,1,0:T(8,128)(2,1)}, u32[]{:S(2)}, u32[]{:S(2)}) collective-permute-start(bf16[3,192,512]{2,1,0:T(8,128)(2,1)} %add_convert_fusion.14), channel_id=1, source_target_pairs={{0,8},{2,6},{8,16},{10,2},{16,24},{18,10},{24,28},{26,18},{28,20},... | collective-permute-start | bytes 1769480 | tf_op jit(solution)/shard_map/ppermute | solution.py:107
  525.2 35.5 %collective-permute-start.22 = (bf16[448,768]{1,0:T(8,128)(2,1)S(1)}, bf16[448,768]{1,0:T(8,128)(2,1)S(1)}, u32[]{:S(2)}, u32[]{:S(2)}) collective-permute-start(bf16[448,768]{1,0:T(8,128)(2,1)S(1)} %copy-done.28), channel_id=1, source_target_pairs={{0,1},{1,0},{2,3},{3,2},{4,5},{5,4},{6,7},{7,6},{8,9},{9,8},{10,11... | collective-permute-start | bytes 2064392 | tf_op jit(solution)/shard_map/ppermute | solution.py:101
  527.1 64.1 %collective-permute-start.100 = (bf16[3,192,512]{2,1,0:T(8,128)(2,1)S(1)}, bf16[3,192,512]{2,1,0:T(8,128)(2,1)S(1)}, u32[]{:S(2)}, u32[]{:S(2)}) collective-permute-start(bf16[3,192,512]{2,1,0:T(8,128)(2,1)S(1)} %add_convert_fusion.27), channel_id=1, source_target_pairs={{0,8},{2,6},{8,16},{10,2},{16,24},{18,10},{24,28},{26,18},{28,20},... | collective-permute-start | bytes 1769480 | tf_op jit(solution)/shard_map/ppermute | solution.py:107
  529.7 62.9 %collective-permute-start.107 = (bf16[3,192,512]{2,1,0:T(8,128)(2,1)S(1)}, bf16[3,192,512]{2,1,0:T(8,128)(2,1)S(1)}, u32[]{:S(2)}, u32[]{:S(2)}) collective-permute-start(bf16[3,192,512]{2,1,0:T(8,128)(2,1)S(1)} %add_convert_fusion.20), channel_id=1, source_target_pairs={{0,8},{2,6},{8,16},{10,2},{16,24},{18,10},{24,28},{26,18},{28,20},... | collective-permute-start | bytes 1769480 | tf_op jit(solution)/shard_map/ppermute | solution.py:107
  540.6 54.1 %collective-permute-start.114 = (bf16[3,192,512]{2,1,0:T(8,128)(2,1)S(1)}, bf16[3,192,512]{2,1,0:T(8,128)(2,1)S(1)}, u32[]{:S(2)}, u32[]{:S(2)}) collective-permute-start(bf16[3,192,512]{2,1,0:T(8,128)(2,1)S(1)} %add_convert_fusion.13), channel_id=1, source_target_pairs={{0,8},{2,6},{8,16},{10,2},{16,24},{18,10},{24,28},{26,18},{28,20},... | collective-permute-start | bytes 1769480 | tf_op jit(solution)/shard_map/ppermute | solution.py:107
  560.3 36.5 %collective-permute-start.121 = (bf16[3,192,512]{2,1,0:T(8,128)(2,1)S(1)}, bf16[3,192,512]{2,1,0:T(8,128)(2,1)S(1)}, u32[]{:S(2)}, u32[]{:S(2)}) collective-permute-start(bf16[3,192,512]{2,1,0:T(8,128)(2,1)S(1)} %add_convert_fusion.6), channel_id=1, source_target_pairs={{0,8},{2,6},{8,16},{10,2},{16,24},{18,10},{24,28},{26,18},{28,20},... | collective-permute-start | bytes 1769480 | tf_op jit(solution)/shard_map/ppermute | solution.py:107
  591.3 131.0 %collective-permute-start.31 = (bf16[384,1536]{1,0:T(8,128)(2,1)S(1)}, bf16[384,1536]{1,0:T(8,128)(2,1)S(1)}, u32[]{:S(2)}, u32[]{:S(2)}) collective-permute-start(bf16[384,1536]{1,0:T(8,128)(2,1)S(1)} %constant_dynamic-slice_fusion.13), channel_id=1, source_target_pairs={{0,2},{2,0},{4,6},{6,4},{8,10},{10,8},{12,14},{14,12},{16,18},{18,... | collective-permute-start | bytes 3538952 | tf_op jit(solution)/shard_map/ppermute | solution.py:104
  592.6 65.0 %collective-permute-start.26 = (bf16[224,768]{1,0:T(8,128)(2,1)S(1)}, bf16[224,768]{1,0:T(8,128)(2,1)S(1)}, u32[]{:S(2)}, u32[]{:S(2)}) collective-permute-start(bf16[224,768]{1,0:T(8,128)(2,1)S(1)} %get-tuple-element.252), channel_id=1, source_target_pairs={{0,1},{1,0},{2,3},{3,2},{4,5},{5,4},{6,7},{7,6},{8,9},{9,8},{10,11... | collective-permute-start | bytes 1032200 | tf_op jit(solution)/shard_map/ppermute | solution.py:101
  600.2 112.0 %collective-permute-start.101 = (bf16[3,192,512]{2,1,0:T(8,128)(2,1)S(1)}, bf16[3,192,512]{2,1,0:T(8,128)(2,1)S(1)}, u32[]{:S(2)}, u32[]{:S(2)}) collective-permute-start(bf16[3,192,512]{2,1,0:T(8,128)(2,1)S(1)} %add_convert_fusion.26), channel_id=1, source_target_pairs={{0,8},{2,6},{8,16},{10,2},{16,24},{18,10},{24,28},{26,18},{28,20},... | collective-permute-start | bytes 1769480 | tf_op jit(solution)/shard_map/ppermute | solution.py:107
  609.7 104.5 %collective-permute-start.108 = (bf16[3,192,512]{2,1,0:T(8,128)(2,1)S(1)}, bf16[3,192,512]{2,1,0:T(8,128)(2,1)S(1)}, u32[]{:S(2)}, u32[]{:S(2)}) collective-permute-start(bf16[3,192,512]{2,1,0:T(8,128)(2,1)S(1)} %add_convert_fusion.19), channel_id=1, source_target_pairs={{0,8},{2,6},{8,16},{10,2},{16,24},{18,10},{24,28},{26,18},{28,20},... | collective-permute-start | bytes 1769480 | tf_op jit(solution)/shard_map/ppermute | solution.py:107
  688.0 46.1 %collective-permute-start.115 = (bf16[3,192,512]{2,1,0:T(8,128)(2,1)S(1)}, bf16[3,192,512]{2,1,0:T(8,128)(2,1)S(1)}, u32[]{:S(2)}, u32[]{:S(2)}) collective-permute-start(bf16[3,192,512]{2,1,0:T(8,128)(2,1)S(1)} %add_convert_fusion.12), channel_id=1, source_target_pairs={{0,8},{2,6},{8,16},{10,2},{16,24},{18,10},{24,28},{26,18},{28,20},... | collective-permute-start | bytes 1769480 | tf_op jit(solution)/shard_map/ppermute | solution.py:107
  714.2 87.6 %collective-permute-start.78 = (bf16[384,512]{1,0:T(8,128)(2,1)S(1)}, bf16[384,512]{1,0:T(8,128)(2,1)S(1)}, u32[]{:S(2)}, u32[]{:S(2)}) collective-permute-start(bf16[384,512]{1,0:T(8,128)(2,1)S(1)} %constant_dynamic-update-slice_fusion.8), channel_id=1, source_target_pairs={{0,2},{2,0},{4,6},{6,4},{8,10},{10,8},{12,14},{14,12},{16,18},{18,... | collective-permute-start | bytes 1179656 | tf_op jit(solution)/shard_map/ppermute | solution.py:104
  722.2 81.0 %collective-permute-start.62 = (bf16[384,512]{1,0:T(8,128)(2,1)S(1)}, bf16[384,512]{1,0:T(8,128)(2,1)S(1)}, u32[]{:S(2)}, u32[]{:S(2)}) collective-permute-start(bf16[384,512]{1,0:T(8,128)(2,1)S(1)} %constant_dynamic-update-slice_fusion.16), channel_id=1, source_target_pairs={{0,2},{2,0},{4,6},{6,4},{8,10},{10,8},{12,14},{14,12},{16,18},{18,... | collective-permute-start | bytes 1179656 | tf_op jit(solution)/shard_map/ppermute | solution.py:104
  751.6 53.0 %collective-permute-start.123 = (bf16[4,3,96,512]{3,2,1,0:T(8,128)(2,1)S(1)}, bf16[4,3,96,512]{3,2,1,0:T(8,128)(2,1)S(1)}, u32[]{:S(2)}, u32[]{:S(2)}) collective-permute-start(bf16[4,3,96,512]{3,2,1,0:T(8,128)(2,1)S(1)} %get-tuple-element.244), channel_id=1, source_target_pairs={{0,2},{2,0},{4,6},{6,4},{8,10},{10,8},{12,14},{14,12},{16,18},{18,... | collective-permute-start | bytes 3538952 | tf_op jit(solution)/shard_map/ppermute | solution.py:104
  768.6 38.7 %collective-permute-start.94 = (bf16[768,768]{1,0:T(8,128)(2,1)S(1)}, bf16[768,768]{1,0:T(8,128)(2,1)S(1)}, u32[]{:S(2)}, u32[]{:S(2)}) collective-permute-start(bf16[768,768]{1,0:T(8,128)(2,1)S(1)} %constant_dynamic-update-slice_fusion), channel_id=1, source_target_pairs={{0,2},{2,0},{4,6},{6,4},{8,10},{10,8},{12,14},{14,12},{16,18},{18,... | collective-permute-start | bytes 3538952 | tf_op jit(solution)/shard_map/ppermute | solution.py:104
  (178 other events, 2027.3 us)

commit v2 on v1

--- a/solution.py
+++ b/solution.py
@@ -1,12 +1,18 @@
+import functools
+
 import jax
 import jax.numpy as jnp
 from jax import lax
+from jax.experimental import pallas as pl
+from jax.experimental.pallas import tpu as pltpu
 from jax.sharding import PartitionSpec as P
 
 HEAD_DIM = 64
+LANES = 128
 EPS = 1e-06
 BF = jnp.bfloat16
 F32 = jnp.float32
+VMEM_LIMIT = 60 << 20
 
 
 def tree_layout(position, seg_len):
@@ -40,19 +46,14 @@
     return related & (key_index[None, :] <= query_index[:, None])
 
 
-def angle_tables(depth_position, half_dim):
-    frequency = 10000.0 ** (-2.0 * jnp.arange(half_dim, dtype=F32) / (2 * half_dim))
+def angle_tables(depth_position):
+    half = HEAD_DIM // 2
+    frequency = 10000.0 ** (-2.0 * jnp.arange(half, dtype=F32) / HEAD_DIM)
     angles = depth_position.astype(F32)[:, None] * frequency[None, :]
-    return (jnp.cos(angles)[:, None, :], jnp.sin(angles)[:, None, :])
-
-
-def rotate(values, tables, sign):
-    cosine, sine = tables
-    half = values.shape[-1] // 2
-    first = values[..., :half]
-    second = values[..., half:]
-    return jnp.concatenate(
-        [first * cosine - sign * second * sine, second * cosine + sign * first * sine], axis=-1
+    cosine, sine = jnp.cos(angles), jnp.sin(angles)
+    return (
+        jnp.concatenate([cosine] * 4, 1),
+        jnp.concatenate([-sine, sine, -sine, sine], 1),
     )
 
 
@@ -186,6 +187,324 @@
             v = v + lax.ppermute(v, "rep", [(r, r ^ bit) for r in range(self.reps)])
             bit *= 2
         return v
+
+
+def pairs(heads):
+    return -(-heads // 2)
+
+
+def rope(v, cos, sin, back):
+    lane = lax.broadcasted_iota(jnp.int32, (1, LANES), 1)
+    first = lane % HEAD_DIM < HEAD_DIM // 2
+    out = []
+    for i in range(v.shape[1] // LANES):
+        x = v[:, i * LANES : (i + 1) * LANES]
+        other = jnp.where(
+            first,
+            pltpu.roll(x, LANES - HEAD_DIM // 2, 1),
+            pltpu.roll(x, HEAD_DIM // 2, 1),
+        )
+        out.append(x * cos - other * sin if back else x * cos + other * sin)
+    return out
+
+
+def halves(x, parity):
+    low = lax.broadcasted_iota(jnp.int32, (1, LANES), 1) < HEAD_DIM
+    zero = jnp.zeros_like(x)
+    turned = pltpu.roll(x, HEAD_DIM, 1)
+    a, b = (x, turned) if parity == 0 else (turned, x)
+    return jnp.where(low, a, zero).astype(BF), jnp.where(low, zero, b).astype(BF)
+
+
+def attend_kernel(
+    q_heads, kv_heads, own_ref, came_ref, cos_ref, sin_ref, bias_ref,
+    out_ref, lse_ref, q_ref, k_ref, v_ref,
+):
+    per = q_heads // kv_heads
+    rows = own_ref.shape[0]
+    qp, kp = pairs(q_heads), pairs(kv_heads)
+    cos, sin = cos_ref[...], sin_ref[...]
+    raw = own_ref[...].astype(F32) + came_ref[...].astype(F32)
+    scale = HEAD_DIM**-0.5
+    q = [(t * scale).astype(BF) for t in rope(raw[:, : qp * LANES], cos, sin, False)]
+    keys = rope(raw[:, qp * LANES : (qp + kp) * LANES], cos, sin, False)
+    for i in range(qp):
+        q_ref[:, i * LANES : (i + 1) * LANES] = q[i]
+    ks, vs = [], []
+    for g in range(kv_heads):
+        at = (qp + kp + g // 2) * LANES
+        ks.append(halves(keys[g // 2], g % 2))
+        vs.append(halves(raw[:, at : at + LANES], g % 2))
+        for p in range(2):
+            k_ref[g, p] = ks[g][p]
+            v_ref[g, p] = vs[g][p]
+    half = rows // 2
+    for lo, n in ((0, half), (half, rows)):
+        bias = bias_ref[lo : lo + half, :n]
+        for i in range(qp):
+            out = jnp.zeros((half, LANES), F32)
+            for h in range(2 * i, min(2 * i + 2, q_heads)):
+                g, p = h // per, h % 2
+                s = nt(q[i][lo : lo + half], ks[g][p][:n]) + bias
+                peak = jnp.max(s, axis=-1, keepdims=True)
+                e = jnp.exp(s - peak)
+                total = jnp.sum(e, axis=-1, keepdims=True)
+                lse_ref[lo : lo + half, h : h + 1] = peak + jnp.log(total)
+                out = out + nn((e * (1.0 / total)).astype(BF), vs[g][p][:n])
+            out_ref[lo : lo + half, i * LANES : (i + 1) * LANES] = out.astype(BF)
+
+
+def attend(own, came, cos, sin, bias, q_heads, kv_heads):
+    rows = own.shape[0]
+    qp = pairs(q_heads)
+    return pl.pallas_call(
+        functools.partial(attend_kernel, q_heads, kv_heads),
+        out_shape=[
+            jax.ShapeDtypeStruct((rows, qp * LANES), BF),
+            jax.ShapeDtypeStruct((rows, LANES), F32),
+            jax.ShapeDtypeStruct((rows, qp * LANES), BF),
+            jax.ShapeDtypeStruct((kv_heads, 2, rows, LANES), BF),
+            jax.ShapeDtypeStruct((kv_heads, 2, rows, LANES), BF),
+        ],
+        compiler_params=pltpu.CompilerParams(vmem_limit_bytes=VMEM_LIMIT),
+        cost_estimate=pl.CostEstimate(
+            flops=1200 * rows * rows * q_heads,
+            bytes_accessed=8 << 20,
+            transcendentals=rows * rows * q_heads,
+        ),
+    )(own, came, cos, sin, bias)
+
+
+def attend_back_kernel(
+    q_heads, kv_heads, own_ref, came_ref, q_ref, k_ref, v_ref, lse_ref,
+    cos_ref, sin_ref, bias_ref, out_ref,
+):
+    per = q_heads // kv_heads
+    rows = own_ref.shape[0]
+    qp, kp = pairs(q_heads), pairs(kv_heads)
+    cos, sin = cos_ref[...], sin_ref[...]
+    scale = HEAD_DIM**-0.5
+    low = lax.broadcasted_iota(jnp.int32, (1, LANES), 1) < HEAD_DIM
+    grad = (own_ref[...].astype(F32) + came_ref[...].astype(F32)).astype(BF)
+    lse = lse_ref[...].T
+    half = rows // 2
+
+    def put(at, v):
+        out_ref[:, at * LANES : (at + 1) * LANES] = v.astype(BF)
+
+    def blocks():
+        return [
+            [[jnp.zeros((half, LANES), F32) for _ in range(2)] for _ in range(2)]
+            for _ in range(kv_heads)
+        ]
+
+    dk, dv = blocks(), blocks()
+    for i in range(qp):
+        parts = []
+        for lo, n in ((0, half), (half, rows)):
+            q = q_ref[lo : lo + half, i * LANES : (i + 1) * LANES]
+            go = grad[lo : lo + half, i * LANES : (i + 1) * LANES]
+            bias = bias_ref[:n, lo : lo + half]
+            dq = jnp.zeros((half, LANES), F32)
+            for h in range(2 * i, min(2 * i + 2, q_heads)):
+                g, p = h // per, h % 2
+                k, v = k_ref[g, p, :n], v_ref[g, p, :n]
+                s = nt(k, q) + bias
+                probs = jnp.exp(s - lse[h : h + 1, lo : lo + half])
+                dp = nt(v, go)
+                delta = jnp.sum(probs * dp, axis=0, keepdims=True)
+                ds = (probs * (dp - delta)).astype(BF)
+                dq = dq + tn(ds, k)
+                ck, cv = nn(ds, q), nn(probs.astype(BF), go)
+                for b in range(n // half):
+                    dk[g][p][b] = dk[g][p][b] + ck[b * half : (b + 1) * half]
+                    dv[g][p][b] = dv[g][p][b] + cv[b * half : (b + 1) * half]
+            parts.append(dq * scale)
+        put(i, rope(jnp.concatenate(parts, 0), cos, sin, True)[0])
+
+    def packed(d, j):
+        got = jnp.zeros((rows, LANES), F32)
+        for g in range(2 * j, min(2 * j + 2, kv_heads)):
+            a, b = (jnp.concatenate(d[g][p], 0) for p in range(2))
+            a, b = jnp.where(low, a, 0.0), jnp.where(low, 0.0, b)
+            if g % 2 == 0:
+                got = got + a + pltpu.roll(b, HEAD_DIM, 1)
+            else:
+                got = got + b + pltpu.roll(a, HEAD_DIM, 1)
+        return got
+
+    for j in range(kp):
+        put(qp + j, rope(packed(dk, j), cos, sin, True)[0])
+        put(qp + kp + j, packed(dv, j))
+
+
+def attend_back(own, came, q, k, v, lse, cos, sin, bias, q_heads, kv_heads):
+    rows = own.shape[0]
+    lanes = (pairs(q_heads) + 2 * pairs(kv_heads)) * LANES
+    return pl.pallas_call(
+        functools.partial(attend_back_kernel, q_heads, kv_heads),
+        out_shape=jax.ShapeDtypeStruct((rows, lanes), BF),
+        compiler_params=pltpu.CompilerParams(vmem_limit_bytes=VMEM_LIMIT),
+        cost_estimate=pl.CostEstimate(
+            flops=1600 * rows * rows * q_heads,
+            bytes_accessed=8 << 20,
+            transcendentals=rows * rows * q_heads,
+        ),
+    )(own, came, q, k, v, lse, cos, sin, bias)
+
+
+def expert_grads_kernel(
+    chained, where, h_ref, g_ref, on_ref, wg_ref, wu_ref, wd_ref, *refs
+):
+    if chained:
+        gg_in, refs = refs[0], refs[2:]
+    mid_ref, gg_ref, own_ref, *acc = refs
+    step, steps = pl.program_id(0), pl.num_programs(0)
+    h, g = h_ref[...], g_ref[...]
+    lane = lax.broadcasted_iota(jnp.int32, (1, on_ref.shape[1]), 1) == where[1]
+    on = jnp.sum(jnp.where(lane, on_ref[...], 0.0), axis=-1, keepdims=True)
+    gate_pre = nn(h, wg_ref[0])
+    up_pre = nn(h, wu_ref[0])
+    grad_mid = nt(g, wd_ref[0])
+    sig = 1.0 / (1.0 + jnp.exp(-gate_pre))
+    silu = gate_pre * sig
+    mid = silu * up_pre
+    column = jnp.where(lane, jnp.sum(grad_mid * mid, axis=-1, keepdims=True), 0.0)
+    gg_ref[...] = gg_in[...] + column if chained else column
+    act = (on * mid).astype(BF)
+    grad_mid = on * grad_mid
+    ggp = (grad_mid * up_pre * (sig * (1.0 + gate_pre * (1.0 - sig)))).astype(BF)
+    gup = (grad_mid * silu).astype(BF)
+    mid_ref[0, 0] = act
+    mid_ref[0, 1] = ggp
+    mid_ref[0, 2] = gup
+    if not acc:
+        own_ref[0] = tn(h, ggp).astype(BF)
+        own_ref[1] = tn(h, gup).astype(BF)
+        own_ref[2] = tn(g, act).astype(BF)
+        return
+    acc = acc[0]
+
+    @pl.when(step == 0)
+    def _():
+        acc[...] = jnp.zeros_like(acc)
+
+    acc[0] += tn(h, ggp)
+    acc[1] += tn(h, gup)
+    acc[2] += tn(g, act)
+
+    @pl.when(step == steps - 1)
+    def _():
+        own_ref[...] = acc[...].astype(BF)
+
+
+def expert_grads(j, per_core, which, column, h, g, on, w_gate, w_up, w_down, before):
+    rows, width = h.shape
+    hidden = w_gate.shape[2]
+    experts = on.shape[1]
+    tile = rows if rows <= 896 else 448
+    steps = rows // tile
+
+    def row(i, w):
+        return (i, 0)
+
+    def weight(i, w):
+        return (w[0], 0, 0)
+
+    chained = before is not None
+    return pl.pallas_call(
+        functools.partial(expert_grads_kernel, chained),
+        grid_spec=pltpu.PrefetchScalarGridSpec(
+            num_scalar_prefetch=1,
+            grid=(steps,),
+            in_specs=[
+                pl.BlockSpec((tile, width), row),
+                pl.BlockSpec((tile, width), row),
+                pl.BlockSpec((tile, experts), row),
+                pl.BlockSpec((1, width, hidden), weight),
+                pl.BlockSpec((1, width, hidden), weight),
+                pl.BlockSpec((1, hidden, width), weight),
+            ]
+            + [pl.BlockSpec((tile, experts), row), pl.BlockSpec(memory_space=pl.ANY)] * chained,
+            out_specs=[
+                pl.BlockSpec((1, 3, tile, hidden), lambda i, w: (j, 0, i, 0)),
+                pl.BlockSpec((tile, experts), row),
+                pl.BlockSpec((3, width, hidden), lambda i, w: (0, 0, 0)),
+            ],
+            scratch_shapes=[pltpu.VMEM((3, width, hidden), F32)] * (steps > 1),
+        ),
+        out_shape=[
+            jax.ShapeDtypeStruct((per_core, 3, rows, hidden), BF),
+            jax.ShapeDtypeStruct((rows, experts), F32),
+            jax.ShapeDtypeStruct((3, width, hidden), BF),
+        ],
+        input_output_aliases={8: 0} if chained else {},
+        compiler_params=pltpu.CompilerParams(vmem_limit_bytes=VMEM_LIMIT),
+        cost_estimate=pl.CostEstimate(
+            flops=20 * rows * width * hidden,
+            bytes_accessed=20 << 20,
+            transcendentals=rows * hidden,
+        ),
+    )(
+        jnp.stack([which, column]).astype(jnp.int32),
+        h, g, on, w_gate, w_up, w_down, *((before[1], before[0]) if chained else ()),
+    )
+
+
+def expert_sums_kernel(first, mid_ref, wg_ref, wu_ref, wd_ref, mix_ref, gh_ref, mix_acc, gh_acc):
+    e, count = pl.program_id(1), pl.num_programs(1)
+    mix = nn(mid_ref[0, 0], wd_ref[0])
+    gh = nt(mid_ref[0, 1], wg_ref[0]) + nt(mid_ref[0, 2], wu_ref[0])
+
+    @pl.when(e == 0)
+    def _():
+        mix_acc[...] = mix
+        gh_acc[...] = gh
+
+    @pl.when(e > 0)
+    def _():
+        mix_acc[...] += mix
+        gh_acc[...] += gh
+
+    @pl.when(e == count - 1)
+    def _():
+        mix_ref[...] = mix_acc[...].astype(BF)
+        gh_ref[...] = gh_acc[...].astype(BF)
+
+
+def expert_sums(first, mid, tree, w_gate, w_up, w_down):
+    count, _, rows, hidden = mid.shape
+    width = w_gate.shape[1]
+    rows //= 2
+    tile = 448
+    tiles = rows // tile
+
+    def weight(i, e, f):
+        return (f[0] + e, 0, 0)
+
+    out = pl.BlockSpec((tile, width), lambda i, e, f: (i, 0))
+    return pl.pallas_call(
+        expert_sums_kernel,
+        grid_spec=pltpu.PrefetchScalarGridSpec(
+            num_scalar_prefetch=1,
+            grid=(tiles, count),
+            in_specs=[
+                pl.BlockSpec((1, 3, tile, hidden), lambda i, e, f: (e, 0, tree * tiles + i, 0)),
+                pl.BlockSpec((1, width, hidden), weight),
+                pl.BlockSpec((1, width, hidden), weight),
+                pl.BlockSpec((1, hidden, width), weight),
+            ],
+            out_specs=[out, out],
+            scratch_shapes=[pltpu.VMEM((tile, width), F32), pltpu.VMEM((tile, width), F32)],
+        ),
+        out_shape=[jax.ShapeDtypeStruct((rows, width), BF)] * 2,
+        compiler_params=pltpu.CompilerParams(vmem_limit_bytes=VMEM_LIMIT),
+        cost_estimate=pl.CostEstimate(
+            flops=10 * count * rows * width * hidden,
+            bytes_accessed=30 << 20,
+            transcendentals=0,
+        ),
+    )(jnp.reshape(first, (1,)).astype(jnp.int32), mid, w_gate, w_up, w_down)
 
 
 def local(
@@ -214,9 +533,20 @@
     per_key = q_heads // kv_heads
     experts = w_gate.shape[0] * me.groups
     per_core = w_gate.shape[0] // 2
-    hidden = w_gate.shape[2]
-    scale = HEAD_DIM ** (-0.5)
     q_width, k_width = q_heads * HEAD_DIM, kv_heads * HEAD_DIM
+    q_lanes, k_lanes = pairs(q_heads) * LANES, pairs(kv_heads) * LANES
+    lanes = q_lanes + 2 * k_lanes
+
+    blocks = []
+    for j in range(me.groups):
+        for weight, size, room in (
+            (w_query, q_width, q_lanes),
+            (key_weight, k_width, k_lanes),
+            (value_weight, k_width, k_lanes),
+        ):
+            block = weight[:, j * size : (j + 1) * size]
+            blocks.append(jnp.pad(block, ((0, 0), (0, room - size))))
+    weights = jnp.concatenate(blocks, 1)
 
     own_rows = tokens.astype(F32)
     inv_rows = lax.rsqrt(jnp.mean(own_rows * own_rows, axis=-1, keepdims=True) + EPS)
@@ -225,9 +555,13 @@
     normed_one = inputs * inv_one
     gain_one = norm_gain.astype(F32)
     hidden_first = (normed_one * gain_one).astype(BF)
-    raw_q = me.scatter(nn(hidden_first, w_query), 1)
-    raw_k = me.scatter(nn(hidden_first, key_weight), 1)
-    value_low = me.scatter(nn(hidden_first, value_weight), 1).astype(BF)
+    if me.groups == 2:
+        theirs = nn(hidden_first, me.part(weights, 1, 1 - me.member)).astype(BF)
+        came = me.swap_shard(theirs)
+        own = nn(hidden_first, me.part(weights, 1, me.member))
+    else:
+        own = me.scatter(nn(hidden_first, weights), 1)
+        came = jnp.zeros(own.shape, BF)
 
     route_hot = jnp.any(
         routes[:, :, None] == jnp.arange(experts, dtype=jnp.int32)[None, None, :], axis=1
@@ -242,37 +576,11 @@
 
     index = jnp.arange(tree_len, dtype=jnp.int32)
     _, depth = tree_layout(index, seg_len)
-    tables = angle_tables(depth, HEAD_DIM // 2)
+    cos, sin = angle_tables(depth)
     visible = tree_mask(index, index, parents[0], seg_len)
-
-    def heads(v):
-        return v.reshape(tree_len, -1, HEAD_DIM)
-
-    query_rot = rotate(heads(raw_q), tables, 1.0).astype(BF)
-    key_rot = rotate(heads(raw_k), tables, 1.0).astype(BF)
-    query_h = query_rot.reshape(tree_len, kv_heads, per_key, HEAD_DIM).transpose(1, 2, 0, 3)
-    key_h = key_rot.transpose(1, 0, 2)
-    value_h = heads(value_low).transpose(1, 0, 2)
-
-    def scores_of(q, k):
-        s = jnp.einsum("gqd,kd->gqk", q, k, preferred_element_type=F32) * scale
-        return jnp.where(visible[None], s, -1e30)
-
-    def head_forward(operands):
-        q, k, v = operands
-        s = scores_of(q, k)
-        peak = jnp.max(s, axis=-1, keepdims=True)
-        e = jnp.exp(s - peak)
-        total = jnp.sum(e, axis=-1, keepdims=True)
-        probs = (e / total).astype(BF)
-        return (
-            jnp.einsum("gqk,kd->gqd", probs, v, preferred_element_type=F32),
-            peak + jnp.log(total),
-        )
-
-    attended_h, log_total = lax.map(head_forward, (query_h, key_h, value_h))
-    attended = attended_h.transpose(2, 0, 1, 3).reshape(tree_len, q_width).astype(BF)
-    attended_full = me.gather(attended, 1)
+    bias = jnp.where(visible, 0.0, -1e30).astype(F32)
+    attended, lse, query, key, value = attend(own, came, cos, sin, bias, q_heads, kv_heads)
+    attended_full = me.gather(attended[:, :q_width], 1)
     middle = inputs + nn(attended_full, w_out)
     squares = me.total(jnp.sum(middle * middle, axis=-1, keepdims=True))
     inv_two = lax.rsqrt(squares / width + EPS)
@@ -291,60 +599,32 @@
     gates_all = gates_of(hidden_all, jnp.concatenate([routed, routed_other], 0))
     gates = gates_all[:tree_len]
 
-    mixed = jnp.zeros((2 * tree_len, width), F32)
-    grad_hidden = jnp.zeros((2 * tree_len, width), F32)
-    grad_gate_columns = []
+    first = me.core * per_core
+    before = None
     sums = []
+    chunk = width // me.chips
     for j in range(per_core):
-        which = me.core * per_core + j
-        gate_w = lax.dynamic_index_in_dim(w_gate, which, 0, keepdims=False)
-        up_w = lax.dynamic_index_in_dim(w_up, which, 0, keepdims=False)
-        down_w = lax.dynamic_index_in_dim(w_down, which, 0, keepdims=False)
-        gate = lax.dynamic_slice_in_dim(
-            gates_all, me.member * (2 * per_core) + which, 1, 1
+        mid, own_columns, grads = expert_grads(
+            j, per_core, first + j, me.member * (2 * per_core) + first + j,
+            hidden_all, grad_all, gates_all, w_gate, w_up, w_down, before,
         )
-        gate_pre = nn(hidden_all, gate_w)
-        up_pre = nn(hidden_all, up_w)
-        grad_mid = nt(grad_all, down_w)
-        sig = jax.nn.sigmoid(gate_pre)
-        silu = gate_pre * sig
-        mid = silu * up_pre
-        grad_gate_columns.append(jnp.sum(grad_mid * mid, axis=-1, keepdims=True))
-        act = (gate * mid).astype(BF)
-        mixed = mixed + nn(act, down_w)
-        grad_mid = gate * grad_mid
-        grad_gate_pre = (grad_mid * up_pre * sig * (1.0 + gate_pre * (1.0 - sig))).astype(BF)
-        grad_up_pre = (grad_mid * silu).astype(BF)
-        grad_hidden = grad_hidden + nt(grad_gate_pre, gate_w) + nt(grad_up_pre, up_w)
-        own = jnp.stack(
-            [
-                tn(hidden_all, grad_gate_pre).astype(BF),
-                tn(hidden_all, grad_up_pre).astype(BF),
-                tn(grad_all, act).astype(BF),
-            ]
-        )
-        chunk = width // me.chips
+        before = (mid, own_columns)
         sums.append(
             me.ring_scatter(
-                lambda chip, own=own: lax.dynamic_slice_in_dim(own, chip * chunk, chunk, 1)
+                lambda chip, grads=grads: lax.dynamic_slice_in_dim(grads, chip * chunk, chunk, 1)
             )
         )
-
-    def over_cores(v):
-        return v[:tree_len] + me.swap_core(v[tree_len:].astype(BF)).astype(F32)
-
-    mixed = over_cores(mixed)
-    grad_hidden = over_cores(grad_hidden)
+    mixed_other, grad_other = expert_sums(first, mid, 1, w_gate, w_up, w_down)
+    mixed_own, grad_own = expert_sums(first, mid, 0, w_gate, w_up, w_down)
+
+    grad_hidden = grad_own.astype(F32) + me.swap_core(grad_other).astype(F32)
+    mixed = mixed_own.astype(F32) + me.swap_core(mixed_other).astype(F32)
     placed = lax.dynamic_update_slice_in_dim(
         jnp.zeros((tree_len, width), F32), middle, me.member * columns, 1
     )
     result = me.scatter(mixed + placed, 0).astype(BF)
 
-    own_columns = jnp.concatenate(grad_gate_columns, 1)
-    both = me.in_order(
-        me.core, own_columns[:tree_len], me.swap_core(own_columns[tree_len:]), 1
-    )
-    grad_gates = me.gather(both, 1)
+    grad_gates = me.total(own_columns[:tree_len] + me.swap_core(own_columns[tree_len:]))
     grad_logits = (
         gates * (grad_gates - jnp.sum(gates * grad_gates, axis=-1, keepdims=True))
     ).astype(BF)
@@ -353,41 +633,32 @@
     grad_gain_two = jnp.sum(grad_hidden_two * normed_two, axis=0)
     scaled = grad_hidden_two * gain_two
     mean = me.total(jnp.sum(scaled * normed_two, axis=-1, keepdims=True)) / width
-    grad_own = me.part(grad_tree, 1, me.member).astype(F32)
-    grad_middle = grad_own + inv_two * (scaled - normed_two * mean)
+    grad_columns = me.part(grad_tree, 1, me.member).astype(F32)
+    grad_middle = grad_columns + inv_two * (scaled - normed_two * mean)
     grad_branch = grad_middle.astype(BF)
     grad_out = me.all_reduce(tn(attended_full, grad_branch))
-    grad_attended = me.scatter(nt(grad_branch, w_out), 1).astype(BF)
-
-    grad_h = grad_attended.reshape(tree_len, kv_heads, per_key, HEAD_DIM).transpose(1, 2, 0, 3)
-
-    def head_backward(operands):
-        q, k, v, g, log_one = operands
-        probs = jnp.exp(scores_of(q, k) - log_one)
-        probs_low = probs.astype(BF)
-        grad_probs = jnp.einsum("gqd,kd->gqk", g, v, preferred_element_type=F32)
-        grad_v = jnp.einsum("gqk,gqd->kd", probs_low, g, preferred_element_type=F32)
-        delta = jnp.sum(probs * grad_probs, axis=-1, keepdims=True)
-        grad_s = (probs * (grad_probs - delta) * scale).astype(BF)
-        grad_q = jnp.einsum("gqk,kd->gqd", grad_s, k, preferred_element_type=F32)
-        grad_k = jnp.einsum("gqk,gqd->kd", grad_s, q, preferred_element_type=F32)
-        return (grad_q, grad_k, grad_v)
-
-    grad_q, grad_k, grad_v = lax.map(head_backward, (query_h, key_h, value_h, grad_h, log_total))
-    grad_q = grad_q.transpose(2, 0, 1, 3).reshape(tree_len, q_heads, HEAD_DIM)
-    grad_q = rotate(grad_q, tables, -1.0).reshape(tree_len, q_width).astype(BF)
-    grad_k = rotate(grad_k.transpose(1, 0, 2), tables, -1.0)
-    grad_k = grad_k.reshape(tree_len, k_width).astype(BF)
-    grad_v = grad_v.transpose(1, 0, 2).reshape(tree_len, k_width).astype(BF)
-    grad_q_full = me.gather(grad_q, 1)
-    grad_k_full = me.gather(grad_k, 1)
-    grad_v_full = me.gather(grad_v, 1)
-    grad_query = me.all_reduce(tn(hidden_first, grad_q_full))
-    grad_key = me.all_reduce(tn(hidden_first, grad_k_full))
-    grad_value = me.all_reduce(tn(hidden_first, grad_v_full))
-    grad_hidden_one = (
-        nt(grad_q_full, w_query) + nt(grad_k_full, key_weight) + nt(grad_v_full, value_weight)
-    )
+    grad_attended = nt(grad_branch, w_out)
+    if me.groups == 2:
+        own = me.part(grad_attended, 1, me.member)
+        came = me.swap_shard(me.part(grad_attended, 1, 1 - me.member).astype(BF))
+    else:
+        own = me.scatter(grad_attended, 1)
+        own = jnp.pad(own, ((0, 0), (0, q_lanes - q_width)))
+        came = jnp.zeros(own.shape, BF)
+    grad_heads = attend_back(
+        own, came, query, key, value, lse, cos, sin, bias.T, q_heads, kv_heads
+    )
+    grad_full = me.gather(grad_heads, 1)
+    grad_weights = me.all_reduce(tn(hidden_first, grad_full))
+    grad_weights = grad_weights.reshape(columns, me.groups, lanes)
+
+    def picked(start, size):
+        return grad_weights[:, :, start : start + size].reshape(columns, me.groups * size)
+
+    grad_query = picked(0, q_width)
+    grad_key = picked(q_lanes, k_width)
+    grad_value = picked(q_lanes + k_lanes, k_width)
+    grad_hidden_one = nt(grad_full, weights)
     grad_gain_one = jnp.sum(grad_hidden_one * normed_one, axis=0)
     scaled = grad_hidden_one * gain_one
     mean = me.total(jnp.sum(scaled * normed_one, axis=-1, keepdims=True)) / width

time: 822 us -> 608 us (0.74)
  matrix products: 308 us -> 23.3 us
  Pallas kernels: 0 us -> 127 us
  starting transfers between devices: 143 us -> 93.4 us
  waiting for transfers between devices: 256 us -> 223 us
  local copies, waits for them, and re-layouts: 31.4 us -> 45.7 us
  other arithmetic: 71.7 us -> 84.6 us
    dot_general x51 -> x10, matrix products: 209 us -> 23.3 us  [dot(): return lax.dot_general(a, b, (dims, ((), ())), preferred_element_type=F32)]
    pallas_call x0 -> x8, Pallas kernels: none -> 127 us  [the longest x4 68.3 us: expert_grads(): pl.pallas_call(functools.partial(expert_grads_kernel, chained), grid_spec...]
    dot_general x28 -> x0, matrix products: 99.2 us -> none  [the longest x4 23.5 us: head_backward(): grad_q = jnp.einsum('gqk,kd->gqd', grad_s, k, preferred_element_type=F32)]
    ppermute x84 -> x56, starting transfers between devices: 116 us -> 71.1 us  [along_ring(): return lax.ppermute(v, 'rep', self.ring)]
    ppermute x84 -> x56, waiting for transfers between devices: 173 us -> 130 us  [along_ring(): return lax.ppermute(v, 'rep', self.ring)]
    convert_element_type x4 -> x2, other arithmetic: 8.33 us -> 21.3 us  [all_reduce(): return self.in_order(self.core, whole, self.swap_core(whole), 0).astype(F32)]
    concatenate x0 -> x4, local copies, waits for them, and re-layouts: none -> 11.4 us  [the longest x2 10.4 us: in_order(): jnp.concatenate([mine, other], axis)]
    concatenate x3 -> x4, other arithmetic: 0.15 us -> 8.86 us  [the longest x1 3.5 us: local(): hidden_all = jnp.concatenate([hidden_tree, me.swap_core(hidden_tree)], 0)]
  transfers between devices with their start and end apart: 124 -> 88, of which waited for: 75 -> 50; matrix products, arithmetic and copies ran while one was open for 40% -> 17% of each run, Pallas kernels for 0% -> 2%
where the time goes in v2:
time: 608 us; the launch traced here: 598 us
  waiting for transfers between devices  223 us (37%)
  Pallas kernels  127 us (21%)
  starting transfers between devices  93.4 us (15%)
  other arithmetic  84.6 us (14%)
  local copies, waits for them, and re-layouts  45.7 us (8%)
  matrix products  23.3 us (4%)
    ppermute x56, waiting for transfers between devices, along_ring(): return lax.ppermute(v, 'rep', self.ring)  130 us
    ppermute x17, waiting for transfers between devices, swap_shard(): return lax.ppermute(v, 'shard', [(0, 1), (1, 0)])  80.2 us
    ppermute x56, starting transfers between devices, along_ring(): return lax.ppermute(v, 'rep', self.ring)  71.1 us
    pallas_call x4, Pallas kernels, expert_grads(): pl.pallas_call(functools.partial(expert_grads_kernel, chained), grid_spec...  68.3 us
    pallas_call x2, Pallas kernels, expert_sums(): pl.pallas_call(expert_sums_kernel, grid_spec=pltpu.PrefetchScalarGridSpec...  31.9 us
    convert_element_type x36, other arithmetic, ring_scatter(): held = (came.astype(F32) + mine.astype(F32)).astype(BF)  29.7 us
    dot_general x10, matrix products, dot(): return lax.dot_general(a, b, (dims, ((), ())), preferred_element_type=F32)  23.3 us
    convert_element_type x2, other arithmetic, all_reduce(): return self.in_order(self.core, whole, self.swap_core(whole), 0).astype(F32)  21.3 us
  transfers between devices with their start and end apart: 88, of which 50 were waited for; matrix products, arithmetic and copies ran while one was open for 17% of the time, Pallas kernels for 2%

profile of v2, /device:TPU:0, one launch (start us, length us, event | category | flops | bytes accessed | tf_op | source)
XLA Modules:
  0.0 598.1 jit_solution(11419508983980003497)
XLA Ops:
  27.2 16.7 %collective-permute-done.2.came_ref = bf16[448,1280]{1,0:T(8,128)(2,1)} collective-permute-done((bf16[448,1280]{1,0:T(8,128)(2,1)S(1)}, bf16[448,1280]{1,0:T(8,128)(2,1)}, u32[]{:S(2)}, u32[]{:S(2)}) %collective-permute-start.2) | collective-permute-done | bytes 1146912 | tf_op jit(solution)/shard_map/ppermute | solution.py:102
  43.9 12.4 %shard_map.229 = (bf16[448,768]{1,0:T(8,128)(2,1)}, f32[448,128]{1,0:T(8,128)}, bf16[448,768]{1,0:T(8,128)(2,1)}, bf16[4,2,448,128]{3,2,1,0:T(8,128)(2,1)}, bf16[4,2,448,128]{3,2,1,0:T(8,128)(2,1)}) custom-call(f32[448,1280]{1,0:T(8,128)} %fusion.4.own_ref, bf16[448,1280]{1,0:T(8,128)(2,1)} %collective-permute-done.2.came_ref, ...), custom_call_target="tpu_custom_call" | custom-call | flops 2890137600 | bytes 8388608 | tf_op jit(solution)/shard_map/pallas_call | solution.py:260
  57.7 14.5 %collective-permute-done.3 = bf16[448,768]{1,0:T(8,128)(2,1)S(1)} collective-permute-done((bf16[448,768]{1,0:T(8,128)(2,1)}, bf16[448,768]{1,0:T(8,128)(2,1)S(1)}, u32[]{:S(2)}, u32[]{:S(2)}) %collective-permute-start.3) | collective-permute-done | bytes 688160 | tf_op jit(solution)/shard_map/ppermute | solution.py:102
  80.7 14.4 %collective-permute-done.7 = bf16[224,1536]{1,0:T(8,128)(2,1)S(1)} collective-permute-done((bf16[224,1536]{1,0:T(8,128)(2,1)S(1)}, bf16[224,1536]{1,0:T(8,128)(2,1)S(1)}, u32[]{:S(2)}, u32[]{:S(2)}) %collective-permute-start.7) | collective-permute-done | bytes 688160 | tf_op jit(solution)/shard_map/ppermute | solution.py:102
  96.7 9.0 %collective-permute-done.5 = bf16[448,768]{1,0:T(8,128)(2,1)S(1)} collective-permute-done((bf16[448,768]{1,0:T(8,128)(2,1)S(1)}, bf16[448,768]{1,0:T(8,128)(2,1)S(1)}, u32[]{:S(2)}, u32[]{:S(2)}) %collective-permute-start.5) | collective-permute-done | bytes 688160 | tf_op jit(solution)/shard_map/ppermute | solution.py:102
  126.0 17.0 %shard_map.230 = (bf16[4,3,896,512]{3,2,1,0:T(8,128)(2,1)}, f32[896,16]{1,0:T(8,128)}, bf16[3,1536,512]{2,1,0:T(8,128)(2,1)}) custom-call(s32[2]{0:T(128)} %get-tuple-element.97.where, bf16[896,1536]{1,0:T(8,128)(2,1)} %pad_maximum_fusion.h_ref, bf16[896,1536]{1,0:T(8,128)(2,1)} %pad_maximum_fusion.1.g_ref, f32[896,16]{1,0:T(8,128)} %broadcast_divide_fusion.on_ref, ...), custom_call_target="tpu_custom_call" | custom-call | flops 14092861440 | bytes 20971520 | tf_op jit(solution)/shard_map/pallas_call | solution.py:415
  143.1 16.9 %shard_map.231 = (bf16[4,3,896,512]{3,2,1,0:T(8,128)(2,1)}, f32[896,16]{1,0:T(8,128)}, bf16[3,1536,512]{2,1,0:T(8,128)(2,1)}) custom-call(s32[2]{0:T(128)} %get-tuple-element.96.where, bf16[896,1536]{1,0:T(8,128)(2,1)} %pad_maximum_fusion.h_ref, bf16[896,1536]{1,0:T(8,128)(2,1)} %pad_maximum_fusion.1.g_ref, ...), custom_call_target="tpu_custom_call", output_to_operand_aliasing={{0}: (8, {})} | custom-call | flops 14092861440 | bytes 20971520 | tf_op jit(solution)/shard_map/pallas_call | solution.py:415
  160.0 17.3 %shard_map.232 = (bf16[4,3,896,512]{3,2,1,0:T(8,128)(2,1)}, f32[896,16]{1,0:T(8,128)}, bf16[3,1536,512]{2,1,0:T(8,128)(2,1)}) custom-call(s32[2]{0:T(128)} %get-tuple-element.95.where, bf16[896,1536]{1,0:T(8,128)(2,1)} %pad_maximum_fusion.h_ref, bf16[896,1536]{1,0:T(8,128)(2,1)} %pad_maximum_fusion.1.g_ref, ...), custom_call_target="tpu_custom_call", output_to_operand_aliasing={{0}: (8, {})} | custom-call | flops 14092861440 | bytes 20971520 | tf_op jit(solution)/shard_map/pallas_call | solution.py:415
  177.3 17.0 %shard_map.233 = (bf16[4,3,896,512]{3,2,1,0:T(8,128)(2,1)}, f32[896,16]{1,0:T(8,128)}, bf16[3,1536,512]{2,1,0:T(8,128)(2,1)}) custom-call(s32[2]{0:T(128)} %get-tuple-element.94.where, bf16[896,1536]{1,0:T(8,128)(2,1)} %pad_maximum_fusion.h_ref, bf16[896,1536]{1,0:T(8,128)(2,1)} %pad_maximum_fusion.1.g_ref, ...), custom_call_target="tpu_custom_call", output_to_operand_aliasing={{0}: (8, {})} | custom-call | flops 14092861440 | bytes 20971520 | tf_op jit(solution)/shard_map/pallas_call | solution.py:415
  194.3 15.9 %shard_map.235 = (bf16[448,1536]{1,0:T(8,128)(2,1)}, bf16[448,1536]{1,0:T(8,128)(2,1)}) custom-call(s32[1]{0:T(128)} %bitcast.first, bf16[4,3,896,512]{3,2,1,0:T(8,128)(2,1)} %get-tuple-element.40.mid_ref, bf16[8,1536,512]{2,1,0:T(8,128)(2,1)} %wg_ref.11, bf16[8,1536,512]{2,1,0:T(8,128)(2,1)} %wu_ref.11, bf16[8,512,1536]{2,1,0:T(8,128)(2,1)} %wd_ref.11), custom_call_target="tpu_custom_call" | custom-call | flops 14092861440 | bytes 31457280 | tf_op jit(solution)/shard_map/pallas_call | solution.py:486
  210.3 16.0 %shard_map.234 = (bf16[448,1536]{1,0:T(8,128)(2,1)}, bf16[448,1536]{1,0:T(8,128)(2,1)}) custom-call(s32[1]{0:T(128)} %bitcast.first, bf16[4,3,896,512]{3,2,1,0:T(8,128)(2,1)} %get-tuple-element.40.mid_ref, bf16[8,1536,512]{2,1,0:T(8,128)(2,1)} %wg_ref.11, bf16[8,1536,512]{2,1,0:T(8,128)(2,1)} %wu_ref.11, bf16[8,512,1536]{2,1,0:T(8,128)(2,1)} %wd_ref.11), custom_call_target="tpu_custom_call" | custom-call | flops 14092861440 | bytes 31457280 | tf_op jit(solution)/shard_map/pallas_call | solution.py:486
  258.1 4.5 collective-permute-done.60
  334.8 13.7 %collective-permute-done.13 = bf16[224,1536]{1,0:T(8,128)(2,1)S(1)} collective-permute-done((bf16[224,1536]{1,0:T(8,128)(2,1)S(1)}, bf16[224,1536]{1,0:T(8,128)(2,1)S(1)}, u32[]{:S(2)}, u32[]{:S(2)}) %collective-permute-start.13) | collective-permute-done | bytes 688160 | tf_op jit(solution)/shard_map/ppermute | solution.py:102
  353.9 14.1 %shard_map.236 = bf16[448,1280]{1,0:T(8,128)(2,1)} custom-call(f32[448,768]{1,0:T(8,128)} %constant_dynamic-slice_fusion.12.own_ref, bf16[448,768]{1,0:T(8,128)(2,1)} %copy-done.32, bf16[448,768]{1,0:T(8,128)(2,1)} %get-tuple-element.46.q_ref, bf16[4,2,448,128]{3,2,1,0:T(8,128)(2,1)} %get-tuple-element.47.k_ref, ...), custom_call_target="tpu_custom_call" | custom-call | flops 3853516800 | bytes 8388608 | tf_op jit(solution)/shard_map/pallas_call | solution.py:344
  379.0 15.1 %collective-permute-done.44 = bf16[96,768]{1,0:T(8,128)(2,1)S(1)} collective-permute-done((bf16[96,768]{1,0:T(8,128)(2,1)S(1)}, bf16[96,768]{1,0:T(8,128)(2,1)S(1)}, u32[]{:S(2)}, u32[]{:S(2)}) %collective-permute-start.44) | collective-permute-done | bytes 147488 | tf_op jit(solution)/shard_map/ppermute | solution.py:108
  400.9 4.7 collective-permute-done.45
  411.1 8.7 %collective-permute-done.46 = bf16[96,768]{1,0:T(8,128)(2,1)S(1)} collective-permute-done((bf16[96,768]{1,0:T(8,128)(2,1)S(1)}, bf16[96,768]{1,0:T(8,128)(2,1)S(1)}, u32[]{:S(2)}, u32[]{:S(2)}) %collective-permute-start.46) | collective-permute-done | bytes 147488 | tf_op jit(solution)/shard_map/ppermute | solution.py:108
  445.7 9.5 %collective-permute-done.26 = f32[18,768]{1,0:T(8,128)S(1)} collective-permute-done((f32[18,768]{1,0:T(8,128)S(1)}, f32[18,768]{1,0:T(8,128)S(1)}, u32[]{:S(2)}, u32[]{:S(2)}) %collective-permute-start.26) | collective-permute-done | bytes 55328 | tf_op jit(solution)/shard_map/ppermute | solution.py:187
  462.1 7.7 %collective-permute-done.30 = bf16[48,2560]{1,0:T(8,128)(2,1)S(1)} collective-permute-done((bf16[48,2560]{1,0:T(8,128)(2,1)S(1)}, bf16[48,2560]{1,0:T(8,128)(2,1)S(1)}, u32[]{:S(2)}, u32[]{:S(2)}) %collective-permute-start.30) | collective-permute-done | bytes 245792 | tf_op jit(solution)/shard_map/ppermute | solution.py:108
  492.9 5.3 collective-permute-done.53
  503.8 4.7 collective-permute-done.55
  561.2 5.2 concatenate.137
  566.4 5.2 concatenate.138
  571.6 18.6 %fusion = f32[768,2,1280]{2,1,0:T(2,128)S(1)} fusion(pred[]{:T(512)S(6)} %eq.210, bf16[384,2,1280]{2,1,0:T(2,128)(2,1)} %concatenate.138, bf16[384,2,1280]{2,1,0:T(2,128)(2,1)} %concatenate.137), kind=kLoop, calls=%fused_computation.2 | loop fusion | flops 7864320 | bytes 11796481 | tf_op jit(solution)/shard_map/convert_element_type | solution.py:182
  (379 shorter events, 312.1 us)
Async XLA Ops:
  17.2 26.6 %collective-permute-start.2 = (bf16[448,1280]{1,0:T(8,128)(2,1)S(1)}, bf16[448,1280]{1,0:T(8,128)(2,1)}, u32[]{:S(2)}, u32[]{:S(2)}) collective-permute-start(bf16[448,1280]{1,0:T(8,128)(2,1)S(1)} %convolution_convert_fusion.2), channel_id=1, source_target_pairs={{0,1},{1,0},{2,3},{3,2},{4,5},{5,4},{6,7},{7,6},{8,9},{9,8},{10,11... | collective-permute-start | bytes 3440648 | tf_op jit(solution)/shard_map/ppermute | solution.py:102
  79.5 26.2 %collective-permute-start.5 = (bf16[448,768]{1,0:T(8,128)(2,1)S(1)}, bf16[448,768]{1,0:T(8,128)(2,1)S(1)}, u32[]{:S(2)}, u32[]{:S(2)}) collective-permute-start(bf16[448,768]{1,0:T(8,128)(2,1)S(1)} %multiply_convert_fusion), channel_id=1, source_target_pairs={{0,1},{1,0},{2,3},{3,2},{4,5},{5,4},{6,7},{7,6},{8,9},{9,8},{10,11... | collective-permute-start | bytes 2064392 | tf_op jit(solution)/shard_map/ppermute | solution.py:102
  241.6 43.9 %collective-permute-start.12 = (bf16[448,1536]{1,0:T(8,128)(2,1)S(1)}, bf16[448,1536]{1,0:T(8,128)(2,1)S(1)}, u32[]{:S(2)}, u32[]{:S(2)}) collective-permute-start(bf16[448,1536]{1,0:T(8,128)(2,1)S(1)} %copy-done.26), channel_id=1, source_target_pairs={{0,2},{2,0},{4,6},{6,4},{8,10},{10,8},{12,14},{14,12},{16,18},{18,... | collective-permute-start | bytes 4128776 | tf_op jit(solution)/shard_map/ppermute | solution.py:105
  242.2 41.2 %collective-permute-start.16 = (bf16[448,1536]{1,0:T(8,128)(2,1)S(1)}, bf16[448,1536]{1,0:T(8,128)(2,1)S(1)}, u32[]{:S(2)}, u32[]{:S(2)}) collective-permute-start(bf16[448,1536]{1,0:T(8,128)(2,1)S(1)} %copy-done.27), channel_id=1, source_target_pairs={{0,2},{2,0},{4,6},{6,4},{8,10},{10,8},{12,14},{14,12},{16,18},{18,... | collective-permute-start | bytes 4128776 | tf_op jit(solution)/shard_map/ppermute | solution.py:105
  289.1 26.7 %collective-permute-start.62 = (bf16[3,192,512]{2,1,0:T(8,128)(2,1)S(1)}, bf16[3,192,512]{2,1,0:T(8,128)(2,1)S(1)}, u32[]{:S(2)}, u32[]{:S(2)}) collective-permute-start(bf16[3,192,512]{2,1,0:T(8,128)(2,1)S(1)} %add_convert_fusion.28), channel_id=1, source_target_pairs={{0,8},{2,6},{8,16},{10,2},{16,24},{18,10},{24,28},{26,18},{28,20},... | collective-permute-start | bytes 1769480 | tf_op jit(solution)/shard_map/ppermute | solution.py:108
  307.0 25.1 %collective-permute-start.83 = (bf16[3,192,512]{2,1,0:T(8,128)(2,1)S(1)}, bf16[3,192,512]{2,1,0:T(8,128)(2,1)S(1)}, u32[]{:S(2)}, u32[]{:S(2)}) collective-permute-start(bf16[3,192,512]{2,1,0:T(8,128)(2,1)S(1)} %add_convert_fusion.7), channel_id=1, source_target_pairs={{0,8},{2,6},{8,16},{10,2},{16,24},{18,10},{24,28},{26,18},{28,20},... | collective-permute-start | bytes 1769480 | tf_op jit(solution)/shard_map/ppermute | solution.py:108
  314.5 60.5 %collective-permute-start.43 = (bf16[768,768]{1,0:T(8,128)(2,1)}, bf16[768,768]{1,0:T(8,128)(2,1)}, u32[]{:S(2)}, u32[]{:S(2)}) collective-permute-start(bf16[768,768]{1,0:T(8,128)(2,1)} %constant_dynamic-slice_fusion.7), channel_id=1, source_target_pairs={{0,2},{2,0},{4,6},{6,4},{8,10},{10,8},{12,14},{14,12},{16,18},{18,... | collective-permute-start | bytes 3538952 | tf_op jit(solution)/shard_map/ppermute | solution.py:105
  315.8 35.2 %collective-permute-start.19 = (bf16[448,768]{1,0:T(8,128)(2,1)S(1)}, bf16[448,768]{1,0:T(8,128)(2,1)S(1)}, u32[]{:S(2)}, u32[]{:S(2)}) collective-permute-start(bf16[448,768]{1,0:T(8,128)(2,1)S(1)} %dynamic-slice_convert_fusion), channel_id=1, source_target_pairs={{0,1},{1,0},{2,3},{3,2},{4,5},{5,4},{6,7},{7,6},{8,9},{9,8},{10,11... | collective-permute-start | bytes 2064392 | tf_op jit(solution)/shard_map/ppermute | solution.py:102
  319.5 29.0 %collective-permute-start.13 = (bf16[224,1536]{1,0:T(8,128)(2,1)S(1)}, bf16[224,1536]{1,0:T(8,128)(2,1)S(1)}, u32[]{:S(2)}, u32[]{:S(2)}) collective-permute-start(bf16[224,1536]{1,0:T(8,128)(2,1)S(1)} %dynamic-slice_convert_fusion.2), channel_id=1, source_target_pairs={{0,1},{1,0},{2,3},{3,2},{4,5},{5,4},{6,7},{7,6},{8,9},{9,8},{10,11... | collective-permute-start | bytes 2064392 | tf_op jit(solution)/shard_map/ppermute | solution.py:102
  325.8 42.2 %collective-permute-start.63 = (bf16[3,192,512]{2,1,0:T(8,128)(2,1)}, bf16[3,192,512]{2,1,0:T(8,128)(2,1)}, u32[]{:S(2)}, u32[]{:S(2)}) collective-permute-start(bf16[3,192,512]{2,1,0:T(8,128)(2,1)} %add_convert_fusion.27), channel_id=1, source_target_pairs={{0,8},{2,6},{8,16},{10,2},{16,24},{18,10},{24,28},{26,18},{28,20},... | collective-permute-start | bytes 1769480 | tf_op jit(solution)/shard_map/ppermute | solution.py:108
  332.1 37.8 %collective-permute-start.70 = (bf16[3,192,512]{2,1,0:T(8,128)(2,1)}, bf16[3,192,512]{2,1,0:T(8,128)(2,1)}, u32[]{:S(2)}, u32[]{:S(2)}) collective-permute-start(bf16[3,192,512]{2,1,0:T(8,128)(2,1)} %add_convert_fusion.20), channel_id=1, source_target_pairs={{0,8},{2,6},{8,16},{10,2},{16,24},{18,10},{24,28},{26,18},{28,20},... | collective-permute-start | bytes 1769480 | tf_op jit(solution)/shard_map/ppermute | solution.py:108
  351.9 25.2 %collective-permute-start.84 = (bf16[3,192,512]{2,1,0:T(8,128)(2,1)}, bf16[3,192,512]{2,1,0:T(8,128)(2,1)}, u32[]{:S(2)}, u32[]{:S(2)}) collective-permute-start(bf16[3,192,512]{2,1,0:T(8,128)(2,1)} %add_convert_fusion.6), channel_id=1, source_target_pairs={{0,8},{2,6},{8,16},{10,2},{16,24},{18,10},{24,28},{26,18},{28,20},... | collective-permute-start | bytes 1769480 | tf_op jit(solution)/shard_map/ppermute | solution.py:108
  368.0 39.3 %collective-permute-start.20 = (bf16[448,1280]{1,0:T(8,128)(2,1)}, bf16[448,1280]{1,0:T(8,128)(2,1)S(1)}, u32[]{:S(2)}, u32[]{:S(2)}) collective-permute-start(bf16[448,1280]{1,0:T(8,128)(2,1)} %shard_map.236), channel_id=1, source_target_pairs={{0,1},{1,0},{2,3},{3,2},{4,5},{5,4},{6,7},{7,6},{8,9},{9,8},{10,11... | collective-permute-start | bytes 3440648 | tf_op jit(solution)/shard_map/ppermute | solution.py:102
  370.0 25.7 %collective-permute-start.64 = (bf16[3,192,512]{2,1,0:T(8,128)(2,1)S(1)}, bf16[3,192,512]{2,1,0:T(8,128)(2,1)S(1)}, u32[]{:S(2)}, u32[]{:S(2)}) collective-permute-start(bf16[3,192,512]{2,1,0:T(8,128)(2,1)S(1)} %add_convert_fusion.26), channel_id=1, source_target_pairs={{0,8},{2,6},{8,16},{10,2},{16,24},{18,10},{24,28},{26,18},{28,20},... | collective-permute-start | bytes 1769480 | tf_op jit(solution)/shard_map/ppermute | solution.py:108
  372.9 24.5 %collective-permute-start.71 = (bf16[3,192,512]{2,1,0:T(8,128)(2,1)S(1)}, bf16[3,192,512]{2,1,0:T(8,128)(2,1)S(1)}, u32[]{:S(2)}, u32[]{:S(2)}) collective-permute-start(bf16[3,192,512]{2,1,0:T(8,128)(2,1)S(1)} %add_convert_fusion.19), channel_id=1, source_target_pairs={{0,8},{2,6},{8,16},{10,2},{16,24},{18,10},{24,28},{26,18},{28,20},... | collective-permute-start | bytes 1769480 | tf_op jit(solution)/shard_map/ppermute | solution.py:108
  394.1 27.3 %collective-permute-start.85 = (bf16[3,192,512]{2,1,0:T(8,128)(2,1)S(1)}, bf16[3,192,512]{2,1,0:T(8,128)(2,1)S(1)}, u32[]{:S(2)}, u32[]{:S(2)}) collective-permute-start(bf16[3,192,512]{2,1,0:T(8,128)(2,1)S(1)} %add_convert_fusion.5), channel_id=1, source_target_pairs={{0,8},{2,6},{8,16},{10,2},{16,24},{18,10},{24,28},{26,18},{28,20},... | collective-permute-start | bytes 1769480 | tf_op jit(solution)/shard_map/ppermute | solution.py:108
  397.4 60.3 %collective-permute-start.65 = (bf16[3,192,512]{2,1,0:T(8,128)(2,1)S(1)}, bf16[3,192,512]{2,1,0:T(8,128)(2,1)S(1)}, u32[]{:S(2)}, u32[]{:S(2)}) collective-permute-start(bf16[3,192,512]{2,1,0:T(8,128)(2,1)S(1)} %add_convert_fusion.25), channel_id=1, source_target_pairs={{0,8},{2,6},{8,16},{10,2},{16,24},{18,10},{24,28},{26,18},{28,20},... | collective-permute-start | bytes 1769480 | tf_op jit(solution)/shard_map/ppermute | solution.py:108
  399.1 70.8 %collective-permute-start.72 = (bf16[3,192,512]{2,1,0:T(8,128)(2,1)S(1)}, bf16[3,192,512]{2,1,0:T(8,128)(2,1)S(1)}, u32[]{:S(2)}, u32[]{:S(2)}) collective-permute-start(bf16[3,192,512]{2,1,0:T(8,128)(2,1)S(1)} %add_convert_fusion.18), channel_id=1, source_target_pairs={{0,8},{2,6},{8,16},{10,2},{16,24},{18,10},{24,28},{26,18},{28,20},... | collective-permute-start | bytes 1769480 | tf_op jit(solution)/shard_map/ppermute | solution.py:108
  411.1 24.5 %collective-permute-start.27 = (bf16[384,2560]{1,0:T(8,128)(2,1)S(1)}, bf16[384,2560]{1,0:T(8,128)(2,1)S(1)}, u32[]{:S(2)}, u32[]{:S(2)}) collective-permute-start(bf16[384,2560]{1,0:T(8,128)(2,1)S(1)} %constant_dynamic-slice_fusion.9), channel_id=1, source_target_pairs={{0,2},{2,0},{4,6},{6,4},{8,10},{10,8},{12,14},{14,12},{16,18},{18,... | collective-permute-start | bytes 5898248 | tf_op jit(solution)/shard_map/ppermute | solution.py:105
  443.8 34.4 %collective-permute-start.79 = (bf16[3,192,512]{2,1,0:T(8,128)(2,1)S(1)}, bf16[3,192,512]{2,1,0:T(8,128)(2,1)S(1)}, u32[]{:S(2)}, u32[]{:S(2)}) collective-permute-start(bf16[3,192,512]{2,1,0:T(8,128)(2,1)S(1)} %add_convert_fusion.11), channel_id=1, source_target_pairs={{0,8},{2,6},{8,16},{10,2},{16,24},{18,10},{24,28},{26,18},{28,20},... | collective-permute-start | bytes 1769480 | tf_op jit(solution)/shard_map/ppermute | solution.py:108
  455.1 29.3 %collective-permute-start.86 = (bf16[3,192,512]{2,1,0:T(8,128)(2,1)S(1)}, bf16[3,192,512]{2,1,0:T(8,128)(2,1)S(1)}, u32[]{:S(2)}, u32[]{:S(2)}) collective-permute-start(bf16[3,192,512]{2,1,0:T(8,128)(2,1)S(1)} %add_convert_fusion.4), channel_id=1, source_target_pairs={{0,8},{2,6},{8,16},{10,2},{16,24},{18,10},{24,28},{26,18},{28,20},... | collective-permute-start | bytes 1769480 | tf_op jit(solution)/shard_map/ppermute | solution.py:108
  456.0 98.7 %collective-permute-start.22 = (bf16[224,768]{1,0:T(8,128)(2,1)S(1)}, bf16[224,768]{1,0:T(8,128)(2,1)S(1)}, u32[]{:S(2)}, u32[]{:S(2)}) collective-permute-start(bf16[224,768]{1,0:T(8,128)(2,1)S(1)} %get-tuple-element.78), channel_id=1, source_target_pairs={{0,1},{1,0},{2,3},{3,2},{4,5},{5,4},{6,7},{7,6},{8,9},{9,8},{10,11... | collective-permute-start | bytes 1032200 | tf_op jit(solution)/shard_map/ppermute | solution.py:102
  492.8 63.0 %collective-permute-start.87 = (bf16[4,3,96,512]{3,2,1,0:T(8,128)(2,1)S(1)}, bf16[4,3,96,512]{3,2,1,0:T(8,128)(2,1)S(1)}, u32[]{:S(2)}, u32[]{:S(2)}) collective-permute-start(bf16[4,3,96,512]{3,2,1,0:T(8,128)(2,1)S(1)} %get-tuple-element.74), channel_id=1, source_target_pairs={{0,2},{2,0},{4,6},{6,4},{8,10},{10,8},{12,14},{14,12},{16,18},{18,... | collective-permute-start | bytes 3538952 | tf_op jit(solution)/shard_map/ppermute | solution.py:105
  508.5 39.5 %collective-permute-start.56 = (bf16[96,768]{1,0:T(8,128)(2,1)S(1)}, bf16[96,768]{1,0:T(8,128)(2,1)S(1)}, u32[]{:S(2)}, u32[]{:S(2)}) collective-permute-start(bf16[96,768]{1,0:T(8,128)(2,1)S(1)} %collective-permute-done.55), channel_id=1, source_target_pairs={{0,8},{2,6},{8,16},{10,2},{16,24},{18,10},{24,28},{26,18},{28,20},... | collective-permute-start | bytes 442376 | tf_op jit(solution)/shard_map/ppermute | solution.py:108
  (97 other events, 1079.8 us)

commit v3 on v2

v3 whole, which is shorter than its diff:
```python
import functools

import jax
import jax.numpy as jnp
from jax import lax
from jax.experimental import pallas as pl
from jax.experimental.pallas import tpu as pltpu
from jax.sharding import PartitionSpec as P

HEAD_DIM = 64
LANES = 128
EPS = 1e-06
BF = jnp.bfloat16
F32 = jnp.float32
VMEM_LIMIT = 60 << 20


def tree_layout(position, seg_len):
    trunk_len = 4 * seg_len
    beyond = position - trunk_len
    segment = jnp.where(position < trunk_len, 0, 1 + beyond // seg_len)
    inner = jnp.where(
        segment <= 4, trunk_len + beyond % seg_len, trunk_len + seg_len + beyond % seg_len
    )
    depth_position = jnp.where(position < trunk_len, position, inner)
    return (segment, depth_position)


def lookup(segment, parents_row):
    labels = jnp.arange(parents_row.shape[0], dtype=jnp.int32)
    picked = jnp.where(segment[:, None] == labels[None, :], parents_row[None, :], 0)
    return jnp.sum(picked, axis=1)


def tree_mask(query_index, key_index, parents_row, seg_len):
    query_seg, _ = tree_layout(query_index, seg_len)
    key_seg, _ = tree_layout(key_index, seg_len)
    parent_one = lookup(query_seg, parents_row)
    parent_two = lookup(parent_one, parents_row)
    key_row = key_seg[None, :]
    related = (
        (key_row == query_seg[:, None])
        | (key_row == parent_one[:, None])
        | (key_row == parent_two[:, None])
    )
    return related & (key_index[None, :] <= query_index[:, None])


def angle_tables(depth_position):
    half = HEAD_DIM // 2
    frequency = 10000.0 ** (-2.0 * jnp.arange(half, dtype=F32) / HEAD_DIM)
    angles = depth_position.astype(F32)[:, None] * frequency[None, :]
    cosine, sine = jnp.cos(angles), jnp.sin(angles)
    return (
        jnp.concatenate([cosine] * 4, 1),
        jnp.concatenate([-sine, sine, -sine, sine], 1),
    )


def dot(a, b, dims):
    return lax.dot_general(a, b, (dims, ((), ())), preferred_element_type=F32)


def nn(a, b):
    return dot(a, b, ((1,), (0,)))


def nt(a, b):
    return dot(a, b, ((1,), (1,)))


def tn(a, b):
    return dot(a, b, ((0,), (0,)))


class Mesh:
    def __init__(self):
        self.groups = lax.axis_size("shard")
        self.member = lax.axis_index("shard")
        self.reps = lax.axis_size("rep")
        self.rep = lax.axis_index("rep")
        self.core = self.rep % 2
        self.chip = self.rep // 2
        self.chips = self.reps // 2
        rows = self.chips // 2
        order = [2 * z for z in range(rows)] + [2 * z + 1 for z in range(rows - 1, -1, -1)]
        self.ring = []
        for place, chip in enumerate(order):
            after, before = order[(place + 1) % self.chips], order[place - 1]
            self.ring += [(2 * chip, 2 * after), (2 * chip + 1, 2 * before + 1)]
        self.place = jnp.where(
            self.chip % 2 == 0, self.chip // 2, self.chips - 1 - self.chip // 2
        )
        self.way = 1 - 2 * self.core

    def chip_at(self, place):
        place = place % self.chips
        rows = self.chips // 2
        return jnp.where(place < rows, 2 * place, 2 * (self.chips - 1 - place) + 1)

    def swap_shard(self, v):
        return lax.ppermute(v, "shard", [(0, 1), (1, 0)])

    def swap_core(self, v):
        return lax.ppermute(v, "rep", [(r, r ^ 1) for r in range(self.reps)])

    def along_ring(self, v):
        return lax.ppermute(v, "rep", self.ring)

    def part(self, v, axis, which):
        size = v.shape[axis] // self.groups
        return lax.dynamic_slice_in_dim(v, which * size, size, axis)

    def gather(self, v, axis):
        if self.groups != 2:
            return lax.all_gather(v, "shard", axis=axis, tiled=True)
        other = self.swap_shard(v)
        return self.in_order(self.member, v, other, axis)

    def in_order(self, which, mine, other, axis):
        return jnp.where(
            which == 0,
            jnp.concatenate([mine, other], axis),
            jnp.concatenate([other, mine], axis),
        )

    def exchange(self, v, split_axis, concat_axis):
        if self.groups != 2:
            return lax.all_to_all(v, "shard", split_axis, concat_axis, tiled=True)
        other = self.swap_shard(self.part(v, split_axis, 1 - self.member))
        mine = self.part(v, split_axis, self.member)
        return self.in_order(self.member, mine, other, concat_axis)

    def scatter(self, v, axis):
        if self.groups != 2:
            return lax.psum_scatter(
                v.astype(BF), "shard", scatter_dimension=axis, tiled=True
            ).astype(F32)
        other = self.swap_shard(self.part(v, axis, 1 - self.member).astype(BF))
        return self.part(v, axis, self.member).astype(F32) + other.astype(F32)

    def total(self, v):
        if self.groups != 2:
            return lax.psum(v, "shard")
        return v + self.swap_shard(v)

    def ring_sum(self, v):
        chunk = v.shape[0] // self.chips
        ring = Scatter(self, lambda chip: lax.dynamic_slice_in_dim(v, chip * chunk, chunk, 0))
        for _ in range(self.chips - 1):
            ring.start()
            ring.finish()
        ring = Gather(self, ring.held)
        for _ in range(self.chips - 1):
            ring.start()
            ring.finish()
        return ring.whole

    def all_reduce(self, v):
        half = v.shape[0] // 2
        v = v.astype(BF)
        mine = lax.dynamic_slice_in_dim(v, self.core * half, half, 0)
        other = self.swap_core(
            lax.dynamic_slice_in_dim(v, (1 - self.core) * half, half, 0)
        )
        whole = self.ring_sum((mine.astype(F32) + other.astype(F32)).astype(BF))
        return self.in_order(self.core, whole, self.swap_core(whole), 0).astype(F32)

    def butterfly(self, v):
        bit = 1
        while bit < self.reps:
            v = v + lax.ppermute(v, "rep", [(r, r ^ bit) for r in range(self.reps)])
            bit *= 2
        return v


class Scatter:
    def __init__(self, me, own):
        self.me, self.own, self.hops = me, own, 0
        self.held = own(me.chip_at(me.place - me.way))

    def start(self, *deps):
        self.came = self.me.along_ring(tie(self.held, deps))

    def finish(self):
        self.hops += 1
        mine = self.own(self.me.chip_at(self.me.place - self.me.way * (self.hops + 1)))
        self.held = (self.came.astype(F32) + mine.astype(F32)).astype(BF)
        return self.came


class Gather:
    def __init__(self, me, held):
        self.me, self.held, self.hops = me, held, 0
        self.size = held.shape[0]
        whole = jnp.zeros((self.size * me.chips, held.shape[1]), held.dtype)
        self.whole = self.put(whole, me.place)

    def put(self, whole, place):
        at = self.me.chip_at(place) * self.size
        return lax.dynamic_update_slice_in_dim(whole, self.held, at, 0)

    def start(self, *deps):
        self.came = self.me.along_ring(tie(self.held, deps))

    def finish(self):
        self.hops += 1
        self.held = self.came
        self.whole = self.put(self.whole, self.me.place - self.me.way * self.hops)
        return self.came


def pairs(heads):
    return -(-heads // 2)


def rope(v, cos, sin, back):
    lane = lax.broadcasted_iota(jnp.int32, (1, LANES), 1)
    first = lane % HEAD_DIM < HEAD_DIM // 2
    out = []
    for i in range(v.shape[1] // LANES):
        x = v[:, i * LANES : (i + 1) * LANES]
        other = jnp.where(
            first,
            pltpu.roll(x, LANES - HEAD_DIM // 2, 1),
            pltpu.roll(x, HEAD_DIM // 2, 1),
        )
        out.append(x * cos - other * sin if back else x * cos + other * sin)
    return out


def halves(x, parity):
    low = lax.broadcasted_iota(jnp.int32, (1, LANES), 1) < HEAD_DIM
    zero = jnp.zeros_like(x)
    turned = pltpu.roll(x, HEAD_DIM, 1)
    a, b = (x, turned) if parity == 0 else (turned, x)
    return jnp.where(low, a, zero).astype(BF), jnp.where(low, zero, b).astype(BF)


def attend_kernel(
    q_heads, kv_heads, own_ref, came_ref, cos_ref, sin_ref, bias_ref, along_ref,
    out_ref, lse_ref, q_ref, k_ref, v_ref, sent_ref,
):
    sent_ref[...] = along_ref[...]
    per = q_heads // kv_heads
    rows = own_ref.shape[0]
    qp, kp = pairs(q_heads), pairs(kv_heads)
    cos, sin = cos_ref[...], sin_ref[...]
    raw = own_ref[...].astype(F32) + came_ref[...].astype(F32)
    scale = HEAD_DIM**-0.5
    q = [(t * scale).astype(BF) for t in rope(raw[:, : qp * LANES], cos, sin, False)]
    keys = rope(raw[:, qp * LANES : (qp + kp) * LANES], cos, sin, False)
    for i in range(qp):
        q_ref[:, i * LANES : (i + 1) * LANES] = q[i]
    ks, vs = [], []
    for g in range(kv_heads):
        at = (qp + kp + g // 2) * LANES
        ks.append(halves(keys[g // 2], g % 2))
        vs.append(halves(raw[:, at : at + LANES], g % 2))
        for p in range(2):
            k_ref[g, p] = ks[g][p]
            v_ref[g, p] = vs[g][p]
    half = rows // 2
    for lo, n in ((0, half), (half, rows)):
        bias = bias_ref[lo : lo + half, :n]
        for i in range(qp):
            out = jnp.zeros((half, LANES), F32)
            for h in range(2 * i, min(2 * i + 2, q_heads)):
                g, p = h // per, h % 2
                s = nt(q[i][lo : lo + half], ks[g][p][:n]) + bias
                peak = jnp.max(s, axis=-1, keepdims=True)
                e = jnp.exp(s - peak)
                total = jnp.sum(e, axis=-1, keepdims=True)
                lse_ref[lo : lo + half, h : h + 1] = peak + jnp.log(total)
                out = out + nn((e * (1.0 / total)).astype(BF), vs[g][p][:n])
            out_ref[lo : lo + half, i * LANES : (i + 1) * LANES] = out.astype(BF)


def attend(own, came, cos, sin, bias, along, q_heads, kv_heads):
    rows = own.shape[0]
    qp = pairs(q_heads)
    return pl.pallas_call(
        functools.partial(attend_kernel, q_heads, kv_heads),
        out_shape=[
            jax.ShapeDtypeStruct((rows, qp * LANES), BF),
            jax.ShapeDtypeStruct((rows, LANES), F32),
            jax.ShapeDtypeStruct((rows, qp * LANES), BF),
            jax.ShapeDtypeStruct((kv_heads, 2, rows, LANES), BF),
            jax.ShapeDtypeStruct((kv_heads, 2, rows, LANES), BF),
            jax.ShapeDtypeStruct(along.shape, along.dtype),
        ],
        compiler_params=pltpu.CompilerParams(vmem_limit_bytes=VMEM_LIMIT),
        cost_estimate=pl.CostEstimate(
            flops=1200 * rows * rows * q_heads,
            bytes_accessed=8 << 20,
            transcendentals=rows * rows * q_heads,
        ),
    )(own, came, cos, sin, bias, along)


def attend_back_kernel(
    q_heads, kv_heads, own_ref, came_ref, q_ref, k_ref, v_ref, lse_ref,
    cos_ref, sin_ref, bias_ref, *refs,
):
    per = q_heads // kv_heads
    rows = own_ref.shape[0]
    qp, kp = pairs(q_heads), pairs(kv_heads)
    cos, sin = cos_ref[...], sin_ref[...]
    scale = HEAD_DIM**-0.5
    low = lax.broadcasted_iota(jnp.int32, (1, LANES), 1) < HEAD_DIM
    grad = (own_ref[...].astype(F32) + came_ref[...].astype(F32)).astype(BF)
    lse = lse_ref[...].T
    half = rows // 2
    out_ref = refs[-1]

    def put(at, v):
        out_ref[:, at * LANES : (at + 1) * LANES] = v.astype(BF)

    def blocks():
        return [
            [[jnp.zeros((half, LANES), F32) for _ in range(2)] for _ in range(2)]
            for _ in range(kv_heads)
        ]

    dk, dv = blocks(), blocks()
    for i in range(qp):
        parts = []
        for lo, n in ((0, half), (half, rows)):
            q = q_ref[lo : lo + half, i * LANES : (i + 1) * LANES]
            go = grad[lo : lo + half, i * LANES : (i + 1) * LANES]
            bias = bias_ref[:n, lo : lo + half]
            dq = jnp.zeros((half, LANES), F32)
            for h in range(2 * i, min(2 * i + 2, q_heads)):
                g, p = h // per, h % 2
                k, v = k_ref[g, p, :n], v_ref[g, p, :n]
                s = nt(k, q) + bias
                probs = jnp.exp(s - lse[h : h + 1, lo : lo + half])
                dp = nt(v, go)
                delta = jnp.sum(probs * dp, axis=0, keepdims=True)
                ds = (probs * (dp - delta)).astype(BF)
                dq = dq + tn(ds, k)
                ck, cv = nn(ds, q), nn(probs.astype(BF), go)
                for b in range(n // half):
                    dk[g][p][b] = dk[g][p][b] + ck[b * half : (b + 1) * half]
                    dv[g][p][b] = dv[g][p][b] + cv[b * half : (b + 1) * half]
            parts.append(dq * scale)
        put(i, rope(jnp.concatenate(parts, 0), cos, sin, True)[0])

    def packed(d, j):
        got = jnp.zeros((rows, LANES), F32)
        for g in range(2 * j, min(2 * j + 2, kv_heads)):
            a, b = (jnp.concatenate(d[g][p], 0) for p in range(2))
            a, b = jnp.where(low, a, 0.0), jnp.where(low, 0.0, b)
            if g % 2 == 0:
                got = got + a + pltpu.roll(b, HEAD_DIM, 1)
            else:
                got = got + b + pltpu.roll(a, HEAD_DIM, 1)
        return got

    for j in range(kp):
        put(qp + j, rope(packed(dk, j), cos, sin, True)[0])
        put(qp + kp + j, packed(dv, j))


def attend_back(own, came, q, k, v, lse, cos, sin, bias, q_heads, kv_heads, deps):
    rows = own.shape[0]
    lanes = (pairs(q_heads) + 2 * pairs(kv_heads)) * LANES
    specs, deps = after(deps)
    return pl.pallas_call(
        functools.partial(attend_back_kernel, q_heads, kv_heads),
        in_specs=[pl.BlockSpec(memory_space=pltpu.VMEM)] * 9 + specs,
        out_shape=jax.ShapeDtypeStruct((rows, lanes), BF),
        compiler_params=pltpu.CompilerParams(vmem_limit_bytes=VMEM_LIMIT),
        cost_estimate=pl.CostEstimate(
            flops=1600 * rows * rows * q_heads,
            bytes_accessed=8 << 20,
            transcendentals=rows * rows * q_heads,
        ),
    )(own, came, q, k, v, lse, cos, sin, bias, *deps)


def after(arrays):
    return [pl.BlockSpec(memory_space=pl.ANY)] * len(arrays), tuple(arrays)


def row_tile(rows):
    return rows if rows <= 896 else 448


def params():
    return pltpu.CompilerParams(vmem_limit_bytes=VMEM_LIMIT)


def cost(flops, megabytes, transcendentals=0):
    return pl.CostEstimate(
        flops=int(flops), bytes_accessed=megabytes << 20, transcendentals=int(transcendentals)
    )


def to_row(column):
    rows = column.shape[0]
    return jnp.broadcast_to(column, (rows, LANES)).T[:1]


def to_column(row):
    return jnp.broadcast_to(row, (LANES, row.shape[1])).T[:, :1]


def put_column(ref, column):
    rows = column.shape[0]
    row = to_row(column)
    high = row.astype(BF)
    low = (row - high.astype(F32)).astype(BF)
    line = lax.broadcasted_iota(jnp.int32, (16, rows), 0)
    ref[rows : rows + 16, :] = jnp.zeros((16, ref.shape[1]), BF)
    ref[rows : rows + 16, :rows] = jnp.where(
        line == 0, high.astype(F32), jnp.where(line == 1, low.astype(F32), 0.0)
    ).astype(BF)


def get_column(ref):
    rows = ref.shape[0] - 16
    last = ref[rows : rows + 16, :rows].astype(F32)
    return to_column(last[0:1] + last[1:2])


def split_kernel(where, x_ref, packet_ref, along_ref, theirs_ref, mine_ref, sent_ref, gone_ref):
    rows, size = x_ref.shape[0], mine_ref.shape[1]
    sent_ref[...] = packet_ref[...]
    gone_ref[...] = along_ref[...]
    x = x_ref[...].astype(F32)
    squares = jnp.sum(x * x, axis=-1, keepdims=True)
    for ref, member in ((theirs_ref, 1 - where[0]), (mine_ref, where[0])):
        ref[:rows, :] = x_ref[:, pl.ds(pl.multiple_of(member * size, LANES), size)]
        put_column(ref, squares)


def split(member, x, packet, along):
    rows, width = x.shape
    out = jax.ShapeDtypeStruct((rows + 16, width // 2), BF)
    return pl.pallas_call(
        split_kernel,
        in_specs=[pl.BlockSpec(memory_space=pltpu.SMEM)]
        + [pl.BlockSpec(memory_space=pltpu.VMEM)] * 3,
        out_shape=[
            out,
            out,
            jax.ShapeDtypeStruct(packet.shape, BF),
            jax.ShapeDtypeStruct(along.shape, BF),
        ],
        compiler_params=params(),
        cost_estimate=cost(0, 2),
    )(jnp.reshape(member, (1,)), x, packet, along)


def heads_product(hidden, member, part, parts, weights):
    found = []
    for w in weights:
        size = w.shape[1] // (2 * parts)
        at = pl.ds(pl.multiple_of((member * parts + part) * size, LANES), size)
        found.append(nn(hidden, w[:, at]))
    return jnp.concatenate(found, 1)


def project_theirs_kernel(parts, where, mine_ref, came_ref, gain_ref, wq, wk, wv, *refs):
    outs, (hidden_ref, x_ref, inv_ref) = refs[:parts], refs[parts:]
    rows, columns = mine_ref.shape[0] - 16, mine_ref.shape[1]
    gain = gain_ref[...].astype(F32)
    for message, member in ((mine_ref, where[0]), (came_ref, 1 - where[0])):
        at = pl.ds(pl.multiple_of(member * rows, 16), rows)
        inv = lax.rsqrt(get_column(message) / (2 * columns) + EPS)
        inv_ref[at, :] = inv
        x = message[:rows, :]
        x_ref[at, :] = x
        hidden_ref[at, :] = (x.astype(F32) * inv * gain).astype(BF)
    for part in range(parts):
        outs[part][...] = heads_product(
            hidden_ref[...], 1 - where[0], part, parts, (wq, wk, wv)
        ).astype(BF)


def project_theirs(member, parts, mine, came, gain, weights):
    rows, columns = 2 * (mine.shape[0] - 16), mine.shape[1]
    lanes = sum(w.shape[1] for w in weights) // (2 * parts)
    return pl.pallas_call(
        functools.partial(project_theirs_kernel, parts),
        in_specs=[pl.BlockSpec(memory_space=pltpu.SMEM)]
        + [pl.BlockSpec(memory_space=pltpu.VMEM)] * 6,
        out_shape=[jax.ShapeDtypeStruct((rows, lanes), BF)] * parts
        + [
            jax.ShapeDtypeStruct((rows, columns), BF),
            jax.ShapeDtypeStruct((rows, columns), BF),
            jax.ShapeDtypeStruct((rows, 1), F32),
        ],
        compiler_params=params(),
        cost_estimate=cost(4 * rows * columns * lanes * parts, 6),
    )(jnp.reshape(member, (1,)), mine, came, gain, *weights)


def project_own_kernel(parts, where, hidden_ref, wq, wk, wv, *refs):
    for part in range(parts):
        refs[part - parts][...] = heads_product(
            hidden_ref[...], where[0], part, parts, (wq, wk, wv)
        )


def project_own(member, parts, hidden, weights, deps):
    rows, columns = hidden.shape
    lanes = sum(w.shape[1] for w in weights) // (2 * parts)
    specs, deps = after(deps)
    return pl.pallas_call(
        functools.partial(project_own_kernel, parts),
        in_specs=[pl.BlockSpec(memory_space=pltpu.SMEM)]
        + [pl.BlockSpec(memory_space=pltpu.VMEM)] * 4
        + specs,
        out_shape=[jax.ShapeDtypeStruct((rows, lanes), F32)] * parts,
        compiler_params=params(),
        cost_estimate=cost(4 * rows * columns * lanes * parts, 6),
    )(jnp.reshape(member, (1,)), hidden, *weights, *deps)


def project_back_kernel(
    parts, where, x_ref, inv_ref, gain_ref, wq_ref, wk_ref, wv_ref, *refs
):
    grads = refs[: 2 * parts]
    scaled_ref, sums_ref, gain_grad_ref = refs[-3:]
    total = jnp.zeros(x_ref.shape, F32)
    for part in range(parts):
        for grad, member in ((grads[2 * part], where[0]), (grads[2 * part + 1], 1 - where[0])):
            start = 0
            for w in (wq_ref, wk_ref, wv_ref):
                size = w.shape[1] // (2 * parts)
                at = pl.ds(pl.multiple_of((member * parts + part) * size, LANES), size)
                total += nt(grad[:, start : start + size], w[:, at])
                start += size
    normed = x_ref[...].astype(F32) * inv_ref[...]
    scaled = total * gain_ref[...].astype(F32)
    scaled_ref[...] = scaled
    sums_ref[...] = jnp.sum(scaled * normed, axis=-1, keepdims=True)
    gain_grad_ref[...] = jnp.sum(total * normed, axis=0, keepdims=True)


def project_back(member, x, inv, gain, weights, grads, deps):
    rows, columns = x.shape
    parts = len(grads)
    flat = [a for pair in grads for a in pair]
    specs, deps = after(deps)
    whole = pl.BlockSpec(memory_space=pltpu.VMEM)
    return pl.pallas_call(
        functools.partial(project_back_kernel, parts),
        in_specs=[pl.BlockSpec(memory_space=pltpu.SMEM)] + [whole] * (6 + len(flat)) + specs,
        out_shape=[
            jax.ShapeDtypeStruct((rows, columns), F32),
            jax.ShapeDtypeStruct((rows, 1), F32),
            jax.ShapeDtypeStruct((1, columns), F32),
        ],
        compiler_params=params(),
        cost_estimate=cost(2 * rows * columns * sum(w.shape[1] for w in weights), 10),
    )(jnp.reshape(member, (1,)), x, inv, gain, *weights, *flat, *deps)


def weight_grads_kernel(where, *refs):
    hidden, out_ref = refs[:2], refs[-1]
    size = refs[2].shape[1]
    out_ref[:, 2 * size :] = refs[10][...]
    for core in range(2):

        @pl.when(where[1] == core)
        def _():
            for i, member in ((0, where[0]), (1, 1 - where[0])):
                total = sum(tn(hidden[t][...], refs[2 + 4 * t + 2 * core + i][...]) for t in range(2))
                at = pl.ds(pl.multiple_of(member * size, LANES), size)
                out_ref[:, at] = total.astype(BF)


def weight_grads(member, core, hidden, grads, beside, deps):
    columns = hidden[0].shape[1]
    flat = [a for tree in grads for pair in tree for a in pair]
    rows, lanes = flat[0].shape
    specs, deps = after(deps)
    return pl.pallas_call(
        weight_grads_kernel,
        in_specs=[pl.BlockSpec(memory_space=pltpu.SMEM)]
        + [pl.BlockSpec(memory_space=pltpu.VMEM)] * (3 + len(flat))
        + specs,
        out_shape=jax.ShapeDtypeStruct((columns, 2 * lanes + beside.shape[1]), BF),
        compiler_params=params(),
        cost_estimate=cost(8 * rows * columns * lanes, 8),
    )(jnp.stack([member, core]), *hidden, *flat, beside, *deps)


def middle_kernel(count, where, *refs):
    pieces, (w_ref, x_ref) = refs[:count], refs[count : count + 2]
    middle_ref, low_ref, squares_ref = refs[-3:]
    total = x_ref[...].astype(F32)
    for i, piece in enumerate(pieces):
        size = piece.shape[1]
        total += nn(piece[...], w_ref[pl.ds(pl.multiple_of(where[i], 64), size), :])
    squares = jnp.sum(total * total, axis=-1, keepdims=True)
    middle_ref[...] = total
    low_ref[: total.shape[0], :] = total.astype(BF)
    squares_ref[...] = squares
    if low_ref.shape[0] > total.shape[0]:
        put_column(low_ref, squares)


def middle_of(pieces, where, w_out, x, packed):
    rows, columns = x.shape
    tile = rows if packed else 448
    more = 16 if packed else 0

    def row(i, w):
        return (i, 0)

    return pl.pallas_call(
        functools.partial(middle_kernel, len(pieces)),
        grid_spec=pltpu.PrefetchScalarGridSpec(
            num_scalar_prefetch=1,
            grid=(rows // tile,),
            in_specs=[pl.BlockSpec((tile, p.shape[1]), row) for p in pieces]
            + [
                pl.BlockSpec(w_out.shape, lambda i, w: (0, 0)),
                pl.BlockSpec((tile, columns), row),
            ],
            out_specs=[
                pl.BlockSpec((tile, columns), row),
                pl.BlockSpec((tile + more, columns), row),
                pl.BlockSpec((tile, 1), row),
            ],
        ),
        out_shape=[
            jax.ShapeDtypeStruct((rows, columns), F32),
            jax.ShapeDtypeStruct((rows + more, columns), BF),
            jax.ShapeDtypeStruct((rows, 1), F32),
        ],
        compiler_params=params(),
        cost_estimate=cost(2 * rows * columns * w_out.shape[0], 6),
    )(where, *pieces, w_out, x)


def hidden_kernel(count, parts, width, where, *refs):
    gain_ref, router_ref = refs[:2]
    h_ref, gates_ref = refs[-2:]
    for tree in range(2):
        mine = refs[2 + tree * (count + parts + 1) :]
        pieces, squares, on = mine[:count], mine[count : count + parts], mine[count + parts][...]
        total = squares[0][...]
        for more in squares[1:]:
            total += more[...]
        inv = lax.rsqrt(total / width + EPS)
        for i, piece in enumerate(pieces):
            size = piece.shape[1]
            at = pl.ds(pl.multiple_of(where[i] * size, LANES), size)
            gain = gain_ref[:, at].astype(F32)
            h_ref[tree, :, at] = (piece[...].astype(F32) * inv * gain).astype(BF)
        logits = jnp.where(on > 0, nn(h_ref[tree], router_ref[...]), -1e30)
        peak = jnp.max(logits, axis=-1, keepdims=True)
        e = jnp.exp(logits - peak) * on
        gates_ref[tree] = e / jnp.sum(e, axis=-1, keepdims=True)


def hidden_of(trees, where, gain, router):
    pieces, squares, on = trees[0]
    rows = on.shape[0]
    width, experts = router.shape
    tile = 448

    def row(i, w):
        return (i, 0)

    def all_of(i, w):
        return (0, 0)

    def both(i, w):
        return (0, i, 0)

    specs = [pl.BlockSpec((tile, p.shape[1]), row) for p in (*pieces, *squares, on)]
    return pl.pallas_call(
        functools.partial(hidden_kernel, len(pieces), len(squares), width),
        grid_spec=pltpu.PrefetchScalarGridSpec(
            num_scalar_prefetch=1,
            grid=(rows // tile,),
            in_specs=[pl.BlockSpec((1, width), all_of), pl.BlockSpec((width, experts), all_of)]
            + specs
            + specs,
            out_specs=[
                pl.BlockSpec((2, tile, width), both),
                pl.BlockSpec((2, tile, experts), both),
            ],
        ),
        out_shape=[
            jax.ShapeDtypeStruct((2, rows, width), BF),
            jax.ShapeDtypeStruct((2, rows, experts), F32),
        ],
        compiler_params=params(),
        cost_estimate=cost(4 * rows * width * 256, 8, rows * 32),
    )(where, gain, router, *(a for p, q, o in trees for a in (*p, *q, o)))


PACKET_ROWS = 48


def hidden_packed_kernel(where, *refs):
    h_ref, gates_ref, inv_ref, on_ref = refs[8:]
    member = (where[0], 1 - where[0])
    for tree in range(2):
        messages, packets = refs[4 * tree : 4 * tree + 2], refs[4 * tree + 2 : 4 * tree + 4]
        rows, columns = messages[0].shape[0] - 16, messages[0].shape[1]
        squares = get_column(messages[0]) + get_column(messages[1])
        inv = lax.rsqrt(squares / (2 * columns) + EPS)
        if tree == 0:
            inv_ref[...] = inv
        logits = 0.0
        for i in range(2):
            at = pl.ds(pl.multiple_of(member[i] * columns, LANES), columns)
            gain = packets[i][16:32, :].astype(F32)[:1]
            h = (messages[i][:rows, :].astype(F32) * inv * gain).astype(BF)
            h_ref[tree, :, at] = h
            logits = logits + nt(h, packets[i][:16, :])
            tokens = rows // 2
            on_ref[pl.ds(pl.multiple_of(member[i] * tokens, 16), tokens), :] = (
                packets[i][32:48, :tokens].astype(F32).T
            )
        on = on_ref[...]
        logits = jnp.where(on > 0, logits, -1e30)
        peak = jnp.max(logits, axis=-1, keepdims=True)
        e = jnp.exp(logits - peak) * on
        gates_ref[tree] = e / jnp.sum(e, axis=-1, keepdims=True)


def hidden_packed(member, trees):
    rows, columns = trees[0][0].shape[0] - 16, trees[0][0].shape[1]
    return pl.pallas_call(
        hidden_packed_kernel,
        in_specs=[pl.BlockSpec(memory_space=pltpu.SMEM)]
        + [pl.BlockSpec(memory_space=pltpu.VMEM)] * 8,
        out_shape=[
            jax.ShapeDtypeStruct((2, rows, 2 * columns), BF),
            jax.ShapeDtypeStruct((2, rows, 16), F32),
            jax.ShapeDtypeStruct((rows, 1), F32),
        ],
        scratch_shapes=[pltpu.VMEM((rows, 16), F32)],
        compiler_params=params(),
        cost_estimate=cost(4 * rows * columns * 256, 8),
    )(jnp.reshape(member, (1,)), *(a for tree in trees for a in tree))


def expert_grads_kernel(
    chained, steps, where, h_ref, g_ref, on_ref, wg_ref, wu_ref, wd_ref, *refs
):
    mid_ref, gg_ref, own_ref = refs[-3:] if steps == 1 else refs[-4:-1]
    step = pl.program_id(0)
    h, g = h_ref[...], g_ref[...]
    lane = lax.broadcasted_iota(jnp.int32, (1, on_ref.shape[1]), 1) == where[1]
    on = jnp.sum(jnp.where(lane, on_ref[...], 0.0), axis=-1, keepdims=True)
    gate_pre = nn(h, wg_ref[0])
    up_pre = nn(h, wu_ref[0])
    grad_mid = nt(g, wd_ref[0])
    sig = 1.0 / (1.0 + jnp.exp(-gate_pre))
    silu = gate_pre * sig
    mid = silu * up_pre
    column = jnp.where(lane, jnp.sum(grad_mid * mid, axis=-1, keepdims=True), 0.0)
    gg_ref[...] = refs[0][...] + column if chained else column
    act = (on * mid).astype(BF)
    grad_mid = on * grad_mid
    ggp = (grad_mid * up_pre * (sig * (1.0 + gate_pre * (1.0 - sig)))).astype(BF)
    gup = (grad_mid * silu).astype(BF)
    mid_ref[0, 0] = act
    mid_ref[0, 1] = ggp
    mid_ref[0, 2] = gup
    if steps == 1:
        own_ref[0] = tn(h, ggp).astype(BF)
        own_ref[1] = tn(h, gup).astype(BF)
        own_ref[2] = tn(g, act).astype(BF)
        return
    acc = refs[-1]

    @pl.when(step == 0)
    def _():
        acc[...] = jnp.zeros_like(acc)

    acc[0] += tn(h, ggp)
    acc[1] += tn(h, gup)
    acc[2] += tn(g, act)

    @pl.when(step == steps - 1)
    def _():
        own_ref[...] = acc[...].astype(BF)


def expert_grads(
    j, per_core, which, column, h, g, on, w_gate, w_up, w_down, before, slot, slots, deps
):
    rows, width = h.shape
    hidden = w_gate.shape[2]
    experts = on.shape[1]
    tile = row_tile(rows)
    steps = rows // tile

    def row(i, w):
        return (i, 0)

    def weight(i, w):
        return (w[0], 0, 0)

    chained = before is not None
    more = [pl.BlockSpec((tile, experts), row), pl.BlockSpec(memory_space=pl.ANY)] * chained
    aliases = {8: 0} if chained else {}
    if slot:
        aliases[9] = 2
        deps = (before[2], *deps)
    specs, deps = after(deps)
    return pl.pallas_call(
        functools.partial(expert_grads_kernel, chained, steps),
        grid_spec=pltpu.PrefetchScalarGridSpec(
            num_scalar_prefetch=1,
            grid=(steps,),
            in_specs=[
                pl.BlockSpec((tile, width), row),
                pl.BlockSpec((tile, width), row),
                pl.BlockSpec((tile, experts), row),
                pl.BlockSpec((1, width, hidden), weight),
                pl.BlockSpec((1, width, hidden), weight),
                pl.BlockSpec((1, hidden, width), weight),
            ]
            + more
            + specs,
            out_specs=[
                pl.BlockSpec((1, 3, tile, hidden), lambda i, w: (j, 0, i, 0)),
                pl.BlockSpec((tile, experts), row),
                pl.BlockSpec((3, width, hidden), lambda i, w: (slot, 0, 0)),
            ],
            scratch_shapes=[pltpu.VMEM((3, width, hidden), F32)] * (steps > 1),
        ),
        out_shape=[
            jax.ShapeDtypeStruct((per_core, 3, rows, hidden), BF),
            jax.ShapeDtypeStruct((rows, experts), F32),
            jax.ShapeDtypeStruct((3 * slots, width, hidden), BF),
        ],
        input_output_aliases=aliases,
        compiler_params=params(),
        cost_estimate=cost(16 * rows * width * hidden, 20, rows * hidden),
    )(
        jnp.stack([which, column]).astype(jnp.int32),
        h, g, on, w_gate, w_up, w_down,
        *((before[1], before[0]) if chained else ()),
        *deps,
    )


def expert_hidden_kernel(given, split, where, gate_ref, up_ref, wg_ref, wu_ref, *refs):
    e, count = pl.program_id(1), pl.num_programs(1)
    acc = refs[-1]
    part = nt(gate_ref[0, 0], wg_ref[0]) + nt(up_ref[0, 0], wu_ref[0])

    @pl.when(e == 0)
    def _():
        acc[...] = part + refs[0][...].astype(F32) if given else part

    @pl.when(e > 0)
    def _():
        acc[...] += part

    @pl.when(e == count - 1)
    def _():
        if not split:
            refs[-2][...] = acc[...].astype(BF)
            return
        size = refs[-2].shape[1]
        for out, member in ((refs[-3], where[1]), (refs[-2], 1 - where[1])):
            at = pl.ds(pl.multiple_of(member * size, LANES), size)
            out[...] = acc[:, at].astype(BF)


def expert_hidden(first, member, mid, tree, w_gate, w_up, came, split, deps):
    count, _, rows, hidden = mid.shape
    width = w_gate.shape[1]
    rows //= 2
    tile = 448
    tiles = rows // tile

    def weight(i, e, f):
        return (f[0] + e, 0, 0)

    def row(i, e, f):
        return (i, 0)

    given = [came] if came is not None else []
    specs, deps = after(deps)
    outs = 2 if split else 1
    return pl.pallas_call(
        functools.partial(expert_hidden_kernel, bool(given), split),
        grid_spec=pltpu.PrefetchScalarGridSpec(
            num_scalar_prefetch=1,
            grid=(tiles, count),
            in_specs=[
                pl.BlockSpec((1, 1, tile, hidden), lambda i, e, f: (e, 1, tree * tiles + i, 0)),
                pl.BlockSpec((1, 1, tile, hidden), lambda i, e, f: (e, 2, tree * tiles + i, 0)),
                pl.BlockSpec((1, width, hidden), weight),
                pl.BlockSpec((1, width, hidden), weight),
            ]
            + [pl.BlockSpec((tile, width), row) for _ in given]
            + specs,
            out_specs=[pl.BlockSpec((tile, width // outs), row)] * outs,
            scratch_shapes=[pltpu.VMEM((tile, width), F32)],
        ),
        out_shape=[jax.ShapeDtypeStruct((rows, width // outs), BF)] * outs,
        compiler_params=params(),
        cost_estimate=cost(6 * count * rows * width * hidden, 20),
    )(jnp.stack([first, member]).astype(jnp.int32), mid, mid, w_gate, w_up, *given, *deps)


def expert_mix_kernel(first, mid_ref, wd_ref, *refs):
    e, count = pl.program_id(1), pl.num_programs(1)
    acc = refs[-1]
    part = nn(mid_ref[0, 0], wd_ref[0])

    @pl.when(e == 0)
    def _():
        acc[...] = part

    @pl.when(e > 0)
    def _():
        acc[...] += part

    @pl.when(e == count - 1)
    def _():
        refs[-2][...] = acc[...].astype(BF)


def expert_mix(first, mid, tree, w_down, deps):
    count, _, rows, hidden = mid.shape
    width = w_down.shape[2]
    rows //= 2
    tile = 448
    tiles = rows // tile
    specs, deps = after(deps)
    return pl.pallas_call(
        expert_mix_kernel,
        grid_spec=pltpu.PrefetchScalarGridSpec(
            num_scalar_prefetch=1,
            grid=(tiles, count),
            in_specs=[
                pl.BlockSpec((1, 1, tile, hidden), lambda i, e, f: (e, 0, tree * tiles + i, 0)),
                pl.BlockSpec((1, hidden, width), lambda i, e, f: (f[0] + e, 0, 0)),
            ]
            + specs,
            out_specs=pl.BlockSpec((tile, width), lambda i, e, f: (i, 0)),
            scratch_shapes=[pltpu.VMEM((tile, width), F32)],
        ),
        out_shape=jax.ShapeDtypeStruct((rows, width), BF),
        compiler_params=params(),
        cost_estimate=cost(3 * count * rows * width * hidden, 10),
    )(jnp.reshape(first, (1,)).astype(jnp.int32), mid, w_down, *deps)


def out_grads_kernel(parts, where, *refs):
    branch, out_ref = refs[4 * parts : 4 * parts + 2], refs[-1]
    for own in range(2):

        @pl.when(where[0] == own)
        def _():
            for part in range(parts):
                at = (1 - own) * parts + part
                total = sum(
                    tn(refs[2 * parts * t + at][...], branch[t][...]) for t in range(2)
                )
                size = total.shape[0]
                out_ref[part * size : (part + 1) * size, :] = total.astype(BF)


def out_grads(own, attended, branch):
    parts = len(attended[0]) // 2
    size, columns = attended[0][0].shape[1], branch[0].shape[1]
    return pl.pallas_call(
        functools.partial(out_grads_kernel, parts),
        in_specs=[pl.BlockSpec(memory_space=pltpu.SMEM)]
        + [pl.BlockSpec(memory_space=pltpu.VMEM)] * (4 * parts + 2),
        out_shape=jax.ShapeDtypeStruct((parts * size, columns), BF),
        compiler_params=params(),
        cost_estimate=cost(4 * branch[0].shape[0] * columns * size * parts, 8),
    )(jnp.reshape(own, (1,)).astype(jnp.int32), *attended[0], *attended[1], *branch)


def tie_kernel(*refs):
    pass


def tie(v, deps):
    if not deps:
        return v
    specs, deps = after((v, *deps))
    return pl.pallas_call(
        tie_kernel,
        in_specs=specs,
        out_specs=pl.BlockSpec(memory_space=pl.ANY),
        out_shape=jax.ShapeDtypeStruct(v.shape, v.dtype),
        input_output_aliases={0: 0},
        cost_estimate=cost(0, 0),
    )(*deps)


def norm_back_kernel(
    mine_ref, came_ref, logits_ref, router_ref, middle_ref, inv_ref, gain_ref, *refs
):
    scaled_ref, sums_ref, gain_grad_ref = refs[-3:]
    total = mine_ref[...].astype(F32) + came_ref[...].astype(F32)
    total += nt(logits_ref[...], router_ref[...])
    normed = middle_ref[...] * inv_ref[...]
    scaled = total * gain_ref[...].astype(F32)
    scaled_ref[...] = scaled
    sums_ref[...] = jnp.sum(scaled * normed, axis=-1, keepdims=True)
    gain_grad_ref[...] = jnp.sum(total * normed, axis=0, keepdims=True)


def norm_back(mine, came, logits, router, middle, inv, gain, deps):
    rows, columns = middle.shape
    specs, deps = after(deps)
    return pl.pallas_call(
        norm_back_kernel,
        in_specs=[pl.BlockSpec(memory_space=pltpu.VMEM)] * 7 + specs,
        out_shape=[
            jax.ShapeDtypeStruct((rows, columns), F32),
            jax.ShapeDtypeStruct((rows, 1), F32),
            jax.ShapeDtypeStruct((1, columns), F32),
        ],
        compiler_params=params(),
        cost_estimate=cost(512 * rows * columns, 6),
    )(mine, came, logits, router, middle, inv, gain, *deps)


def branch_kernel(parts, where, grad_ref, scaled_ref, middle_ref, inv_ref, m_ref, c_ref, w_ref, *refs):
    full_ref, low_ref = refs[-2 - 2 * parts : -2 * parts]
    theirs, own = refs[-2 * parts : -parts], refs[-parts:]
    columns = middle_ref.shape[1]
    inv = inv_ref[...]
    mean = (m_ref[...] + c_ref[...]) / (2 * columns)
    at = pl.ds(pl.multiple_of(where[0] * columns, LANES), columns)
    grad = grad_ref[:, at].astype(F32)
    grad += inv * (scaled_ref[...] - middle_ref[...] * inv * mean)
    full_ref[...] = grad
    low = grad.astype(BF)
    low_ref[...] = low
    for outs, member in ((theirs, 1 - where[0]), (own, where[0])):
        for part in range(parts):
            size = outs[part].shape[1]
            rows = pl.ds(pl.multiple_of((member * parts + part) * size, 16), size)
            outs[part][...] = nt(low, w_ref[rows, :]).astype(outs[part].dtype)


def branch_back(member, parts, grad, scaled, middle, inv, sums_mine, sums_came, w_out, deps):
    rows, columns = middle.shape
    size = w_out.shape[0] // (2 * parts)
    specs, deps = after(deps)
    vmem = pl.BlockSpec(memory_space=pltpu.VMEM)
    first = pl.BlockSpec((rows, grad.shape[1]), lambda i: (0, 0))
    outs = [
        jax.ShapeDtypeStruct((rows, columns), F32),
        jax.ShapeDtypeStruct((rows, columns), BF),
        *[jax.ShapeDtypeStruct((rows, size), BF)] * parts,
        *[jax.ShapeDtypeStruct((rows, size), F32)] * parts,
    ]
    return pl.pallas_call(
        functools.partial(branch_kernel, parts),
        grid=(1,),
        in_specs=[pl.BlockSpec(memory_space=pltpu.SMEM), first] + [vmem] * 6 + specs,
        out_specs=[pl.BlockSpec(o.shape, lambda i: (0, 0)) for o in outs],
        out_shape=outs,
        compiler_params=params(),
        cost_estimate=cost(2 * rows * columns * w_out.shape[0], 10),
    )(
        jnp.reshape(member, (1,)),
        grad, scaled, middle, inv, sums_mine, sums_came, w_out, *deps,
    )


def finish_kernel(layout, where, *refs):
    outs, last = refs[2:-1], refs[-1]
    for g in range(2):
        for out, to, start, size in layout[g]:
            at = slice(start, start + size)
            v = jnp.where(where[0] == g, refs[0][:, at], refs[1][:, at])
            outs[out][:, to : to + size] = v.astype(F32)
    start = refs[0].shape[1] - last.shape[2]
    last[where[0]] = refs[0][:, start:].astype(F32)
    last[1 - where[0]] = refs[1][:, start:].astype(F32)


def finish(core, mine, other, layout, widths, out_width):
    rows, columns = mine.shape
    tile = rows // 4

    def row(i, w):
        return (i, 0)

    return pl.pallas_call(
        functools.partial(finish_kernel, layout),
        grid_spec=pltpu.PrefetchScalarGridSpec(
            num_scalar_prefetch=1,
            grid=(4,),
            in_specs=[pl.BlockSpec((tile, columns), row)] * 2,
            out_specs=[pl.BlockSpec((tile, w), row) for w in widths]
            + [pl.BlockSpec((2, tile, out_width), lambda i, w: (0, i, 0))],
        ),
        out_shape=[jax.ShapeDtypeStruct((rows, w), F32) for w in widths]
        + [jax.ShapeDtypeStruct((2, rows, out_width), F32)],
        compiler_params=params(),
        cost_estimate=cost(0, 12),
    )(jnp.reshape(core, (1,)).astype(jnp.int32), mine, other)


def finish_experts_kernel(per_core, half, where, *refs):
    mine, came, outs = refs[:per_core], refs[per_core : 2 * per_core], refs[2 * per_core :]
    rows = pl.ds(pl.multiple_of(where[0] * half, 16), half)
    for j in range(per_core):
        for source, at in ((mine, where[0] * per_core + j), ((came), (1 - where[0]) * per_core + j)):
            v = source[j][:, rows, :].astype(F32)
            outs[0][at] = v[0]
            outs[1][at] = v[1]
            outs[2][at] = v[2]


def finish_experts(core, mine, came):
    per_core = len(mine)
    _, rows, hidden = mine[0].shape
    half = rows // 2
    whole = pl.BlockSpec(memory_space=pltpu.VMEM)
    return pl.pallas_call(
        functools.partial(finish_experts_kernel, per_core, half),
        in_specs=[pl.BlockSpec(memory_space=pltpu.SMEM)] + [whole] * (2 * per_core),
        out_shape=[
            jax.ShapeDtypeStruct((2 * per_core, half, hidden), F32),
            jax.ShapeDtypeStruct((2 * per_core, half, hidden), F32),
            jax.ShapeDtypeStruct((2 * per_core, half, hidden), F32),
        ],
        compiler_params=params(),
        cost_estimate=cost(0, 10),
    )(jnp.reshape(core, (1,)), *mine, *came)


def local(
    tokens,
    norm_gain,
    w_query,
    key_weight,
    value_weight,
    w_out,
    ffn_gain,
    w_router,
    w_gate,
    w_up,
    w_down,
    parents,
    routes,
    cotangent,
):
    me = Mesh()
    paired = me.groups == 2
    tok_rows, width = tokens.shape
    tree_len = tok_rows * me.groups
    seg_len = tree_len // 16
    columns = width // me.groups
    all_q, all_k = w_query.shape[1], key_weight.shape[1]
    q_width, k_width = all_q // me.groups, all_k // me.groups
    kv_heads = k_width // HEAD_DIM
    parts = kv_heads // 2 if kv_heads % 2 == 0 else 1
    q_part, k_part = q_width // parts, k_width // parts
    gq, gk = q_part // HEAD_DIM, k_part // HEAD_DIM
    q_room, k_room = pairs(gq) * LANES, pairs(gk) * LANES
    lanes = q_room + 2 * k_room
    experts = w_gate.shape[0] * me.groups
    per_core = w_gate.shape[0] // 2
    partner = 1 - me.member

    def heads_of(member):
        found = []
        for weight, size, room in (
            (w_query, q_width, q_room),
            (key_weight, k_width, k_room),
            (value_weight, k_width, k_room),
        ):
            block = lax.dynamic_slice_in_dim(weight, member * size, size, 1)
            found.append(jnp.pad(block, ((0, 0), (0, room - size))))
        return jnp.concatenate(found, 1)

    projections = (w_query, key_weight, value_weight)
    gain_row = norm_gain[None]
    own, came = [], []
    along = jnp.split(cotangent, 2, 0)
    grad_came = []
    if paired:
        hot = jnp.any(
            routes.T[:, None, :] == jnp.arange(experts, dtype=jnp.int32)[None, :, None], axis=0
        )
        packet = jnp.concatenate(
            [
                w_router.T,
                jnp.pad(ffn_gain[None], ((0, 15), (0, 0))),
                jnp.pad(hot.astype(BF), ((0, 0), (0, columns - tok_rows))),
            ],
            0,
        )
        x_theirs, x_mine, packet_sent, gone = split(me.member, tokens, packet, along[0])
        x_came = me.swap_shard(x_theirs)
        grad_came.append(me.swap_shard(gone))
        packets = [packet_sent, me.swap_shard(packet_sent)]
        *theirs, hidden_first, x_columns, inv_one = project_theirs(
            me.member, parts, x_mine, x_came, gain_row, projections
        )
        came = [me.swap_shard(v) for v in theirs]
        own = project_own(me.member, parts, hidden_first, projections, (theirs[-1],))
    else:
        every_head = jnp.concatenate([heads_of(j) for j in range(me.groups)], 1)
        own_rows = tokens.astype(F32)
        inv_rows = lax.rsqrt(jnp.mean(own_rows * own_rows, axis=-1, keepdims=True) + EPS)
        x_columns = me.exchange(tokens, 1, 0)
        inv_one = me.gather(inv_rows, 0)
        hidden_first = (x_columns.astype(F32) * inv_one * norm_gain.astype(F32)).astype(BF)
        own.append(me.scatter(nn(hidden_first, every_head), 1))
        came.append(jnp.zeros(own[-1].shape, BF))

    gain_two = ffn_gain.astype(F32)

    index = jnp.arange(tree_len, dtype=jnp.int32)
    _, depth = tree_layout(index, seg_len)
    cos, sin = angle_tables(depth)
    visible = tree_mask(index, index, parents[0], seg_len)
    bias = jnp.where(visible, 0.0, -1e30).astype(F32)

    attended, lse, query, key, value, att_came = [], [], [], [], [], []
    for part in range(parts):
        a, b, c, d, e, f = attend(
            own[part], came[part], cos, sin, bias, along[1] if part == parts - 1 else cos, gq, gk
        )
        attended.append(a)
        lse.append(b)
        query.append(c)
        key.append(d)
        value.append(e)
        if paired:
            att_came.append(me.swap_shard(a))
    if paired:
        grad_came.append(me.swap_shard(f))
        mine = [cotangent, me.swap_core(cotangent)]
        others = [*grad_came, *(me.swap_core(v) for v in grad_came)]
        grad_all = jnp.where(
            me.member == 0,
            jnp.concatenate([mine[0], *others[:2], mine[1], *others[2:]], 0),
            jnp.concatenate([*others[:2], mine[0], *others[2:], mine[1]], 0),
        )
        starts = [
            member * q_width + part * q_part
            for member in (me.member, partner)
            for part in range(parts)
        ]
        middle, middle_low, squares = middle_of(
            attended + att_came, jnp.stack(starts).astype(jnp.int32), w_out, x_columns, True
        )
        attended_full = me.in_order(
            me.member, jnp.concatenate(attended, 1), jnp.concatenate(att_came, 1), 1
        )
        messages = [middle_low, me.swap_shard(middle_low)]
        hidden_all, gates_all, inv_two = hidden_packed(
            me.member,
            [
                (*messages, *packets),
                (*(me.swap_core(v) for v in messages), *(me.swap_core(v) for v in packets)),
            ],
        )
    else:
        grad_tree = me.gather(cotangent, 0)
        grad_all = jnp.concatenate([grad_tree, me.swap_core(grad_tree)], 0)
        attended_full = me.gather(attended[0][:, :q_width], 1)
        where = jnp.zeros((1,), jnp.int32)
        middle, middle_low, squares = middle_of([attended_full], where, w_out, x_columns, False)
        route_hot = jnp.any(
            routes[:, :, None] == jnp.arange(experts, dtype=jnp.int32)[None, None, :], axis=1
        ).astype(F32)
        routed = me.gather(route_hot, 0)
        middle_low, squares = me.gather(middle_low, 1), me.total(squares)
        hidden_all, gates_all = hidden_of(
            [
                ([middle_low], [squares], routed),
                (
                    [me.swap_core(middle_low)],
                    [me.swap_core(squares)],
                    me.swap_core(routed),
                ),
            ],
            where,
            me.gather(ffn_gain, 0)[None],
            me.gather(w_router, 0),
        )
        inv_two = lax.rsqrt(squares / width + EPS)
    grad_tree = grad_all[:tree_len]
    gates = gates_all[0]
    hidden_all = hidden_all.reshape(2 * tree_len, width)
    gates_all = gates_all.reshape(2 * tree_len, experts)
    normed_two = middle * inv_two
    hidden_own = (normed_two * gain_two).astype(BF)

    first = me.core * per_core
    chunk = width // me.chips
    def gates_grad(own_columns):
        grad = me.total(own_columns[:tree_len] + me.swap_core(own_columns[tree_len:]))
        return (gates * (grad - jnp.sum(gates * grad, axis=-1, keepdims=True))).astype(BF)

    def output_of(mixed_own, mixed_other, *deps):
        mixed = mixed_own.astype(F32) + me.swap_core(mixed_other).astype(F32)
        placed = lax.dynamic_update_slice_in_dim(
            jnp.zeros((tree_len, width), F32), middle, me.member * columns, 1
        )
        return me.scatter(tie((mixed + placed).astype(BF), deps), 0).astype(BF)

    def input_of(grad_middle, scaled, row_sums):
        normed = x_columns.astype(F32) * inv_one
        grad = grad_middle + inv_one * (scaled - normed * (me.total(row_sums) / width))
        return me.exchange(grad.astype(BF), 0, 1)

    flipped = bias.T
    if not paired:
        before, rings = None, []
        for j in range(per_core):
            before = expert_grads(
                j, per_core, first + j, me.member * (2 * per_core) + first + j,
                hidden_all, grad_all, gates_all, w_gate, w_up, w_down, before, 0, 1, (),
            )
            mid, own_columns, grads = before
            ring = Scatter(me, lambda chip: lax.dynamic_slice_in_dim(grads, chip * chunk, chunk, 1))
            for _ in range(me.chips - 1):
                ring.start()
                ring.finish()
            rings.append(ring.held)
        grad_logits = gates_grad(own_columns)
        (grad_other,) = expert_hidden(first, me.member, mid, 1, w_gate, w_up, None, False, ())
        (grad_own,) = expert_hidden(
            first, me.member, mid, 0, w_gate, w_up, me.swap_core(grad_other), False, ()
        )
        mixed_other = expert_mix(first, mid, 1, w_down, ())
        mixed_own = expert_mix(first, mid, 0, w_down, ())
        result = output_of(mixed_own, mixed_other)
        grad_hidden_two = nt(grad_logits, w_router) + me.scatter(grad_own, 1)
        grad_gain_two = jnp.sum(grad_hidden_two * normed_two, axis=0)[None]
        scaled = grad_hidden_two * gain_two
        mean = me.total(jnp.sum(scaled * normed_two, axis=-1, keepdims=True)) / width
        grad_columns = me.part(grad_tree, 1, me.member).astype(F32)
        grad_middle = grad_columns + inv_two * (scaled - normed_two * mean)
        grad_branch = grad_middle.astype(BF)
        own = me.scatter(nt(grad_branch, w_out), 1)
        own = jnp.pad(own, ((0, 0), (0, q_room - q_width)))
        grad_heads = attend_back(
            own, jnp.zeros(own.shape, BF), query[0], key[0], value[0], lse[0],
            cos, sin, flipped, gq, gk, (),
        )
        grad_out = me.all_reduce(tn(attended_full, grad_branch))
        grad_full = me.gather(grad_heads, 1)
        every = me.all_reduce(tn(hidden_first, grad_full))
        every = every.reshape(columns, me.groups, lanes)
        grad_query, grad_key, grad_value = (
            every[:, :, start : start + size].reshape(columns, me.groups * size)
            for start, size in ((0, q_width), (q_room, k_width), (q_room + k_room, k_width))
        )
        grad_hidden_one = nt(grad_full, every_head)
        normed_one = x_columns.astype(F32) * inv_one
        grad_gain_one = jnp.sum(grad_hidden_one * normed_one, axis=0)[None]
        scaled = grad_hidden_one * norm_gain.astype(F32)
        row_sums = jnp.sum(scaled * normed_one, axis=-1, keepdims=True)
        input_grad = input_of(grad_middle, scaled, row_sums)
        grad_router = tn(hidden_own, grad_logits)
        small = me.butterfly(jnp.concatenate([grad_gain_one, grad_gain_two, grad_router.T], 0))
        sums = rings
        grad_gate, grad_up, grad_down = finish_experts(
            me.core, sums, [me.swap_core(v) for v in sums]
        )
    else:

        def expert(j, before, deps):
            return expert_grads(
                j, per_core, first + j, me.member * (2 * per_core) + first + j,
                hidden_all, grad_all, gates_all, w_gate, w_up, w_down, before, j % 2, 2, deps,
            )

        def ring_of(grads):
            return Scatter(me, lambda chip: lax.dynamic_slice_in_dim(grads, chip * chunk, chunk, 1))

        one = expert(1, expert(0, None, ()), ())
        ring_a = ring_of(one[2])
        ring_a.start()
        two = expert(2, one, ())
        a = ring_a.finish()
        ring_a.start(two[1])
        mid, own_columns, grads = expert(3, two, (a,))
        ring_b = ring_of(grads)
        a = ring_a.finish()
        ring_a.start(own_columns)
        ring_b.start()
        grad_logits = gates_grad(own_columns)
        (grad_other,) = expert_hidden(first, me.member, mid, 1, w_gate, w_up, None, False, (a,))
        a, b = ring_a.finish(), ring_b.finish()
        ring_a.start(grad_other)
        ring_b.start(grad_other)
        grad_mine, grad_theirs = expert_hidden(
            first, me.member, mid, 0, w_gate, w_up, me.swap_core(grad_other), True, (a, b)
        )
        hidden_came = me.swap_shard(grad_theirs)
        a, b = ring_a.finish(), ring_b.finish()
        ring_a.start(grad_mine)
        ring_b.start(grad_mine)
        mixed_other = expert_mix(first, mid, 1, w_down, (grad_mine, a, b))
        mixed_own = expert_mix(first, mid, 0, w_down, (mixed_other, grad_logits))
        scaled, row_sums, grad_gain_two = norm_back(
            grad_mine, hidden_came, grad_logits, w_router, middle, inv_two, ffn_gain[None],
            (mixed_own,),
        )
        sums_came = me.swap_shard(row_sums)
        a = ring_a.finish()
        ring_a.start(scaled)
        grad_middle, grad_branch, *both = branch_back(
            me.member, parts, grad_all, scaled, middle, inv_two, row_sums, sums_came, w_out, (a,)
        )
        came = [me.swap_shard(v) for v in both[:parts]]
        own = both[parts:]
        b = ring_b.finish()
        ring_b.start(grad_branch)
        grad_out = out_grads(
            me.core == me.member,
            [attended + att_came, [me.swap_core(v) for v in attended + att_came]],
            [grad_branch, me.swap_core(grad_branch)],
        )
        a = ring_a.finish()
        ring_a.start(grad_out)
        heads_a = attend_back(
            own[0], came[0], query[0], key[0], value[0], lse[0], cos, sin, flipped, gq, gk,
            (b, a, grad_out),
        )
        back_a = me.swap_shard(heads_a)
        b = ring_b.finish()
        ring_b.start(heads_a)
        heads_b = attend_back(
            own[1], came[1], query[1], key[1], value[1], lse[1], cos, sin, flipped, gq, gk,
            (b, heads_a),
        )
        back_b = me.swap_shard(heads_b)
        a = ring_a.finish()
        grad_pairs = [(heads_a, back_a), (heads_b, back_b)]
        grads_mine = weight_grads(
            me.member,
            me.core,
            (hidden_first, me.swap_core(hidden_first)),
            (grad_pairs, [tuple(me.swap_core(v) for v in pair) for pair in grad_pairs]),
            grad_out,
            (a,),
        )
        head_chunk = grads_mine.shape[0] // me.chips
        ring_w = Scatter(
            me, lambda chip: lax.dynamic_slice_in_dim(grads_mine, chip * head_chunk, head_chunk, 0)
        )
        ring_w.start()
        grad_router = tn(hidden_own, grad_logits)
        beside = {}
        hops = me.chips - 1
        for hop in range(1, 2 * hops):
            w = ring_w.finish()
            if hop == hops:
                ring_w = Gather(me, ring_w.held)
            if hop == 4:
                result = output_of(mixed_own, mixed_other, w)
                beside[12] = (result,)
            if hop == hops:
                scaled, row_sums, grad_gain_one = project_back(
                    me.member, x_columns, inv_one, gain_row, projections, grad_pairs, (w,)
                )
                input_grad = input_of(grad_middle, scaled, row_sums)
                small = me.butterfly(
                    jnp.concatenate([grad_gain_one, grad_gain_two, grad_router.T], 0)
                )
                beside[hop + 1] = (scaled,)
                beside[hop + 4] = (small,)
                beside[hop + 6] = (input_grad,)
            deps = beside.get(hop, ())
            if hop in (1, 3, 5) and ring_b.hops < hops:
                deps = (*deps, ring_b.finish())
                if ring_b.hops < hops:
                    ring_b.start(w)
                else:
                    sums = [h for r in (ring_a, ring_b) for h in jnp.split(r.held, 2, 0)]
                    experts_done = finish_experts(me.core, sums, [me.swap_core(v) for v in sums])
                    beside[hop + 5] = (*beside.get(hop + 5, ()), experts_done[0])
            ring_w.start(*deps)
        ring_w.finish()
        grad_gate, grad_up, grad_down = experts_done
        layout = [
            [
                (out, j * step + part * size, j * lanes + start, size)
                for j in range(2)
                for out, step, start, size in (
                    (0, q_width, 0, q_part),
                    (1, k_width, q_room, k_part),
                    (2, k_width, q_room + k_room, k_part),
                )
            ]
            for part in range(parts)
        ]
        grad_query, grad_key, grad_value, grad_out = finish(
            me.core, ring_w.whole, me.swap_core(ring_w.whole), layout, (all_q, all_k, all_k), columns
        )
        grad_out = grad_out.reshape(-1, columns)

    return (
        result,
        input_grad,
        small[0],
        grad_query,
        grad_key,
        grad_value,
        grad_out,
        small[1],
        small[2:].T,
        grad_gate,
        grad_up,
        grad_down.transpose(0, 2, 1),
    )


def solution(mesh):
    return jax.shard_map(
        local,
        mesh=mesh,
        in_specs=(
            P(("rep", "shard"), None),
            P("shard"),
            P("shard", None),
            P("shard", None),
            P("shard", None),
            P(None, "shard"),
            P("shard"),
            P("shard", None),
            P("shard", None, None),
            P("shard", None, None),
            P("shard", None, None),
            P("rep", None),
            P(("rep", "shard"), None),
            P(("rep", "shard"), None),
        ),
        out_specs=(
            P(("rep", "shard"), None),
            P(("rep", "shard"), None),
            P("shard"),
            P("shard", None),
            P("shard", None),
            P("shard", None),
            P(None, "shard"),
            P("shard"),
            P("shard", None),
            P("shard", "rep", None),
            P("shard", "rep", None),
            P("shard", None, "rep"),
        ),
        check_vma=False,
    )
```

time: 608 us -> 547 us (0.90)
  waiting for transfers between devices: 223 us -> 142 us
  Pallas kernels: 127 us -> 204 us
  starting transfers between devices: 93.4 us -> 66.8 us
  matrix products: 23.3 us -> 0.93 us
  local copies, waits for them, and re-layouts: 45.7 us -> 39.4 us
    pallas_call x6 -> x41, Pallas kernels: 100 us -> 174 us  [the longest x4 68 us: expert_grads(): pl.pallas_call(functools.partial(expert_grads_kernel, chained, steps), gr...]
    ppermute x56 -> x28, waiting for transfers between devices: 130 us -> 71.4 us  [along_ring(): return lax.ppermute(v, 'rep', self.ring)]
    ppermute x56 -> x28, starting transfers between devices: 71.1 us -> 33 us  [along_ring(): return lax.ppermute(v, 'rep', self.ring)]
    dot_general x10 -> x1, matrix products: 23.3 us -> 0.93 us  [dot(): return lax.dot_general(a, b, (dims, ((), ())), preferred_element_type=F32)]
    ppermute x17 -> x19, waiting for transfers between devices: 80.2 us -> 59.4 us  [swap_shard(): return lax.ppermute(v, 'shard', [(0, 1), (1, 0)])]
    concatenate x4 -> x2, local copies, waits for them, and re-layouts: 11.4 us -> 2.08 us  [the longest x1 2.05 us: local(): jnp.concatenate([*others[:2], mine[0], *others[2:], mine[1]], 0)]
    unnamed x74 -> x117, local copies, waits for them, and re-layouts: 10.9 us -> 19.3 us
    ppermute x17 -> x19, starting transfers between devices: 19 us -> 26.5 us  [swap_shard(): return lax.ppermute(v, 'shard', [(0, 1), (1, 0)])]
  transfers between devices with their start and end apart: 88 -> 76, of which waited for: 50 -> 31; matrix products, arithmetic and copies ran while one was open for 17% -> 19% of each run, Pallas kernels for 2% -> 29%
where the time goes in v3:
time: 547 us; the launch traced here: 537 us
  Pallas kernels  204 us (37%)
  waiting for transfers between devices  142 us (26%)
  other arithmetic  81.7 us (15%)
  starting transfers between devices  66.8 us (12%)
  local copies, waits for them, and re-layouts  39.4 us (7%)
    ppermute x28, waiting for transfers between devices, along_ring(): return lax.ppermute(v, 'rep', self.ring)  71.4 us
    pallas_call x4, Pallas kernels, expert_grads(): pl.pallas_call(functools.partial(expert_grads_kernel, chained, steps), gr...  68 us
    ppermute x19, waiting for transfers between devices, swap_shard(): return lax.ppermute(v, 'shard', [(0, 1), (1, 0)])  59.4 us
    convert_element_type x20, other arithmetic, finish(): self.held = (self.came.astype(F32) + mine.astype(F32)).astype(BF)  50.9 us
    ppermute x28, starting transfers between devices, along_ring(): return lax.ppermute(v, 'rep', self.ring)  33 us
    ppermute x19, starting transfers between devices, swap_shard(): return lax.ppermute(v, 'shard', [(0, 1), (1, 0)])  26.5 us
    pallas_call x2, Pallas kernels, expert_hidden(): pl.pallas_call(functools.partial(expert_hidden_kernel, bool(given), split...  24.7 us
    unnamed x117, local copies, waits for them, and re-layouts  19.3 us
  transfers between devices with their start and end apart: 76, of which 31 were waited for; matrix products, arithmetic and copies ran while one was open for 19% of the time, Pallas kernels for 29%

profile of v3, /device:TPU:0, one launch (start us, length us, event | category | flops | bytes accessed | tf_op | source)
XLA Modules:
  0.0 536.8 jit_solution(12762289078717629418)
XLA Ops:
  36.5 6.2 %collective-permute-done.2.came_ref = bf16[448,640]{1,0:T(8,128)(2,1)S(1)} collective-permute-done((bf16[448,640]{1,0:T(8,128)(2,1)}, bf16[448,640]{1,0:T(8,128)(2,1)S(1)}, u32[]{:S(2)}, u32[]{:S(2)}) %collective-permute-start.2) | collective-permute-done | bytes 573472 | tf_op jit(solution)/shard_map/ppermute | solution.py:102
  43.5 7.0 %shard_map.233 = (bf16[448,384]{1,0:T(8,128)(2,1)}, f32[448,128]{1,0:T(8,128)}, bf16[448,384]{1,0:T(8,128)(2,1)}, bf16[2,2,448,128]{3,2,1,0:T(8,128)(2,1)}, bf16...) custom-call(f32[448,640]{1,0:T(8,128)} %get-tuple-element.79.own_ref, bf16[448,640]{1,0:T(8,128)(2,1)} %copy-done.52, ...), custom_call_target="tpu_custom_call" | custom-call | flops 1445068800 | bytes 8388608 | tf_op jit(solution)/shard_map/pallas_call | solution.py:282
  55.8 7.0 %shard_map.232 = (bf16[448,384]{1,0:T(8,128)(2,1)}, f32[448,128]{1,0:T(8,128)}, bf16[448,384]{1,0:T(8,128)(2,1)}, bf16[2,2,448,128]{3,2,1,0:T(8,128)(2,1)}, bf16...) custom-call(f32[448,640]{1,0:T(8,128)} %get-tuple-element.76.own_ref, bf16[448,640]{1,0:T(8,128)(2,1)} %copy-done.51, ...), custom_call_target="tpu_custom_call" | custom-call | flops 1445068800 | bytes 8388608 | tf_op jit(solution)/shard_map/pallas_call | solution.py:282
  78.6 5.9 %shard_map.234 = (f32[448,768]{1,0:T(8,128)}, bf16[464,768]{1,0:T(8,128)(2,1)}, f32[448,1]{1,0:T(8,128)}) custom-call(s32[4]{0:T(128)} %pad_add_fusion.1.where, bf16[448,384]{1,0:T(8,128)(2,1)} %get-tuple-element.78.refs_0_, bf16[448,384]{1,0:T(8,128)(2,1)} %get-tuple-element.80.refs_1_, bf16[448,384]{1,0:T(8,128)(2,1)} %collective-permute-done.3.refs_2_, ...), custom_call_target="tpu_custom_call" | custom-call | flops 1056964608 | bytes 6291456 | tf_op jit(solution)/shard_map/pallas_call | solution.py:615
  89.9 13.2 %collective-permute-done.5.refs_1_ = bf16[464,768]{1,0:T(8,128)(2,1)S(1)} collective-permute-done((bf16[464,768]{1,0:T(8,128)(2,1)}, bf16[464,768]{1,0:T(8,128)(2,1)S(1)}, u32[]{:S(2)}, u32[]{:S(2)}) %collective-permute-start.5) | collective-permute-done | bytes 712736 | tf_op jit(solution)/shard_map/ppermute | solution.py:102
  111.2 17.2 %shard_map.236 = (bf16[4,3,896,512]{3,2,1,0:T(8,128)(2,1)}, f32[896,16]{1,0:T(8,128)}, bf16[6,1536,512]{2,1,0:T(8,128)(2,1)}) custom-call(s32[2]{0:T(128)} %pad_add_fusion.4.where, bf16[896,1536]{1,0:T(8,128)(2,1)} %bitcast.32, bf16[896,1536]{1,0:T(8,128)(2,1)} %broadcast_select_fusion.g_ref.grad_ref, f32[896,16]{1,0:T(8,128)} %bitcast.36, ...), custom_call_target="tpu_custom_call" | custom-call | flops 11274289152 | bytes 20971520 | tf_op jit(solution)/shard_map/pallas_call | solution.py:813
  128.5 16.9 %shard_map.237 = (bf16[4,3,896,512]{3,2,1,0:T(8,128)(2,1)}, f32[896,16]{1,0:T(8,128)}, bf16[6,1536,512]{2,1,0:T(8,128)(2,1)}) custom-call(s32[2]{0:T(128)} %get-tuple-element.158.where, bf16[896,1536]{1,0:T(8,128)(2,1)} %bitcast.33, bf16[896,1536]{1,0:T(8,128)(2,1)} %broadcast_select_fusion.g_ref.grad_ref, ...), custom_call_target="tpu_custom_call", output_to_operand_aliasing={{0}: (8, {}), {2}: (9, {})} | custom-call | flops 11274289152 | bytes 20971520 | tf_op jit(solution)/shard_map/pallas_call | solution.py:813
  149.8 16.9 %shard_map.238 = (bf16[4,3,896,512]{3,2,1,0:T(8,128)(2,1)}, f32[896,16]{1,0:T(8,128)}, bf16[6,1536,512]{2,1,0:T(8,128)(2,1)}) custom-call(s32[2]{0:T(128)} %get-tuple-element.157.where, bf16[896,1536]{1,0:T(8,128)(2,1)} %bitcast.34, bf16[896,1536]{1,0:T(8,128)(2,1)} %broadcast_select_fusion.g_ref.grad_ref, ...), custom_call_target="tpu_custom_call", output_to_operand_aliasing={{0}: (8, {})} | custom-call | flops 11274289152 | bytes 20971520 | tf_op jit(solution)/shard_map/pallas_call | solution.py:813
  171.6 16.9 %shard_map.239 = (bf16[4,3,896,512]{3,2,1,0:T(8,128)(2,1)}, f32[896,16]{1,0:T(8,128)}, bf16[6,1536,512]{2,1,0:T(8,128)(2,1)}) custom-call(s32[2]{0:T(128)} %pad_add_fusion.where, bf16[896,1536]{1,0:T(8,128)(2,1)} %bitcast.35, bf16[896,1536]{1,0:T(8,128)(2,1)} %broadcast_select_fusion.g_ref.grad_ref, ...), custom_call_target="tpu_custom_call", output_to_operand_aliasing={{0}: (8, {}), {2}: (9, {})} | custom-call | flops 11274289152 | bytes 20971520 | tf_op jit(solution)/shard_map/pallas_call | solution.py:813
  197.0 12.0 %shard_map.241.refs_1_ = bf16[448,1536]{1,0:T(8,128)(2,1)} custom-call(s32[2]{0:T(128)} %pad_add_fusion.5.where, bf16[4,3,896,512]{3,2,1,0:T(8,128)(2,1)} %get-tuple-element.97.gate_ref.up_ref.mid_ref, bf16[4,3,896,512]{3,2,1,0:T(8,128)(2,1)} %get-tuple-element.97.gate_ref.up_ref.mid_ref, bf16[8,1536,512]{2,1,0:T(8,128)(2,1)} %wg_ref.11, ...), custom_call_target="tpu_custom_call" | custom-call | flops 8455716864 | bytes 20971520 | tf_op jit(solution)/shard_map/pallas_call | solution.py:891
  229.6 12.7 %shard_map.243 = (bf16[448,768]{1,0:T(8,128)(2,1)}, bf16[448,768]{1,0:T(8,128)(2,1)}) custom-call(s32[2]{0:T(128)} %pad_add_fusion.5.where, bf16[4,3,896,512]{3,2,1,0:T(8,128)(2,1)} %get-tuple-element.97.gate_ref.up_ref.mid_ref, bf16[4,3,896,512]{3,2,1,0:T(8,128)(2,1)} %get-tuple-element.97.gate_ref.up_ref.mid_ref, bf16[8,1536,512]{2,1,0:T(8,128)(2,1)} %wg_ref.11, ...), custom_call_target="tpu_custom_call" | custom-call | flops 8455716864 | bytes 20971520 | tf_op jit(solution)/shard_map/pallas_call | solution.py:891
  259.9 7.7 %shard_map.246.refs_0_ = bf16[448,1536]{1,0:T(8,128)(2,1)} custom-call(s32[1]{0:T(128)} %bitcast.first, bf16[4,3,896,512]{3,2,1,0:T(8,128)(2,1)} %get-tuple-element.97.gate_ref.up_ref.mid_ref, bf16[8,512,1536]{2,1,0:T(8,128)(2,1)} %wd_ref.11, bf16[448,768]{1,0:T(8,128)(2,1)} %get-tuple-element.100.refs_0_.mine_ref.refs_1_, ...), custom_call_target="tpu_custom_call" | custom-call | flops 4227858432 | bytes 10485760 | tf_op jit(solution)/shard_map/pallas_call | solution.py:938
  267.6 7.7 %shard_map.247.refs_0_ = bf16[448,1536]{1,0:T(8,128)(2,1)} custom-call(s32[1]{0:T(128)} %bitcast.first, bf16[4,3,896,512]{3,2,1,0:T(8,128)(2,1)} %get-tuple-element.97.gate_ref.up_ref.mid_ref, bf16[8,512,1536]{2,1,0:T(8,128)(2,1)} %wd_ref.11, bf16[448,1536]{1,0:T(8,128)(2,1)} %shard_map.246.refs_0_, bf16[448,16]{1,0:T(8,128)(2,1)} %fusion.8.refs_1_.logits_ref), custom_call_target="tpu_custom_call" | custom-call | flops 4227858432 | bytes 10485760 | tf_op jit(solution)/shard_map/pallas_call | solution.py:938
  291.2 5.9 %shard_map.250 = (f32[448,768]{1,0:T(8,128)}, bf16[448,768]{1,0:T(8,128)(2,1)}, bf16[448,384]{1,0:T(8,128)(2,1)}, bf16[448,384]{1,0:T(8,128)(2,1)}, f32[448,384]{1,0:T(8,128)}, /*index=5*/f32[448,384]{1,0:T(8,128)}) custom-call(s32[1]{0:T(128)} %bitcast.3.where, bf16[896,1536]{1,0:T(8,128)(2,1)} %broadcast_select_fusion.g_ref.grad_ref, ...), custom_call_target="tpu_custom_call" | custom-call | flops 1056964608 | bytes 10485760 | tf_op jit(solution)/shard_map/pallas_call | solution.py:1063
  315.1 8.2 %shard_map.254.refs_1_.refs_2_.refs_0_ = bf16[448,640]{1,0:T(8,128)(2,1)} custom-call(f32[448,384]{1,0:T(8,128)} %get-tuple-element.106.own_ref, bf16[448,384]{1,0:T(8,128)(2,1)} %copy-done.38, bf16[448,384]{1,0:T(8,128)(2,1)} %get-tuple-element.108.q_ref, bf16[2,2,448,128]{3,2,1,0:T(8,128)(2,1)} %get-tuple-element.109.k_ref, ...), custom_call_target="tpu_custom_call" | custom-call | flops 1926758400 | bytes 8388608 | tf_op jit(solution)/shard_map/pallas_call | solution.py:369
  327.3 8.2 %shard_map.256.refs_4_.refs_2_ = bf16[448,640]{1,0:T(8,128)(2,1)} custom-call(f32[448,384]{1,0:T(8,128)} %get-tuple-element.113.own_ref, bf16[448,384]{1,0:T(8,128)(2,1)} %collective-permute-done.39.came_ref, bf16[448,384]{1,0:T(8,128)(2,1)} %get-tuple-element.115.q_ref, bf16[2,2,448,128]{3,2,1,0:T(8,128)(2,1)} %get-tuple-element.116.k_ref, ...), custom_call_target="tpu_custom_call" | custom-call | flops 1926758400 | bytes 8388608 | tf_op jit(solution)/shard_map/pallas_call | solution.py:369
  338.1 11.3 %collective-permute-done.41.refs_5_.refs_3_ = bf16[448,640]{1,0:T(8,128)(2,1)S(1)} collective-permute-done((bf16[448,640]{1,0:T(8,128)(2,1)}, bf16[448,640]{1,0:T(8,128)(2,1)S(1)}, u32[]{:S(2)}, u32[]{:S(2)}) %collective-permute-start.41) | collective-permute-done | bytes 573472 | tf_op jit(solution)/shard_map/ppermute | solution.py:102
  355.5 7.7 %shard_map.258 = bf16[768,2048]{1,0:T(8,128)(2,1)} custom-call(s32[2]{0:T(128)} %pad_add_fusion.6.where, bf16[448,768]{1,0:T(8,128)(2,1)} %get-tuple-element.74.hidden_ref.refs_0_, bf16[448,768]{1,0:T(8,128)(2,1)} %collective-permute-done.26.refs_1_, bf16[448,640]{1,0:T(8,128)(2,1)} %shard_map.254.refs_1_.refs_2_.refs_0_, bf16[448,640]{1,0:T(8,128)(2,1)} %copy-done.18, ...), custom_call_target="tpu_custom_call" | custom-call | flops 1761607680 | bytes 8388608 | tf_op jit(solution)/shard_map/pallas_call | solution.py:581
  365.2 8.6 %collective-permute-done.47.refs_1_ = bf16[96,2048]{1,0:T(8,128)(2,1)S(1)} collective-permute-done((bf16[96,2048]{1,0:T(8,128)(2,1)S(1)}, bf16[96,2048]{1,0:T(8,128)(2,1)S(1)}, u32[]{:S(2)}, u32[]{:S(2)}) %collective-permute-start.47) | collective-permute-done | bytes 393248 | tf_op jit(solution)/shard_map/ppermute | solution.py:108
  387.3 14.5 %collective-permute-done.50.refs_1_ = bf16[96,2048]{1,0:T(8,128)(2,1)S(1)} collective-permute-done((bf16[96,2048]{1,0:T(8,128)(2,1)S(1)}, bf16[96,2048]{1,0:T(8,128)(2,1)S(1)}, u32[]{:S(2)}, u32[]{:S(2)}) %collective-permute-start.50) | collective-permute-done | bytes 393248 | tf_op jit(solution)/shard_map/ppermute | solution.py:108
  417.1 12.6 %collective-permute-done.54 = bf16[96,2048]{1,0:T(8,128)(2,1)S(1)} collective-permute-done((bf16[96,2048]{1,0:T(8,128)(2,1)}, bf16[96,2048]{1,0:T(8,128)(2,1)S(1)}, u32[]{:S(2)}, u32[]{:S(2)}) %collective-permute-start.54) | collective-permute-done | bytes 393248 | tf_op jit(solution)/shard_map/ppermute | solution.py:108
  454.2 7.4 %shard_map.266 = (f32[448,768]{1,0:T(8,128)}, f32[448,1]{1,0:T(8,128)}, f32[1,768]{1,0:T(1,128)}) custom-call(s32[1]{0:T(128)} %bitcast.3.where, bf16[448,768]{1,0:T(8,128)(2,1)} %get-tuple-element.81.refs_5_.x_ref, f32[448,1]{1,0:T(8,128)} %get-tuple-element.120.inv_ref, bf16[1,768]{1,0:T(2,128)(2,1)} %broadcast_in_dim.60.gain_ref, ...), custom_call_target="tpu_custom_call" | custom-call | flops 1761607680 | bytes 10485760 | tf_op jit(solution)/shard_map/pallas_call | solution.py:549
  514.9 7.7 %collective-permute-done.74 = bf16[96,2048]{1,0:T(8,128)(2,1)S(1)} collective-permute-done((bf16[96,2048]{1,0:T(8,128)(2,1)}, bf16[96,2048]{1,0:T(8,128)(2,1)S(1)}, u32[]{:S(2)}, u32[]{:S(2)}) %collective-permute-start.74) | collective-permute-done | bytes 393248 | tf_op jit(solution)/shard_map/ppermute | solution.py:108
  528.5 7.9 %shard_map.273 = (f32[768,1536]{1,0:T(8,128)}, f32[768,512]{1,0:T(8,128)}, f32[768,512]{1,0:T(8,128)}, f32[2,768,768]{2,1,0:T(8,128)}) custom-call(s32[1]{0:T(128)} %bitcast.19.where, bf16[768,2048]{1,0:T(8,128)(2,1)} %copy-done.1, bf16[768,2048]{1,0:T(8,128)(2,1)} %collective-permute-done.75.refs_1_), custom_call_target="tpu_custom_call" | custom-call | bytes 12582912 | tf_op jit(solution)/shard_map/pallas_call | solution.py:1096
  (371 shorter events, 287.7 us)
Async XLA Ops:
  0.7 87.1 %collective-permute-start.13 = (bf16[224,1536]{1,0:T(8,128)(2,1)}, bf16[224,1536]{1,0:T(8,128)(2,1)}, u32[]{:S(2)}, u32[]{:S(2)}) collective-permute-start(bf16[224,1536]{1,0:T(8,128)(2,1)} %param.27), channel_id=1, source_target_pairs={{0,2},{2,0},{4,6},{6,4},{8,10},{10,8},{12,14},{14,12},{16,18},{18,... | collective-permute-start | bytes 2064392 | tf_op jit(solution)/shard_map/ppermute | solution.py:105
  10.9 56.8 %collective-permute-start.6 = (bf16[48,768]{1,0:T(8,128)(2,1)}, bf16[48,768]{1,0:T(8,128)(2,1)}, u32[]{:S(2)}, u32[]{:S(2)}) collective-permute-start(bf16[48,768]{1,0:T(8,128)(2,1)} %get-tuple-element.83.refs_2_), channel_id=1, source_target_pairs={{0,1},{1,0},{2,3},{3,2},{4,5},{5,4},{6,7},{7,6},{8,9},{9,8},{10,11... | collective-permute-start | bytes 221192 | tf_op jit(solution)/shard_map/ppermute | solution.py:102
  30.8 24.1 %collective-permute-start.1 = (bf16[448,640]{1,0:T(8,128)(2,1)}, bf16[448,640]{1,0:T(8,128)(2,1)S(1)}, u32[]{:S(2)}, u32[]{:S(2)}) collective-permute-start(bf16[448,640]{1,0:T(8,128)(2,1)} %get-tuple-element.77), channel_id=1, source_target_pairs={{0,1},{1,0},{2,3},{3,2},{4,5},{5,4},{6,7},{7,6},{8,9},{9,8},{10,11... | collective-permute-start | bytes 1720328 | tf_op jit(solution)/shard_map/ppermute | solution.py:102
  31.5 53.0 %collective-permute-start.14 = (bf16[112,1536]{1,0:T(8,128)(2,1)S(1)}, bf16[112,1536]{1,0:T(8,128)(2,1)S(1)}, u32[]{:S(2)}, u32[]{:S(2)}) collective-permute-start(bf16[112,1536]{1,0:T(8,128)(2,1)S(1)} %collective-permute-done.11), channel_id=1, source_target_pairs={{0,2},{2,0},{4,6},{6,4},{8,10},{10,8},{12,14},{14,12},{16,18},{18,... | collective-permute-start | bytes 1032200 | tf_op jit(solution)/shard_map/ppermute | solution.py:105
  74.3 30.6 %collective-permute-start.9 = (bf16[48,768]{1,0:T(8,128)(2,1)}, bf16[48,768]{1,0:T(8,128)(2,1)}, u32[]{:S(2)}, u32[]{:S(2)}) collective-permute-start(bf16[48,768]{1,0:T(8,128)(2,1)} %get-tuple-element.83.refs_2_), channel_id=1, source_target_pairs={{0,2},{2,0},{4,6},{6,4},{8,10},{10,8},{12,14},{14,12},{16,18},{18,... | collective-permute-start | bytes 221192 | tf_op jit(solution)/shard_map/ppermute | solution.py:105
  78.6 26.3 %collective-permute-start.10 = (bf16[48,768]{1,0:T(8,128)(2,1)}, bf16[48,768]{1,0:T(8,128)(2,1)}, u32[]{:S(2)}, u32[]{:S(2)}) collective-permute-start(bf16[48,768]{1,0:T(8,128)(2,1)} %collective-permute-done.6.refs_3_), channel_id=1, source_target_pairs={{0,2},{2,0},{4,6},{6,4},{8,10},{10,8},{12,14},{14,12},{16,18},{18,... | collective-permute-start | bytes 221192 | tf_op jit(solution)/shard_map/ppermute | solution.py:105
  169.8 22.7 %collective-permute-start.17 = (bf16[6,192,512]{2,1,0:T(8,128)(2,1)}, bf16[6,192,512]{2,1,0:T(8,128)(2,1)S(1)}, u32[]{:S(2)}, u32[]{:S(2)}) collective-permute-start(bf16[6,192,512]{2,1,0:T(8,128)(2,1)} %shard_map.240), channel_id=1, source_target_pairs={{0,8},{2,6},{8,16},{10,2},{16,24},{18,10},{24,28},{26,18},{28,20},... | collective-permute-start | bytes 3538952 | tf_op jit(solution)/shard_map/ppermute | solution.py:108
  190.9 33.8 %collective-permute-start.20 = (bf16[6,192,512]{2,1,0:T(8,128)(2,1)}, bf16[6,192,512]{2,1,0:T(8,128)(2,1)S(1)}, u32[]{:S(2)}, u32[]{:S(2)}) collective-permute-start(bf16[6,192,512]{2,1,0:T(8,128)(2,1)} %constant_dynamic-slice_fusion.4), channel_id=1, source_target_pairs={{0,8},{2,6},{8,16},{10,2},{16,24},{18,10},{24,28},{26,18},{28,20},... | collective-permute-start | bytes 3538952 | tf_op jit(solution)/shard_map/ppermute | solution.py:108
  195.5 24.4 %collective-permute-start.19 = (bf16[6,192,512]{2,1,0:T(8,128)(2,1)}, bf16[6,192,512]{2,1,0:T(8,128)(2,1)S(1)}, u32[]{:S(2)}, u32[]{:S(2)}) collective-permute-start(bf16[6,192,512]{2,1,0:T(8,128)(2,1)} %shard_map.242), channel_id=1, source_target_pairs={{0,8},{2,6},{8,16},{10,2},{16,24},{18,10},{24,28},{26,18},{28,20},... | collective-permute-start | bytes 3538952 | tf_op jit(solution)/shard_map/ppermute | solution.py:108
  209.0 20.6 %collective-permute-start.18 = (bf16[448,1536]{1,0:T(8,128)(2,1)}, bf16[448,1536]{1,0:T(8,128)(2,1)}, u32[]{:S(2)}, u32[]{:S(2)}) collective-permute-start(bf16[448,1536]{1,0:T(8,128)(2,1)} %shard_map.241.refs_1_), channel_id=1, source_target_pairs={{0,2},{2,0},{4,6},{6,4},{8,10},{10,8},{12,14},{14,12},{16,18},{18,... | collective-permute-start | bytes 4128776 | tf_op jit(solution)/shard_map/ppermute | solution.py:105
  227.7 24.3 %collective-permute-start.22 = (bf16[6,192,512]{2,1,0:T(8,128)(2,1)}, bf16[6,192,512]{2,1,0:T(8,128)(2,1)S(1)}, u32[]{:S(2)}, u32[]{:S(2)}) collective-permute-start(bf16[6,192,512]{2,1,0:T(8,128)(2,1)} %shard_map.245), channel_id=1, source_target_pairs={{0,8},{2,6},{8,16},{10,2},{16,24},{18,10},{24,28},{26,18},{28,20},... | collective-permute-start | bytes 3538952 | tf_op jit(solution)/shard_map/ppermute | solution.py:108
  245.3 34.6 %collective-permute-start.29 = (bf16[6,192,512]{2,1,0:T(8,128)(2,1)}, bf16[6,192,512]{2,1,0:T(8,128)(2,1)S(1)}, u32[]{:S(2)}, u32[]{:S(2)}) collective-permute-start(bf16[6,192,512]{2,1,0:T(8,128)(2,1)} %shard_map.249), channel_id=1, source_target_pairs={{0,8},{2,6},{8,16},{10,2},{16,24},{18,10},{24,28},{26,18},{28,20},... | collective-permute-start | bytes 3538952 | tf_op jit(solution)/shard_map/ppermute | solution.py:108
  258.3 38.8 %collective-permute-start.31 = (bf16[6,192,512]{2,1,0:T(8,128)(2,1)}, bf16[6,192,512]{2,1,0:T(8,128)(2,1)}, u32[]{:S(2)}, u32[]{:S(2)}) collective-permute-start(bf16[6,192,512]{2,1,0:T(8,128)(2,1)} %shard_map.251), channel_id=1, source_target_pairs={{0,8},{2,6},{8,16},{10,2},{16,24},{18,10},{24,28},{26,18},{28,20},... | collective-permute-start | bytes 3538952 | tf_op jit(solution)/shard_map/ppermute | solution.py:108
  283.0 31.0 %collective-permute-start.32 = (bf16[6,192,512]{2,1,0:T(8,128)(2,1)}, bf16[6,192,512]{2,1,0:T(8,128)(2,1)S(1)}, u32[]{:S(2)}, u32[]{:S(2)}) collective-permute-start(bf16[6,192,512]{2,1,0:T(8,128)(2,1)} %shard_map.252), channel_id=1, source_target_pairs={{0,8},{2,6},{8,16},{10,2},{16,24},{18,10},{24,28},{26,18},{28,20},... | collective-permute-start | bytes 3538952 | tf_op jit(solution)/shard_map/ppermute | solution.py:108
  300.1 27.2 %collective-permute-start.40 = (bf16[6,192,512]{2,1,0:T(8,128)(2,1)}, bf16[6,192,512]{2,1,0:T(8,128)(2,1)}, u32[]{:S(2)}, u32[]{:S(2)}) collective-permute-start(bf16[6,192,512]{2,1,0:T(8,128)(2,1)} %shard_map.255), channel_id=1, source_target_pairs={{0,8},{2,6},{8,16},{10,2},{16,24},{18,10},{24,28},{26,18},{28,20},... | collective-permute-start | bytes 3538952 | tf_op jit(solution)/shard_map/ppermute | solution.py:108
  303.5 34.1 %collective-permute-start.26 = (bf16[448,768]{1,0:T(8,128)(2,1)}, bf16[448,768]{1,0:T(8,128)(2,1)}, u32[]{:S(2)}, u32[]{:S(2)}) collective-permute-start(bf16[448,768]{1,0:T(8,128)(2,1)} %get-tuple-element.74.hidden_ref.refs_0_), channel_id=1, source_target_pairs={{0,2},{2,0},{4,6},{6,4},{8,10},{10,8},{12,14},{14,12},{16,18},{18,... | collective-permute-start | bytes 2064392 | tf_op jit(solution)/shard_map/ppermute | solution.py:105
  303.6 23.7 %collective-permute-start.39 = (bf16[448,384]{1,0:T(8,128)(2,1)}, bf16[448,384]{1,0:T(8,128)(2,1)}, u32[]{:S(2)}, u32[]{:S(2)}) collective-permute-start(bf16[448,384]{1,0:T(8,128)(2,1)} %get-tuple-element.114), channel_id=1, source_target_pairs={{0,1},{1,0},{2,3},{3,2},{4,5},{5,4},{6,7},{7,6},{8,9},{9,8},{10,11... | collective-permute-start | bytes 1032200 | tf_op jit(solution)/shard_map/ppermute | solution.py:102
  326.3 28.2 %collective-permute-start.46 = (bf16[6,192,512]{2,1,0:T(8,128)(2,1)}, bf16[6,192,512]{2,1,0:T(8,128)(2,1)S(1)}, u32[]{:S(2)}, u32[]{:S(2)}) collective-permute-start(bf16[6,192,512]{2,1,0:T(8,128)(2,1)} %shard_map.257), channel_id=1, source_target_pairs={{0,8},{2,6},{8,16},{10,2},{16,24},{18,10},{24,28},{26,18},{28,20},... | collective-permute-start | bytes 3538952 | tf_op jit(solution)/shard_map/ppermute | solution.py:108
  353.1 22.7 %collective-permute-start.48 = (bf16[6,192,512]{2,1,0:T(8,128)(2,1)}, bf16[6,192,512]{2,1,0:T(8,128)(2,1)S(1)}, u32[]{:S(2)}, u32[]{:S(2)}) collective-permute-start(bf16[6,192,512]{2,1,0:T(8,128)(2,1)} %shard_map.259), channel_id=1, source_target_pairs={{0,8},{2,6},{8,16},{10,2},{16,24},{18,10},{24,28},{26,18},{28,20},... | collective-permute-start | bytes 3538952 | tf_op jit(solution)/shard_map/ppermute | solution.py:108
  381.1 22.6 %collective-permute-start.51 = (bf16[6,192,512]{2,1,0:T(8,128)(2,1)}, bf16[6,192,512]{2,1,0:T(8,128)(2,1)S(1)}, u32[]{:S(2)}, u32[]{:S(2)}) collective-permute-start(bf16[6,192,512]{2,1,0:T(8,128)(2,1)} %shard_map.261), channel_id=1, source_target_pairs={{0,8},{2,6},{8,16},{10,2},{16,24},{18,10},{24,28},{26,18},{28,20},... | collective-permute-start | bytes 3538952 | tf_op jit(solution)/shard_map/ppermute | solution.py:108
  406.0 26.7 %collective-permute-start.25 = (bf16[448,1536]{1,0:T(8,128)(2,1)}, bf16[448,1536]{1,0:T(8,128)(2,1)}, u32[]{:S(2)}, u32[]{:S(2)}) collective-permute-start(bf16[448,1536]{1,0:T(8,128)(2,1)} %shard_map.246.refs_0_), channel_id=1, source_target_pairs={{0,2},{2,0},{4,6},{6,4},{8,10},{10,8},{12,14},{14,12},{16,18},{18,... | collective-permute-start | bytes 4128776 | tf_op jit(solution)/shard_map/ppermute | solution.py:105
  409.0 22.5 %collective-permute-start.55 = (bf16[6,192,512]{2,1,0:T(8,128)(2,1)}, bf16[6,192,512]{2,1,0:T(8,128)(2,1)}, u32[]{:S(2)}, u32[]{:S(2)}) collective-permute-start(bf16[6,192,512]{2,1,0:T(8,128)(2,1)} %shard_map.264), channel_id=1, source_target_pairs={{0,8},{2,6},{8,16},{10,2},{16,24},{18,10},{24,28},{26,18},{28,20},... | collective-permute-start | bytes 3538952 | tf_op jit(solution)/shard_map/ppermute | solution.py:108
  444.5 21.7 %collective-permute-start.67 = (bf16[3,192,512]{2,1,0:T(8,128)(2,1)}, bf16[3,192,512]{2,1,0:T(8,128)(2,1)}, u32[]{:S(2)}, u32[]{:S(2)}) collective-permute-start(bf16[3,192,512]{2,1,0:T(8,128)(2,1)} %get-tuple-element.141.refs_0_), channel_id=1, source_target_pairs={{0,2},{2,0},{4,6},{6,4},{8,10},{10,8},{12,14},{14,12},{16,18},{18,... | collective-permute-start | bytes 1769480 | tf_op jit(solution)/shard_map/ppermute | solution.py:105
  444.5 27.7 %collective-permute-start.68 = (bf16[3,192,512]{2,1,0:T(8,128)(2,1)}, bf16[3,192,512]{2,1,0:T(8,128)(2,1)}, u32[]{:S(2)}, u32[]{:S(2)}) collective-permute-start(bf16[3,192,512]{2,1,0:T(8,128)(2,1)} %get-tuple-element.140.refs_1_), channel_id=1, source_target_pairs={{0,2},{2,0},{4,6},{6,4},{8,10},{10,8},{12,14},{14,12},{16,18},{18,... | collective-permute-start | bytes 1769480 | tf_op jit(solution)/shard_map/ppermute | solution.py:105
  (106 other events, 832.0 us)
